TPU v7x, 256 devices: a whole 4x4x8 slice. The times are simulated.
256 devices in a mesh: feat: 8 (over y, x_hi), tok: 32 (over z, x_lo, core).
Axes of the slice: x: 4 (x_hi: 2, x_lo: 2; x = x_hi * 2 + x_lo), y: 4, z: 8, core: 2. Of those that a mesh axis runs over, the one named last changes fastest.
Arguments:
- tokens: bfloat16 [8192, 12288], P('tok', 'feat'), may hold values from -6 to 6
- gate_weight: bfloat16 [16, 5, 768, 768], P('feat', None, 'tok'), may hold values from -0.09375 to 0.09375
- up_weight: bfloat16 [16, 5, 768, 768], P('feat', None, 'tok'), may hold values from -0.09375 to 0.09375
- gate_scale: float32 [16, 5], P('feat'), may hold values from 0.35 to 2.8
- up_scale: float32 [16, 5], P('feat'), may hold values from 0.35 to 2.8
- partners: int32 [16, 5], replicated, may hold values from 0 to 15, as said below
- latent_in: bfloat16 [12288, 768], P('feat'), may hold values from -0.0546875 to 0.0546875
- latent_out: bfloat16 [768, 12288], P(None, 'feat'), may hold values from -0.21875 to 0.21875
Outputs:
- hidden: bfloat16 [8192, 12288], P('tok', 'feat')
- rank_term: bfloat16 [8192, 12288], P('tok', 'feat')
Inputs may be any that keep to these rules, and one draw needn't show every extreme that they name: `partners`: row i lists the blocks i, i xor 1, i xor 2, i xor 4 and i xor 8, each once, in some order.
All inputs are finite; a program needn't handle non-finite values.
Results may differ from a plain program's by a relative error of at most 0.015.
Values may be sent and summed in bfloat16 or wider, within the bound.
No kernel may reach another device: no remote copies, remote signals or barrier semaphores. Data moves between devices by JAX's collectives and lax.ppermute only.
A program may use at most 128 MiB of HBM per device.

v0:
```python
import functools
import jax
import jax.numpy as jnp
from jax import lax
from jax.experimental import pallas as pl
from jax.experimental.pallas import tpu as pltpu
from jax.sharding import PartitionSpec as P

GROUP = 4
HBM = pl.BlockSpec(memory_space=pltpu.HBM)
SMEM = pl.BlockSpec(memory_space=pltpu.SMEM)
VMEM = pl.BlockSpec(memory_space=pltpu.VMEM)
VMEM_BYTES = 44 * 2**20


def swapped(value, axis, mask):
    return lax.ppermute(value, axis, [(i, i ^ mask) for i in range(lax.axis_size(axis))])


def shifted(value, step):
    count = lax.axis_size("tok")
    return lax.ppermute(value, "tok", [(i, (i + step * GROUP) % count) for i in range(count)])


def pack_kernel(own_ref, gate_ref, up_ref, *out_refs):
    half = gate_ref.shape[3] // 2
    for m in range(4):
        to = own_ref[0] ^ m
        at = pl.ds(pl.multiple_of(to % 2 * half, 128), half)
        for side, ref in enumerate((gate_ref, up_ref)):
            out_refs[m][side] = ref[to // 2, :, :, at]


def place_kernel(own_ref, *refs):
    for m in range(4):
        refs[4][:, :, own_ref[0] ^ m] = refs[m][...]


def gate_up_kernel(cand_ref, gs_ref, us_ref, *refs, rows, z_count):
    n_w = z_count + 1
    w_refs, s_refs, p_refs, out_ref = refs[:n_w], refs[n_w : n_w + 2], refs[n_w + 2 : n_w + 8], refs[n_w + 8]
    x_mem, w_mem, acc, x_sem, w_sem = refs[n_w + 9 :]
    x_lo, z = cand_ref[5], cand_ref[6]
    slots, blk, both = w_mem.shape
    share, width = blk // z_count, both // 2
    w_copies = []
    for k in range(slots):
        mine = []
        for i, ref in enumerate(w_refs):
            if i < z_count - 1:
                origin, sides = (z - (i + 1) // 2 if i % 2 else z + i // 2), (0, 1)
            else:
                origin, sides = z + z_count // 2, (i - z_count + 1,)
            at = pl.ds(pl.multiple_of((origin + z_count) % z_count * share, 16), share)
            for n, side in enumerate(sides):
                there = w_mem.at[k, at, pl.ds(side * width, width)]
                mine.append(pltpu.make_async_copy(ref.at[n, k], there, w_sem.at[k, i, n]))
        w_copies.append(mine)
    x_copies = []
    for m in range(2):
        at = pl.ds(m * rows, rows)
        for j in range(2):
            col = pl.multiple_of((x_lo ^ j) * blk, blk)
            x_copies.append(pltpu.make_async_copy(s_refs[m].at[:, pl.ds(col, blk)], x_mem.at[j, at], x_sem.at[m, j]))
        for d in range(3):
            x_copies.append(pltpu.make_async_copy(p_refs[d * 2 + m], x_mem.at[2 + d, at], x_sem.at[m, 2 + d]))
    for copy in w_copies[0] + x_copies:
        copy.start()
    for mine in w_copies[1:]:
        for copy in mine:
            copy.start()
    for copy in x_copies:
        copy.wait()
    for k in range(slots):
        for copy in w_copies[k]:
            copy.wait()
        term = jnp.dot(x_mem[cand_ref[k]], w_mem[k], preferred_element_type=jnp.float32)
        g, u = term[:, :width] * gs_ref[k], term[:, width:] * us_ref[k]
        if k == 0:
            acc[:, :width] = g
            acc[:, width:] = u
        else:
            acc[:, :width] += g
            acc[:, width:] += u
    g = acc[:, :width]
    out = (g / (1.0 + jnp.exp(-g)) * acc[:, width:]).astype(jnp.bfloat16)
    out_ref[0] = out[:rows]
    out_ref[1] = out[rows:]


def gate_up(cand, gs, us, weights, own_rows, partner_rows):
    rows, features = own_rows[0].shape
    blk = features // 2
    _, slots, share, width = weights[0].shape
    z_count = blk // share
    flops = 2 * 2 * 2 * rows * slots * blk * width
    return pl.pallas_call(
        functools.partial(gate_up_kernel, rows=rows, z_count=z_count),
        out_shape=jax.ShapeDtypeStruct((2, rows, width), jnp.bfloat16),
        in_specs=[SMEM] * 3 + [HBM] * (len(weights) + 8),
        out_specs=VMEM,
        scratch_shapes=[
            pltpu.VMEM((slots, 2 * rows, blk), jnp.bfloat16),
            pltpu.VMEM((slots, blk, 2 * width), jnp.bfloat16),
            pltpu.VMEM((2 * rows, 2 * width), jnp.float32),
            pltpu.SemaphoreType.DMA((2, 5)),
            pltpu.SemaphoreType.DMA((slots, z_count + 1, 2)),
        ],
        compiler_params=pltpu.CompilerParams(vmem_limit_bytes=VMEM_BYTES),
        cost_estimate=pl.CostEstimate(flops=flops, bytes_accessed=10 * 2**20, transcendentals=2 * rows * width),
    )(cand, gs, us, *weights, *own_rows, *partner_rows)


def latent_kernel(own_ref, lin_ref, *refs):
    pieces, hidden_ref, part_ref = refs[:4], refs[4], refs[5]
    width = pieces[0].shape[1]
    total = None
    for m in range(4):
        at = pl.ds(pl.multiple_of((own_ref[0] ^ m) * width, width), width)
        piece = pieces[m][...]
        hidden_ref[:, at] = piece
        term = jnp.dot(piece, lin_ref[at], preferred_element_type=jnp.float32)
        total = term if total is None else total + term
    part_ref[...] = total.astype(jnp.bfloat16)


def per_device(tokens, gate_weight, up_weight, gate_scale, up_scale, partners, latent_in, latent_out):
    rows, features = tokens.shape
    blocks, slots, share, blk = gate_weight.shape
    feat_count = lax.axis_size("feat")
    half = blk // 2
    feat, tok = lax.axis_index("feat"), lax.axis_index("tok")
    member, z = tok % GROUP, tok // GROUP
    x_lo, core = member // 2, member % 2
    block_id = feat * blocks + x_lo

    own = member[None].astype(jnp.int32)
    packed = pl.pallas_call(
        pack_kernel,
        out_shape=[jax.ShapeDtypeStruct((2, slots, share, half), jnp.bfloat16)] * 4,
        in_specs=[SMEM, VMEM, VMEM],
        out_specs=[VMEM] * 4,
    )(own, gate_weight, up_weight)

    def place(got):
        shape = got[0].shape
        out = pl.pallas_call(
            place_kernel,
            out_shape=jax.ShapeDtypeStruct(shape[:2] + (4,) + shape[2:], jnp.bfloat16),
            in_specs=[SMEM] + [VMEM] * 4,
            out_specs=VMEM,
        )(own, *got)
        return out.reshape(shape[:2] + (4 * shape[2],) + shape[3:])

    def block_of(value):
        return lax.dynamic_slice(value, (0, x_lo * blk), (rows, blk))

    def step(forward, back):
        return shifted(forward, 1), shifted(back, -1)

    far = [swapped(packed[m], "tok", m) for m in (2, 3)]
    near = swapped(packed[1], "tok", 1)
    w0 = place([packed[0], near, *far])
    barrier = lax.optimization_barrier
    first = block_of(tokens)
    p0_y1, p0_y2 = swapped(first, "feat", 2), swapped(first, "feat", 4)
    w0, later = barrier((w0, tokens))
    w1 = step(w0, w0)
    s2 = swapped(later, "tok", 2)
    first, p0_y1, p0_y2 = barrier((first, p0_y1, p0_y2))
    p0 = [swapped(first, "feat", 1), p0_y1, p0_y2]
    w1, s2, p0, later = barrier((w1, s2, p0, later))
    w2 = step(*w1)
    second = block_of(s2)
    p2 = [swapped(second, "feat", mask) for mask in (1, 2, 4)]
    w2, p2, p0, s2, later = barrier((w2, p2, p0, s2, later))
    w3 = step(*w2)
    s3 = swapped(s2, "tok", 1)
    p3 = [swapped(v, "tok", 1) for v in p2]
    w3, s3, p3, p0, later = barrier((w3, s3, p3, p0, later))
    w4 = step(w3[0][:1], w3[1][1:])
    s1 = swapped(later, "tok", 1)
    p1 = [swapped(v, "tok", 1) for v in p0]
    full = (w0, *w1, *w2, *w3, *w4)

    wanted = lax.dynamic_index_in_dim(partners, block_id, 0, keepdims=False)
    labels = block_id ^ jnp.array([0, 1, 2, 4, 8], jnp.int32)
    order = jnp.sum(jnp.where(wanted[:, None] == labels[None, :], jnp.arange(5, dtype=jnp.int32)[None, :], 0), axis=1)
    cand = jnp.concatenate([order, jnp.stack([x_lo, z]).astype(jnp.int32)])
    gs = lax.dynamic_index_in_dim(gate_scale, x_lo, 0, keepdims=False)
    us = lax.dynamic_index_in_dim(up_scale, x_lo, 0, keepdims=False)

    made = gate_up(cand, gs, us, full, [s2, s3], [p[d] for d in range(3) for p in (p2, p3)])
    hidden2, hidden3 = swapped(made[0], "tok", 2), swapped(made[1], "tok", 3)
    made = gate_up(cand, gs, us, full, [tokens, s1], [p[d] for d in range(3) for p in (p0, p1)])
    hidden_pieces = [made[0], swapped(made[1], "tok", 1), hidden2, hidden3]
    hidden, part = pl.pallas_call(
        latent_kernel,
        out_shape=(
            jax.ShapeDtypeStruct((rows, features), jnp.bfloat16),
            jax.ShapeDtypeStruct((rows, latent_in.shape[1]), jnp.bfloat16),
        ),
        in_specs=[SMEM] + [VMEM] * 5,
        out_specs=(VMEM, VMEM),
        compiler_params=pltpu.CompilerParams(vmem_limit_bytes=VMEM_BYTES),
        cost_estimate=pl.CostEstimate(flops=2 * rows * features * latent_in.shape[1], bytes_accessed=4 * 2**20, transcendentals=0),
    )(own, latent_in, *hidden_pieces)

    parts = part.reshape(feat_count, rows // feat_count, -1)
    terms = lax.all_to_all(parts, "feat", 0, 0)
    mine = jnp.sum(terms.astype(jnp.float32), axis=0).astype(jnp.bfloat16)
    latent = lax.all_to_all(jnp.broadcast_to(mine[None], parts.shape), "feat", 0, 0).reshape(rows, -1)
    rank_term = jnp.dot(latent, latent_out, preferred_element_type=jnp.float32).astype(jnp.bfloat16)
    return hidden, rank_term


def solution(mesh):
    placed = (
        P("tok", "feat"),
        P("feat", None, "tok", None),
        P("feat", None, "tok", None),
        P("feat", None),
        P("feat", None),
        P(),
        P("feat", None),
        P(None, "feat"),
    )
    return jax.shard_map(
        per_device,
        mesh=mesh,
        in_specs=placed,
        out_specs=(P("tok", "feat"), P("tok", "feat")),
        check_vma=False,
    )
```

profile of v0, /device:TPU:1, one launch (start us, length us, event | category | flops | bytes accessed | tf_op | source)
XLA Modules:
  0.0 169.2 jit_solution(11090636393014203548)
XLA Ops:
  0.7 2.2 %shard_map.104 = (bf16[2,5,24,384]{3,2,1,0:T(8,128)(2,1)}, bf16[2,5,24,384]{3,2,1,0:T(8,128)(2,1)}, bf16[2,5,24,384]{3,2,1,0:T(8,128)(2,1)}, bf16[2,5,24,384]{3,2,1,0:T(8,128)(2,1)}) custom-call(s32[1]{0:T(128)} %bitcast.own_ref, bf16[2,5,24,768]{3,2,1,0:T(8,128)(2,1)} %gate_ref.1, bf16[2,5,24,768]{3,2,1,0:T(8,128)(2,1)} %up_ref.1), custom_call_target="tpu_custom_call" | custom-call | tf_op jit(solution)/shard_map/pallas_call | solution.py:138
  2.9 3.3 %collective-permute-start = (bf16[2,5,24,384]{3,2,1,0:T(8,128)(2,1)}, bf16[2,5,24,384]{3,2,1,0:T(8,128)(2,1)}, u32[]{:S(2)}, u32[]{:S(2)}) collective-permute-start(bf16[2,5,24,384]{3,2,1,0:T(8,128)(2,1)} %get-tuple-element.41), channel_id=1, source_target_pairs={{0,1},{1,0},{2,3},{3,2},{4,5},{5,4},{6,7},{7,6},{8,9},{9,8},{10,11... | collective-permute-start | bytes 552968 | tf_op jit(solution)/shard_map/ppermute | solution.py:17
  12.7 4.3 %collective-permute-done.2.refs_3_ = bf16[2,5,24,384]{3,2,1,0:T(8,128)(2,1)} collective-permute-done((bf16[2,5,24,384]{3,2,1,0:T(8,128)(2,1)}, bf16[2,5,24,384]{3,2,1,0:T(8,128)(2,1)}, u32[]{:S(2)}, u32[]{:S(2)}) %collective-permute-start.2) | collective-permute-done | bytes 184352 | tf_op jit(solution)/shard_map/ppermute | solution.py:17
  17.1 2.1 %shard_map.105 = bf16[2,5,4,24,384]{4,3,2,1,0:T(8,128)(2,1)} custom-call(s32[1]{0:T(128)} %bitcast.own_ref, bf16[2,5,24,384]{3,2,1,0:T(8,128)(2,1)} %get-tuple-element.40.refs_0_, bf16[2,5,24,384]{3,2,1,0:T(8,128)(2,1)} %collective-permute-done.refs_1_, bf16[2,5,24,384]{3,2,1,0:T(8,128)(2,1)} %collective-permute-done.1.refs_2_, ...), custom_call_target="tpu_custom_call" | custom-call | tf_op jit(solution)/shard_map/pallas_call | solution.py:147
  19.2 5.0 %collective-permute-start.4 = (bf16[2,5,96,384]{3,2,1,0:T(8,128)(2,1)}, bf16[2,5,96,384]{3,2,1,0:T(8,128)(2,1)S(1)}, u32[]{:S(2)}, u32[]{:S(2)}) collective-permute-start(bf16[2,5,96,384]{3,2,1,0:T(8,128)(2,1)} %bitcast.20), channel_id=1, source_target_pairs={{0,28},{1,29},{2,30},{3,31},{4,0},{5,1},{6,2},{7,3},{8,4},{9,5},{1... | collective-permute-start | bytes 2211848 | tf_op jit(solution)/shard_map/ppermute | solution.py:22
  24.2 4.9 %collective-permute-done.6.refs_13_ = bf16[256,768]{1,0:T(8,128)(2,1)} collective-permute-done((bf16[256,768]{1,0:T(8,128)(2,1)}, bf16[256,768]{1,0:T(8,128)(2,1)}, u32[]{:S(2)}, u32[]{:S(2)}) %collective-permute-start.6) | collective-permute-done | bytes 393248 | tf_op jit(solution)/shard_map/ppermute | solution.py:17
  29.1 2.7 %collective-permute-start.8 = (bf16[256,768]{1,0:T(8,128)(2,1)}, bf16[256,768]{1,0:T(8,128)(2,1)S(1)}, u32[]{:S(2)}, u32[]{:S(2)}) collective-permute-start(bf16[256,768]{1,0:T(8,128)(2,1)} %constant_dynamic-slice_fusion.1), channel_id=1, source_target_pairs={{0,32},{32,0},{64,96},{96,64},{128,160},{160,128},{192,224},{224,1... | collective-permute-start | bytes 1179656 | tf_op jit(solution)/shard_map/ppermute | solution.py:17
  31.9 15.3 %collective-permute-done.8.refs_11_ = bf16[256,768]{1,0:T(8,128)(2,1)S(1)} collective-permute-done((bf16[256,768]{1,0:T(8,128)(2,1)}, bf16[256,768]{1,0:T(8,128)(2,1)S(1)}, u32[]{:S(2)}, u32[]{:S(2)}) %collective-permute-start.8) | collective-permute-done | bytes 393248 | tf_op jit(solution)/shard_map/ppermute | solution.py:17
  49.8 4.6 %collective-permute-start.10 = (bf16[2,5,96,384]{3,2,1,0:T(8,128)(2,1)S(1)}, bf16[2,5,96,384]{3,2,1,0:T(8,128)(2,1)}, u32[]{:S(2)}, u32[]{:S(2)}) collective-permute-start(bf16[2,5,96,384]{3,2,1,0:T(8,128)(2,1)S(1)} %collective-permute-done.4.refs_2_), channel_id=1, source_target_pairs={{0,28},{1,29},{2,30},{3,31},{4,0},{5,1},{6,2},{7,3},{8,4},{9,5},{1... | collective-permute-start | bytes 2211848 | tf_op jit(solution)/shard_map/ppermute | solution.py:22
  56.3 3.0 %collective-permute-start.13 = (bf16[256,768]{1,0:T(8,128)(2,1)S(1)}, bf16[256,768]{1,0:T(8,128)(2,1)}, u32[]{:S(2)}, u32[]{:S(2)}) collective-permute-start(bf16[256,768]{1,0:T(8,128)(2,1)S(1)} %constant_dynamic-slice_fusion), channel_id=1, source_target_pairs={{0,128},{32,160},{64,192},{96,224},{128,0},{160,32},{192,64},{224,... | collective-permute-start | bytes 1179656 | tf_op jit(solution)/shard_map/ppermute | solution.py:17
  60.2 7.3 %collective-permute-done.13.refs_15_ = bf16[256,768]{1,0:T(8,128)(2,1)} collective-permute-done((bf16[256,768]{1,0:T(8,128)(2,1)S(1)}, bf16[256,768]{1,0:T(8,128)(2,1)}, u32[]{:S(2)}, u32[]{:S(2)}) %collective-permute-start.13) | collective-permute-done | bytes 393248 | tf_op jit(solution)/shard_map/ppermute | solution.py:17
  67.5 8.8 %collective-permute-done.12.refs_13_ = bf16[256,768]{1,0:T(8,128)(2,1)} collective-permute-done((bf16[256,768]{1,0:T(8,128)(2,1)S(1)}, bf16[256,768]{1,0:T(8,128)(2,1)}, u32[]{:S(2)}, u32[]{:S(2)}) %collective-permute-start.12) | collective-permute-done | bytes 393248 | tf_op jit(solution)/shard_map/ppermute | solution.py:17
  76.3 2.1 %collective-permute-start.17 = (bf16[256,768]{1,0:T(8,128)(2,1)S(1)}, bf16[256,768]{1,0:T(8,128)(2,1)S(1)}, u32[]{:S(2)}, u32[]{:S(2)}) collective-permute-start(bf16[256,768]{1,0:T(8,128)(2,1)S(1)} %collective-permute-done.11.refs_11_), channel_id=1, source_target_pairs={{0,1},{1,0},{2,3},{3,2},{4,5},{5,4},{6,7},{7,6},{8,9},{9,8},{10,11... | collective-permute-start | bytes 1179656 | tf_op jit(solution)/shard_map/ppermute | solution.py:17
  79.2 2.7 %collective-permute-start.15 = (bf16[2,5,96,384]{3,2,1,0:T(8,128)(2,1)}, bf16[2,5,96,384]{3,2,1,0:T(8,128)(2,1)}, u32[]{:S(2)}, u32[]{:S(2)}) collective-permute-start(bf16[2,5,96,384]{3,2,1,0:T(8,128)(2,1)} %collective-permute-done.10.refs_4_), channel_id=1, source_target_pairs={{0,28},{1,29},{2,30},{3,31},{4,0},{5,1},{6,2},{7,3},{8,4},{9,5},{1... | collective-permute-start | bytes 2211848 | tf_op jit(solution)/shard_map/ppermute | solution.py:22
  85.7 12.5 %collective-permute-done.14.refs_5_ = bf16[2,5,96,384]{3,2,1,0:T(8,128)(2,1)} collective-permute-done((bf16[2,5,96,384]{3,2,1,0:T(8,128)(2,1)}, bf16[2,5,96,384]{3,2,1,0:T(8,128)(2,1)}, u32[]{:S(2)}, u32[]{:S(2)}) %collective-permute-start.14) | collective-permute-done | bytes 737312 | tf_op jit(solution)/shard_map/ppermute | solution.py:22
  101.9 2.3 %collective-permute-start.21 = (bf16[1,5,96,384]{3,2,1,0:T(8,128)(2,1)}, bf16[1,5,96,384]{3,2,1,0:T(8,128)(2,1)}, u32[]{:S(2)}, u32[]{:S(2)}) collective-permute-start(bf16[1,5,96,384]{3,2,1,0:T(8,128)(2,1)} %slice.19), channel_id=1, source_target_pairs={{0,28},{1,29},{2,30},{3,31},{4,0},{5,1},{6,2},{7,3},{8,4},{9,5},{1... | collective-permute-start | bytes 1105928 | tf_op jit(solution)/shard_map/ppermute | solution.py:22
  105.0 2.0 %collective-permute-start.22 = (bf16[256,1536]{1,0:T(8,128)(2,1)S(1)}, bf16[256,1536]{1,0:T(8,128)(2,1)}, u32[]{:S(2)}, u32[]{:S(2)}) collective-permute-start(bf16[256,1536]{1,0:T(8,128)(2,1)S(1)} %copy-done.3), channel_id=1, source_target_pairs={{0,1},{1,0},{2,3},{3,2},{4,5},{5,4},{6,7},{7,6},{8,9},{9,8},{10,11... | collective-permute-start | bytes 2359304 | tf_op jit(solution)/shard_map/ppermute | solution.py:17
  108.5 2.4 %collective-permute-done.21.refs_8_ = bf16[1,5,96,384]{3,2,1,0:T(8,128)(2,1)} collective-permute-done((bf16[1,5,96,384]{3,2,1,0:T(8,128)(2,1)}, bf16[1,5,96,384]{3,2,1,0:T(8,128)(2,1)}, u32[]{:S(2)}, u32[]{:S(2)}) %collective-permute-start.21) | collective-permute-done | bytes 368672 | tf_op jit(solution)/shard_map/ppermute | solution.py:22
  110.9 2.4 %collective-permute-start.25 = (bf16[256,768]{1,0:T(8,128)(2,1)S(1)}, bf16[256,768]{1,0:T(8,128)(2,1)S(1)}, u32[]{:S(2)}, u32[]{:S(2)}) collective-permute-start(bf16[256,768]{1,0:T(8,128)(2,1)S(1)} %collective-permute-done.7.refs_15_), channel_id=1, source_target_pairs={{0,1},{1,0},{2,3},{3,2},{4,5},{5,4},{6,7},{7,6},{8,9},{9,8},{10,11... | collective-permute-start | bytes 1179656 | tf_op jit(solution)/shard_map/ppermute | solution.py:17
  119.2 8.7 %shard_map.107 = bf16[2,256,384]{2,1,0:T(8,128)(2,1)S(1)} custom-call(s32[7]{0:T(128)S(1)} %pad_add_fusion.cand_ref, f32[5]{0:T(128)S(1)} %get-tuple-element.82.gs_ref, f32[5]{0:T(128)S(1)} %get-tuple-element.83.us_ref, bf16[2,5,96,384]{3,2,1,0:T(8,128)(2,1)S(1)} %bitcast.22, bf16[2,5,96,384]{3,2,1,0:T(8,128)(2,1)S(1)} %copy-done.7, ...), custom_call_target="tpu_custom_call" | custom-call | flops 3019898880 | bytes 10485760 | tf_op jit(solution)/shard_map/pallas_call | solution.py:97
  128.0 2.8 %collective-permute-start.28 = (bf16[256,384]{1,0:T(8,128)(2,1)S(1)}, bf16[256,384]{1,0:T(8,128)(2,1)S(1)}, u32[]{:S(2)}, u32[]{:S(2)}) collective-permute-start(bf16[256,384]{1,0:T(8,128)(2,1)S(1)} %get-tuple-element.78), channel_id=1, source_target_pairs={{0,3},{1,2},{2,1},{3,0},{4,7},{5,6},{6,5},{7,4},{8,11},{9,10},{10,... | collective-permute-start | bytes 589832 | tf_op jit(solution)/shard_map/ppermute | solution.py:17
  132.3 8.2 %shard_map.106 = bf16[2,256,384]{2,1,0:T(8,128)(2,1)S(1)} custom-call(s32[7]{0:T(128)S(1)} %pad_add_fusion.cand_ref, f32[5]{0:T(128)S(1)} %get-tuple-element.82.gs_ref, f32[5]{0:T(128)S(1)} %get-tuple-element.83.us_ref, bf16[2,5,96,384]{3,2,1,0:T(8,128)(2,1)S(1)} %bitcast.23, bf16[2,5,96,384]{3,2,1,0:T(8,128)(2,1)S(1)} %copy-done.7, ...), custom_call_target="tpu_custom_call" | custom-call | flops 3019898880 | bytes 10485760 | tf_op jit(solution)/shard_map/pallas_call | solution.py:97
  143.7 12.7 %all_to_all.10 = bf16[8,32,768]{2,1,0:T(8,128)(2,1)S(1)} all-to-all(bf16[8,32,768]{2,1,0:T(8,128)(2,1)S(1)} %bitcast.24), channel_id=1, replica_groups=mesh['feat'=8,'tok'=32] {'feat'}, dimensions={0} | all-to-all | bytes 786432 | tf_op jit(solution)/shard_map/all_to_all | solution.py:210
  156.5 11.0 %all_to_all.11 = bf16[8,32,768]{2,1,0:T(8,128)(2,1)S(1)} all-to-all(bf16[8,32,768]{2,1,0:T(8,128)(2,1)S(1)} %broadcast_in_dim.27), channel_id=1, replica_groups=mesh['feat'=8,'tok'=32] {'feat'}, dimensions={0} | all-to-all | bytes 786432 | tf_op jit(solution)/shard_map/all_to_all | solution.py:212
  (91 shorter events, 34.8 us)
Async XLA Ops:
  2.9 8.4 %collective-permute-start = (bf16[2,5,24,384]{3,2,1,0:T(8,128)(2,1)}, bf16[2,5,24,384]{3,2,1,0:T(8,128)(2,1)}, u32[]{:S(2)}, u32[]{:S(2)}) collective-permute-start(bf16[2,5,24,384]{3,2,1,0:T(8,128)(2,1)} %get-tuple-element.41), channel_id=1, source_target_pairs={{0,1},{1,0},{2,3},{3,2},{4,5},{5,4},{6,7},{7,6},{8,9},{9,8},{10,11... | collective-permute-start | bytes 552968 | tf_op jit(solution)/shard_map/ppermute | solution.py:17
  6.2 10.8 %collective-permute-start.2 = (bf16[2,5,24,384]{3,2,1,0:T(8,128)(2,1)}, bf16[2,5,24,384]{3,2,1,0:T(8,128)(2,1)}, u32[]{:S(2)}, u32[]{:S(2)}) collective-permute-start(bf16[2,5,24,384]{3,2,1,0:T(8,128)(2,1)} %get-tuple-element.43), channel_id=1, source_target_pairs={{0,3},{1,2},{2,1},{3,0},{4,7},{5,6},{6,5},{7,4},{8,11},{9,10},{10,... | collective-permute-start | bytes 552968 | tf_op jit(solution)/shard_map/ppermute | solution.py:17
  9.7 14.5 %collective-permute-start.7 = (bf16[256,768]{1,0:T(8,128)(2,1)}, bf16[256,768]{1,0:T(8,128)(2,1)S(1)}, u32[]{:S(2)}, u32[]{:S(2)}) collective-permute-start(bf16[256,768]{1,0:T(8,128)(2,1)} %constant_dynamic-slice_fusion.1), channel_id=1, source_target_pairs={{0,128},{32,160},{64,192},{96,224},{128,0},{160,32},{192,64},{224,... | collective-permute-start | bytes 1179656 | tf_op jit(solution)/shard_map/ppermute | solution.py:17
  10.9 18.2 %collective-permute-start.6 = (bf16[256,768]{1,0:T(8,128)(2,1)}, bf16[256,768]{1,0:T(8,128)(2,1)}, u32[]{:S(2)}, u32[]{:S(2)}) collective-permute-start(bf16[256,768]{1,0:T(8,128)(2,1)} %constant_dynamic-slice_fusion.1), channel_id=1, source_target_pairs={{0,64},{32,96},{64,0},{96,32},{128,192},{160,224},{192,128},{224,1... | collective-permute-start | bytes 1179656 | tf_op jit(solution)/shard_map/ppermute | solution.py:17
  19.2 28.1 %collective-permute-start.5 = (bf16[256,1536]{1,0:T(8,128)(2,1)S(1)}, bf16[256,1536]{1,0:T(8,128)(2,1)}, u32[]{:S(2)}, u32[]{:S(2)}) collective-permute-start(bf16[256,1536]{1,0:T(8,128)(2,1)S(1)} %copy-done.3), channel_id=1, source_target_pairs={{0,2},{1,3},{2,0},{3,1},{4,6},{5,7},{6,4},{7,5},{8,10},{9,11},{10,... | collective-permute-start | bytes 2359304 | tf_op jit(solution)/shard_map/ppermute | solution.py:17
  19.2 28.0 %collective-permute-start.4 = (bf16[2,5,96,384]{3,2,1,0:T(8,128)(2,1)}, bf16[2,5,96,384]{3,2,1,0:T(8,128)(2,1)S(1)}, u32[]{:S(2)}, u32[]{:S(2)}) collective-permute-start(bf16[2,5,96,384]{3,2,1,0:T(8,128)(2,1)} %bitcast.20), channel_id=1, source_target_pairs={{0,28},{1,29},{2,30},{3,31},{4,0},{5,1},{6,2},{7,3},{8,4},{9,5},{1... | collective-permute-start | bytes 2211848 | tf_op jit(solution)/shard_map/ppermute | solution.py:22
  24.2 23.0 %collective-permute-start.3 = (bf16[2,5,96,384]{3,2,1,0:T(8,128)(2,1)}, bf16[2,5,96,384]{3,2,1,0:T(8,128)(2,1)S(1)}, u32[]{:S(2)}, u32[]{:S(2)}) collective-permute-start(bf16[2,5,96,384]{3,2,1,0:T(8,128)(2,1)} %bitcast.21), channel_id=1, source_target_pairs={{0,4},{1,5},{2,6},{3,7},{4,8},{5,9},{6,10},{7,11},{8,12},{9,13},{1... | collective-permute-start | bytes 2211848 | tf_op jit(solution)/shard_map/ppermute | solution.py:22
  29.1 18.1 %collective-permute-start.8 = (bf16[256,768]{1,0:T(8,128)(2,1)}, bf16[256,768]{1,0:T(8,128)(2,1)S(1)}, u32[]{:S(2)}, u32[]{:S(2)}) collective-permute-start(bf16[256,768]{1,0:T(8,128)(2,1)} %constant_dynamic-slice_fusion.1), channel_id=1, source_target_pairs={{0,32},{32,0},{64,96},{96,64},{128,160},{160,128},{192,224},{224,1... | collective-permute-start | bytes 1179656 | tf_op jit(solution)/shard_map/ppermute | solution.py:17
  47.3 29.1 %collective-permute-start.9 = (bf16[2,5,96,384]{3,2,1,0:T(8,128)(2,1)S(1)}, bf16[2,5,96,384]{3,2,1,0:T(8,128)(2,1)}, u32[]{:S(2)}, u32[]{:S(2)}) collective-permute-start(bf16[2,5,96,384]{3,2,1,0:T(8,128)(2,1)S(1)} %collective-permute-done.3.refs_1_), channel_id=1, source_target_pairs={{0,4},{1,5},{2,6},{3,7},{4,8},{5,9},{6,10},{7,11},{8,12},{9,13},{1... | collective-permute-start | bytes 2211848 | tf_op jit(solution)/shard_map/ppermute | solution.py:22
  49.8 26.5 %collective-permute-start.10 = (bf16[2,5,96,384]{3,2,1,0:T(8,128)(2,1)S(1)}, bf16[2,5,96,384]{3,2,1,0:T(8,128)(2,1)}, u32[]{:S(2)}, u32[]{:S(2)}) collective-permute-start(bf16[2,5,96,384]{3,2,1,0:T(8,128)(2,1)S(1)} %collective-permute-done.4.refs_2_), channel_id=1, source_target_pairs={{0,28},{1,29},{2,30},{3,31},{4,0},{5,1},{6,2},{7,3},{8,4},{9,5},{1... | collective-permute-start | bytes 2211848 | tf_op jit(solution)/shard_map/ppermute | solution.py:22
  56.3 11.2 %collective-permute-start.13 = (bf16[256,768]{1,0:T(8,128)(2,1)S(1)}, bf16[256,768]{1,0:T(8,128)(2,1)}, u32[]{:S(2)}, u32[]{:S(2)}) collective-permute-start(bf16[256,768]{1,0:T(8,128)(2,1)S(1)} %constant_dynamic-slice_fusion), channel_id=1, source_target_pairs={{0,128},{32,160},{64,192},{96,224},{128,0},{160,32},{192,64},{224,... | collective-permute-start | bytes 1179656 | tf_op jit(solution)/shard_map/ppermute | solution.py:17
  59.3 17.0 %collective-permute-start.12 = (bf16[256,768]{1,0:T(8,128)(2,1)S(1)}, bf16[256,768]{1,0:T(8,128)(2,1)}, u32[]{:S(2)}, u32[]{:S(2)}) collective-permute-start(bf16[256,768]{1,0:T(8,128)(2,1)S(1)} %constant_dynamic-slice_fusion), channel_id=1, source_target_pairs={{0,64},{32,96},{64,0},{96,32},{128,192},{160,224},{192,128},{224,1... | collective-permute-start | bytes 1179656 | tf_op jit(solution)/shard_map/ppermute | solution.py:17
  59.7 16.6 %collective-permute-start.11 = (bf16[256,768]{1,0:T(8,128)(2,1)S(1)}, bf16[256,768]{1,0:T(8,128)(2,1)S(1)}, u32[]{:S(2)}, u32[]{:S(2)}) collective-permute-start(bf16[256,768]{1,0:T(8,128)(2,1)S(1)} %constant_dynamic-slice_fusion), channel_id=1, source_target_pairs={{0,32},{32,0},{64,96},{96,64},{128,160},{160,128},{192,224},{224,1... | collective-permute-start | bytes 1179656 | tf_op jit(solution)/shard_map/ppermute | solution.py:17
  79.2 19.1 %collective-permute-start.16 = (bf16[256,1536]{1,0:T(8,128)(2,1)}, bf16[256,1536]{1,0:T(8,128)(2,1)}, u32[]{:S(2)}, u32[]{:S(2)}) collective-permute-start(bf16[256,1536]{1,0:T(8,128)(2,1)} %collective-permute-done.5.refs_9_), channel_id=1, source_target_pairs={{0,1},{1,0},{2,3},{3,2},{4,5},{5,4},{6,7},{7,6},{8,9},{9,8},{10,11... | collective-permute-start | bytes 2359304 | tf_op jit(solution)/shard_map/ppermute | solution.py:17
  79.2 19.1 %collective-permute-start.14 = (bf16[2,5,96,384]{3,2,1,0:T(8,128)(2,1)}, bf16[2,5,96,384]{3,2,1,0:T(8,128)(2,1)}, u32[]{:S(2)}, u32[]{:S(2)}) collective-permute-start(bf16[2,5,96,384]{3,2,1,0:T(8,128)(2,1)} %collective-permute-done.9.refs_3_), channel_id=1, source_target_pairs={{0,4},{1,5},{2,6},{3,7},{4,8},{5,9},{6,10},{7,11},{8,12},{9,13},{1... | collective-permute-start | bytes 2211848 | tf_op jit(solution)/shard_map/ppermute | solution.py:22
  79.2 19.1 %collective-permute-start.15 = (bf16[2,5,96,384]{3,2,1,0:T(8,128)(2,1)}, bf16[2,5,96,384]{3,2,1,0:T(8,128)(2,1)}, u32[]{:S(2)}, u32[]{:S(2)}) collective-permute-start(bf16[2,5,96,384]{3,2,1,0:T(8,128)(2,1)} %collective-permute-done.10.refs_4_), channel_id=1, source_target_pairs={{0,28},{1,29},{2,30},{3,31},{4,0},{5,1},{6,2},{7,3},{8,4},{9,5},{1... | collective-permute-start | bytes 2211848 | tf_op jit(solution)/shard_map/ppermute | solution.py:22
  101.9 9.1 %collective-permute-start.21 = (bf16[1,5,96,384]{3,2,1,0:T(8,128)(2,1)}, bf16[1,5,96,384]{3,2,1,0:T(8,128)(2,1)}, u32[]{:S(2)}, u32[]{:S(2)}) collective-permute-start(bf16[1,5,96,384]{3,2,1,0:T(8,128)(2,1)} %slice.19), channel_id=1, source_target_pairs={{0,28},{1,29},{2,30},{3,31},{4,0},{5,1},{6,2},{7,3},{8,4},{9,5},{1... | collective-permute-start | bytes 1105928 | tf_op jit(solution)/shard_map/ppermute | solution.py:22
  104.2 9.7 %collective-permute-start.20 = (bf16[1,5,96,384]{3,2,1,0:T(8,128)(2,1)}, bf16[1,5,96,384]{3,2,1,0:T(8,128)(2,1)}, u32[]{:S(2)}, u32[]{:S(2)}) collective-permute-start(bf16[1,5,96,384]{3,2,1,0:T(8,128)(2,1)} %slice.18), channel_id=1, source_target_pairs={{0,4},{1,5},{2,6},{3,7},{4,8},{5,9},{6,10},{7,11},{8,12},{9,13},{1... | collective-permute-start | bytes 1105928 | tf_op jit(solution)/shard_map/ppermute | solution.py:22
  105.0 27.3 %collective-permute-start.22 = (bf16[256,1536]{1,0:T(8,128)(2,1)S(1)}, bf16[256,1536]{1,0:T(8,128)(2,1)}, u32[]{:S(2)}, u32[]{:S(2)}) collective-permute-start(bf16[256,1536]{1,0:T(8,128)(2,1)S(1)} %copy-done.3), channel_id=1, source_target_pairs={{0,1},{1,0},{2,3},{3,2},{4,5},{5,4},{6,7},{7,6},{8,9},{9,8},{10,11... | collective-permute-start | bytes 2359304 | tf_op jit(solution)/shard_map/ppermute | solution.py:17
  107.9 22.8 %collective-permute-start.23 = (bf16[256,768]{1,0:T(8,128)(2,1)}, bf16[256,768]{1,0:T(8,128)(2,1)S(1)}, u32[]{:S(2)}, u32[]{:S(2)}) collective-permute-start(bf16[256,768]{1,0:T(8,128)(2,1)} %copy-done.8), channel_id=1, source_target_pairs={{0,1},{1,0},{2,3},{3,2},{4,5},{5,4},{6,7},{7,6},{8,9},{9,8},{10,11... | collective-permute-start | bytes 1179656 | tf_op jit(solution)/shard_map/ppermute | solution.py:17
  108.0 24.3 %collective-permute-start.24 = (bf16[256,768]{1,0:T(8,128)(2,1)}, bf16[256,768]{1,0:T(8,128)(2,1)S(1)}, u32[]{:S(2)}, u32[]{:S(2)}) collective-permute-start(bf16[256,768]{1,0:T(8,128)(2,1)} %collective-permute-done.6.refs_13_), channel_id=1, source_target_pairs={{0,1},{1,0},{2,3},{3,2},{4,5},{5,4},{6,7},{7,6},{8,9},{9,8},{10,11... | collective-permute-start | bytes 1179656 | tf_op jit(solution)/shard_map/ppermute | solution.py:17
  110.9 21.4 %collective-permute-start.25 = (bf16[256,768]{1,0:T(8,128)(2,1)S(1)}, bf16[256,768]{1,0:T(8,128)(2,1)S(1)}, u32[]{:S(2)}, u32[]{:S(2)}) collective-permute-start(bf16[256,768]{1,0:T(8,128)(2,1)S(1)} %collective-permute-done.7.refs_15_), channel_id=1, source_target_pairs={{0,1},{1,0},{2,3},{3,2},{4,5},{5,4},{6,7},{7,6},{8,9},{9,8},{10,11... | collective-permute-start | bytes 1179656 | tf_op jit(solution)/shard_map/ppermute | solution.py:17
  128.0 12.7 %collective-permute-start.28 = (bf16[256,384]{1,0:T(8,128)(2,1)S(1)}, bf16[256,384]{1,0:T(8,128)(2,1)S(1)}, u32[]{:S(2)}, u32[]{:S(2)}) collective-permute-start(bf16[256,384]{1,0:T(8,128)(2,1)S(1)} %get-tuple-element.78), channel_id=1, source_target_pairs={{0,3},{1,2},{2,1},{3,0},{4,7},{5,6},{6,5},{7,4},{8,11},{9,10},{10,... | collective-permute-start | bytes 589832 | tf_op jit(solution)/shard_map/ppermute | solution.py:17
  130.8 9.9 %collective-permute-start.27 = (bf16[256,384]{1,0:T(8,128)(2,1)S(1)}, bf16[256,384]{1,0:T(8,128)(2,1)S(1)}, u32[]{:S(2)}, u32[]{:S(2)}) collective-permute-start(bf16[256,384]{1,0:T(8,128)(2,1)S(1)} %get-tuple-element.79), channel_id=1, source_target_pairs={{0,2},{1,3},{2,0},{3,1},{4,6},{5,7},{6,4},{7,5},{8,10},{9,11},{10,... | collective-permute-start | bytes 589832 | tf_op jit(solution)/shard_map/ppermute | solution.py:17
  (23 other events, 652.9 us)
where the time goes:
time: 170 us; the launch traced here: 169 us
  waiting for transfers between devices  61.1 us (36%)
  starting transfers between devices  42.3 us (25%)
  blocking collectives  23.8 us (14%)
  Pallas kernels  22.8 us (13%)
  local copies, waits for them, and re-layouts  15.3 us (9%)
    ppermute x21, waiting for transfers between devices, swapped(): lax.ppermute(value, axis, [(i, i ^ mask) for i in range(lax.axis_size(axi...  45.6 us
    ppermute x21, starting transfers between devices, swapped(): lax.ppermute(value, axis, [(i, i ^ mask) for i in range(lax.axis_size(axi...  25.9 us
    pallas_call x2, Pallas kernels, gate_up(): pl.pallas_call(functools.partial(gate_up_kernel, rows=rows, z_count=z_cou...  16.9 us
    ppermute x8, starting transfers between devices, shifted(): lax.ppermute(value, 'tok', [(i, (i + step * GROUP) % count) for i in rang...  16.4 us
    ppermute x8, waiting for transfers between devices, shifted(): lax.ppermute(value, 'tok', [(i, (i + step * GROUP) % count) for i in rang...  15.5 us
    all_to_all x1, blocking collectives, per_device(): terms = lax.all_to_all(parts, 'feat', 0, 0)  12.7 us
    all_to_all x1, blocking collectives, per_device(): lax.all_to_all(jnp.broadcast_to(mine[None], parts.shape), 'feat', 0, 0)  11 us
    unnamed x36, local copies, waits for them, and re-layouts  8.63 us
  transfers between devices with their start and end apart: 29, of which 12 were waited for; matrix products, arithmetic and copies ran while one was open for 3% of the time, Pallas kernels for 11%

commit v1 on v0

v1 whole, which is shorter than its diff:
```python
import functools
import jax
import jax.numpy as jnp
from jax import lax
from jax.experimental import pallas as pl
from jax.experimental.pallas import tpu as pltpu
from jax.sharding import PartitionSpec as P

GROUP = 4
HBM = pl.BlockSpec(memory_space=pltpu.HBM)
SMEM = pl.BlockSpec(memory_space=pltpu.SMEM)
VMEM = pl.BlockSpec(memory_space=pltpu.VMEM)
VMEM_BYTES = 60 * 2**20
SMALL_BYTES = 16 * 2**20
ANY = pl.BlockSpec(memory_space=pl.ANY)


def swapped(value, axis, mask):
    return lax.ppermute(value, axis, [(i, i ^ mask) for i in range(lax.axis_size(axis))])


def shifted(value, step):
    count = lax.axis_size("tok")
    return lax.ppermute(value, "tok", [(i, (i + step * GROUP) % count) for i in range(count)])


def pack_kernel(own_ref, gate_ref, up_ref, *out_refs):
    half = gate_ref.shape[3] // 2
    for m in range(4):
        to = own_ref[0] ^ m
        at = pl.ds(pl.multiple_of(to % 2 * half, 128), half)
        for side, ref in enumerate((gate_ref, up_ref)):
            out_refs[m][side] = ref[to // 2, :, :, at]


def place_kernel(own_ref, *refs):
    for m in range(4):
        refs[4][:, :, own_ref[0] ^ m] = refs[m][...]


def halves_kernel(f_ref, b_ref, f_out, b_out, sem):
    copies = [
        pltpu.make_async_copy(f_ref.at[pl.ds(0, 1)], f_out, sem.at[0]),
        pltpu.make_async_copy(b_ref.at[pl.ds(1, 1)], b_out, sem.at[1]),
    ]
    for copy in copies:
        copy.start()
    for copy in copies:
        copy.wait()


def join_kernel(*refs):
    t_ref, s_ref, x_ref, *y_refs = refs[:7]
    own_out, partner_out, sem = refs[7:]
    rows = t_ref.shape[0]
    pairs = [(t_ref, own_out.at[pl.ds(0, rows)]), (s_ref, own_out.at[pl.ds(rows, rows)]), (x_ref, partner_out.at[0])]
    for i, y_ref in enumerate(y_refs):
        pairs.append((y_ref, partner_out.at[1 + i // 2, pl.ds(i % 2 * rows, rows)]))
    copies = [pltpu.make_async_copy(source, there, sem.at[i]) for i, (source, there) in enumerate(pairs)]
    for copy in copies:
        copy.start()
    for copy in copies:
        copy.wait()


def token_copies(own_refs, partner_refs, x_mem, x_sem, x_lo, first, rows, start, width):
    blk = partner_refs[0].shape[2]
    copies = []
    for j in range(5):
        mine = []
        for core in range(2):
            if j < 2:
                column = pl.multiple_of((x_lo ^ j) * blk + start, 128)
                source = own_refs[core].at[pl.ds(first, rows), pl.ds(column, width)]
            else:
                column = pl.multiple_of(start, 128)
                source = partner_refs[core].at[j - 2, pl.ds(first, rows), pl.ds(column, width)]
            mine.append(pltpu.make_async_copy(source, x_mem.at[j, pl.ds(core * rows, rows)], x_sem.at[core, j]))
        copies.append(mine)
    return copies


def early_kernel(place_ref, gs_ref, us_ref, *refs, z_count):
    n_w = z_count - 1
    w_refs, own_refs, partner_refs, acc = refs[:n_w], refs[n_w : n_w + 2], refs[n_w + 2 : n_w + 4], refs[n_w + 4]
    x_mem, w_mem, x_sem, w_sem = refs[n_w + 5 :]
    x_lo, z = place_ref[5], place_ref[6]
    _, blk, both = w_mem.shape
    share, width = blk // z_count, both // 2
    copies = token_copies(own_refs, partner_refs, x_mem, x_sem, x_lo, 0, own_refs[0].shape[0], 0, blk)
    for j in range(5):
        for i, ref in enumerate(w_refs):
            origin = z - (i + 1) // 2 if i % 2 else z + i // 2
            at = pl.ds(pl.multiple_of((origin + z_count) % z_count * share, 16), share)
            for side in range(2):
                there = w_mem.at[j, at, pl.ds(side * width, width)]
                copies[j].append(pltpu.make_async_copy(ref.at[side, place_ref[j]], there, w_sem.at[j, i, side]))
        for copy in copies[j]:
            copy.start()
    last = pl.ds(pl.multiple_of((z + z_count // 2) % z_count * share, 16), share)
    for j in range(5):
        w_mem[j, last] = jnp.zeros((share, both), w_mem.dtype)
    for j in range(5):
        for copy in copies[j]:
            copy.wait()
        term = jnp.dot(x_mem[j], w_mem[j], preferred_element_type=jnp.float32)
        g, u = term[:, :width] * gs_ref[place_ref[j]], term[:, width:] * us_ref[place_ref[j]]
        if j == 0:
            acc[:, :width] = g
            acc[:, width:] = u
        else:
            acc[:, :width] += g
            acc[:, width:] += u


def early(place, gs, us, weights, own_rows, partner_rows):
    rows, features = own_rows[0].shape
    rows //= 2
    blk = features // 2
    _, slots, share, width = weights[0].shape
    z_count = blk // share
    return pl.pallas_call(
        functools.partial(early_kernel, z_count=z_count),
        out_shape=jax.ShapeDtypeStruct((4 * rows, 2 * width), jnp.float32),
        in_specs=[SMEM] * 3 + [HBM] * (len(weights) + 4),
        out_specs=VMEM,
        scratch_shapes=[
            pltpu.VMEM((slots, 4 * rows, blk), jnp.bfloat16),
            pltpu.VMEM((slots, blk, 2 * width), jnp.bfloat16),
            pltpu.SemaphoreType.DMA((2, slots)),
            pltpu.SemaphoreType.DMA((slots, z_count - 1, 2)),
        ],
        compiler_params=pltpu.CompilerParams(vmem_limit_bytes=VMEM_BYTES),
        cost_estimate=pl.CostEstimate(
            flops=2 * 2 * 4 * rows * slots * blk * width, bytes_accessed=17 * 2**20, transcendentals=0
        ),
    )(place, gs, us, *weights, *own_rows, *partner_rows)


def late_kernel(place_ref, gs_ref, us_ref, *refs, z_count, window, first):
    w_refs, acc_ref, own_refs, partner_refs, out_refs = refs[:2], refs[2], refs[3:5], refs[5:7], refs[7:9]
    x_mem, w_mem, acc, x_sem, w_sem, acc_sem = refs[9:]
    x_lo, z = place_ref[5], place_ref[6]
    share, width = w_refs[0].shape[2:]
    rows, blk = own_refs[0].shape[0] // 2, own_refs[0].shape[1] // 2
    row = (z + z_count // 2) % z_count * share
    start = jnp.minimum(row // 128 * 128, blk - window)
    at = pl.ds(pl.multiple_of(row - start, 16), share)
    acc_copies = [
        pltpu.make_async_copy(
            acc_ref.at[pl.ds((2 * core + first) * rows, rows)], acc.at[pl.ds(core * rows, rows)], acc_sem.at[core]
        )
        for core in range(2)
    ]
    copies = token_copies(own_refs, partner_refs, x_mem, x_sem, x_lo, first * rows, rows, start, window)
    for mine in copies:
        for copy in mine:
            copy.start()
    for copy in acc_copies:
        copy.start()
    w_mem[...] = jnp.zeros_like(w_mem)
    w_copies = []
    for j in range(5):
        w_copies.append([])
        for side in range(2):
            there = w_mem.at[j, at, pl.ds(side * width, width)]
            w_copies[j].append(pltpu.make_async_copy(w_refs[side].at[0, place_ref[j]], there, w_sem.at[j, side]))
            w_copies[j][side].start()
    for copy in acc_copies:
        copy.wait()
    for j in range(5):
        for copy in copies[j] + w_copies[j]:
            copy.wait()
        term = jnp.dot(x_mem[j], w_mem[j], preferred_element_type=jnp.float32)
        acc[:, :width] += term[:, :width] * gs_ref[place_ref[j]]
        acc[:, width:] += term[:, width:] * us_ref[place_ref[j]]
    g = acc[:, :width]
    out = (g / (1.0 + jnp.exp(-g)) * acc[:, width:]).astype(jnp.bfloat16)
    out_refs[0][...] = out[:rows]
    out_refs[1][...] = out[rows:]


def late(place, gs, us, weights, acc, own_rows, partner_rows, first):
    rows, features = own_rows[0].shape
    rows //= 2
    blk = features // 2
    _, slots, share, width = weights[0].shape
    window = min(2 * 128 * ((share + 127) // 128), blk)
    return pl.pallas_call(
        functools.partial(late_kernel, z_count=blk // share, window=window, first=first),
        out_shape=[jax.ShapeDtypeStruct((rows, width), jnp.bfloat16)] * 2,
        in_specs=[SMEM] * 3 + [HBM] * 7,
        out_specs=[VMEM] * 2,
        scratch_shapes=[
            pltpu.VMEM((slots, 2 * rows, window), jnp.bfloat16),
            pltpu.VMEM((slots, window, 2 * width), jnp.bfloat16),
            pltpu.VMEM((2 * rows, 2 * width), jnp.float32),
            pltpu.SemaphoreType.DMA((2, slots)),
            pltpu.SemaphoreType.DMA((slots, 2)),
            pltpu.SemaphoreType.DMA((2,)),
        ],
        compiler_params=pltpu.CompilerParams(vmem_limit_bytes=VMEM_BYTES),
        cost_estimate=pl.CostEstimate(
            flops=2 * 2 * 2 * rows * slots * window * width, bytes_accessed=4 * 2**20, transcendentals=2 * rows * width
        ),
    )(place, gs, us, *weights, acc, *own_rows, *partner_rows)


def latent_kernel(own_ref, lin_ref, *refs):
    pieces, hidden_ref, part_ref = refs[:4], refs[4], refs[5]
    width = pieces[0].shape[1]
    total = None
    for m in range(4):
        at = pl.ds(pl.multiple_of((own_ref[0] ^ m) * width, width), width)
        piece = pieces[m][...]
        hidden_ref[:, at] = piece
        term = jnp.dot(piece, lin_ref[at], preferred_element_type=jnp.float32)
        total = term if total is None else total + term
    part_ref[...] = total.astype(jnp.bfloat16)


def per_device(tokens, gate_weight, up_weight, gate_scale, up_scale, partners, latent_in, latent_out):
    rows, features = tokens.shape
    blocks, slots, share, blk = gate_weight.shape
    feat_count = lax.axis_size("feat")
    half = blk // 2
    feat, tok = lax.axis_index("feat"), lax.axis_index("tok")
    member, z = tok % GROUP, tok // GROUP
    x_lo, core = member // 2, member % 2
    block_id = feat * blocks + x_lo

    own = member[None].astype(jnp.int32)
    packed = pl.pallas_call(
        pack_kernel,
        out_shape=[jax.ShapeDtypeStruct((2, slots, share, half), jnp.bfloat16)] * 4,
        in_specs=[SMEM, VMEM, VMEM],
        out_specs=[VMEM] * 4,
        compiler_params=pltpu.CompilerParams(vmem_limit_bytes=SMALL_BYTES),
    )(own, gate_weight, up_weight)

    def place(got):
        shape = got[0].shape
        out = pl.pallas_call(
            place_kernel,
            out_shape=jax.ShapeDtypeStruct(shape[:2] + (4,) + shape[2:], jnp.bfloat16),
            in_specs=[SMEM] + [VMEM] * 4,
            out_specs=VMEM,
            compiler_params=pltpu.CompilerParams(vmem_limit_bytes=SMALL_BYTES),
        )(own, *got)
        return out.reshape(shape[:2] + (4 * shape[2],) + shape[3:])

    def block_of(value):
        return lax.dynamic_slice(value, (0, x_lo * blk), (rows, blk))

    def step(forward, back):
        return shifted(forward, 1), shifted(back, -1)

    far = [swapped(packed[m], "tok", m) for m in (2, 3)]
    near = swapped(packed[1], "tok", 1)
    w0 = place([packed[0], near, *far])
    barrier = lax.optimization_barrier
    first = block_of(tokens)
    p0_y1, p0_y2 = swapped(first, "feat", 2), swapped(first, "feat", 4)
    w0, later = barrier((w0, tokens))
    w1 = step(w0, w0)
    s2 = swapped(later, "tok", 2)
    w1, s2, p0_y1, p0_y2, first, later = barrier((w1, s2, p0_y1, p0_y2, first, later))
    w2 = step(*w1)
    second = block_of(s2)
    p_x = swapped(jnp.concatenate([first, second]), "feat", 1)
    p2_y1, p2_y2 = swapped(second, "feat", 2), swapped(second, "feat", 4)
    w2, p_x, p2_y1, p2_y2, p0_y1, p0_y2, s2, later = barrier((w2, p_x, p2_y1, p2_y2, p0_y1, p0_y2, s2, later))
    w3 = step(*w2)
    own0, partner0 = pl.pallas_call(
        join_kernel,
        out_shape=[
            jax.ShapeDtypeStruct((2 * rows, features), jnp.bfloat16),
            jax.ShapeDtypeStruct((3, 2 * rows, blk), jnp.bfloat16),
        ],
        in_specs=[HBM] * 7,
        out_specs=[HBM] * 2,
        scratch_shapes=[pltpu.SemaphoreType.DMA((7,))],
    )(later, s2, p_x, p0_y1, p2_y1, p0_y2, p2_y2)
    own1, partner1 = swapped(own0, "tok", 1), swapped(partner0, "tok", 1)
    w3, own0, own1, partner0, partner1 = barrier((w3, own0, own1, partner0, partner1))
    cut = pl.pallas_call(
        halves_kernel,
        out_shape=[jax.ShapeDtypeStruct((1,) + w3[0].shape[1:], jnp.bfloat16)] * 2,
        in_specs=[ANY] * 2,
        out_specs=[ANY] * 2,
        scratch_shapes=[pltpu.SemaphoreType.DMA((2,))],
        compiler_params=pltpu.CompilerParams(vmem_limit_bytes=SMALL_BYTES),
    )(*w3)
    w4 = step(*cut)

    wanted = lax.dynamic_index_in_dim(partners, block_id, 0, keepdims=False)
    labels = block_id ^ jnp.array([0, 1, 2, 4, 8], jnp.int32)
    order = jnp.sum(jnp.where(labels[:, None] == wanted[None, :], jnp.arange(5, dtype=jnp.int32)[None, :], 0), axis=1)
    here = jnp.concatenate([order, jnp.stack([x_lo, z]).astype(jnp.int32)])
    gs = lax.dynamic_index_in_dim(gate_scale, x_lo, 0, keepdims=False)
    us = lax.dynamic_index_in_dim(up_scale, x_lo, 0, keepdims=False)

    sides = (own0, own1), (partner0, partner1)
    acc = early(here, gs, us, (w0, *w1, *w2, *w3), *sides)
    far_hidden = [swapped(v, "tok", mask) for v, mask in zip(late(here, gs, us, w4, acc, *sides, 1), (2, 3))]
    made = late(here, gs, us, w4, acc, *sides, 0)
    hidden_pieces = [made[0], swapped(made[1], "tok", 1), *far_hidden]
    hidden, part = pl.pallas_call(
        latent_kernel,
        out_shape=(
            jax.ShapeDtypeStruct((rows, features), jnp.bfloat16),
            jax.ShapeDtypeStruct((rows, latent_in.shape[1]), jnp.bfloat16),
        ),
        in_specs=[SMEM] + [VMEM] * 5,
        out_specs=(VMEM, VMEM),
        compiler_params=pltpu.CompilerParams(vmem_limit_bytes=SMALL_BYTES),
        cost_estimate=pl.CostEstimate(flops=2 * rows * features * latent_in.shape[1], bytes_accessed=4 * 2**20, transcendentals=0),
    )(own, latent_in, *hidden_pieces)

    parts = part.reshape(feat_count, rows // feat_count, -1)
    terms = lax.all_to_all(parts, "feat", 0, 0)
    mine = jnp.sum(terms.astype(jnp.float32), axis=0).astype(jnp.bfloat16)
    latent = lax.all_to_all(jnp.broadcast_to(mine[None], parts.shape), "feat", 0, 0).reshape(rows, -1)
    rank_term = jnp.dot(latent, latent_out, preferred_element_type=jnp.float32).astype(jnp.bfloat16)
    return hidden, rank_term


def solution(mesh):
    placed = (
        P("tok", "feat"),
        P("feat", None, "tok", None),
        P("feat", None, "tok", None),
        P("feat", None),
        P("feat", None),
        P(),
        P("feat", None),
        P(None, "feat"),
    )
    return jax.shard_map(
        per_device,
        mesh=mesh,
        in_specs=placed,
        out_specs=(P("tok", "feat"), P("tok", "feat")),
        check_vma=False,
    )
```

time: 170 us -> 280 us (1.65)
  Pallas kernels: 22.8 us -> 150 us
  starting transfers between devices: 42.3 us -> 32.7 us
  local copies, waits for them, and re-layouts: 15.3 us -> 10.8 us
  waiting for transfers between devices: 61.1 us -> 56.7 us
    pallas_call x2 -> x5, Pallas kernels: 16.9 us -> 148 us  [the longest x1 120 us: per_device(): pl.pallas_call(join_kernel, out_shape=[jax.ShapeDtypeStruct((2 * rows, fe...]
    ppermute x21 -> x14, starting transfers between devices: 25.9 us -> 19.6 us  [swapped(): lax.ppermute(value, axis, [(i, i ^ mask) for i in range(lax.axis_size(axi...]
    ppermute x21 -> x14, waiting for transfers between devices: 45.6 us -> 41.9 us  [swapped(): lax.ppermute(value, axis, [(i, i ^ mask) for i in range(lax.axis_size(axi...]
    slice x2 -> x0, local copies, waits for them, and re-layouts: 3.58 us -> none  [per_device(): w4 = step(w3[0][:1], w3[1][1:])]
    ppermute x8, starting transfers between devices: 16.4 us -> 13.1 us  [shifted(): lax.ppermute(value, 'tok', [(i, (i + step * GROUP) % count) for i in rang...]
    unnamed x36 -> x34, local copies, waits for them, and re-layouts: 8.63 us -> 8.01 us
  transfers between devices with their start and end apart: 29 -> 22, of which waited for: 12 -> 8; matrix products, arithmetic and copies ran while one was open for 3% -> 1% of each run, Pallas kernels for 11% -> 7%
where the time goes in v1:
time: 280 us
  Pallas kernels  150 us (54%)
  waiting for transfers between devices  56.7 us (20%)
  starting transfers between devices  32.7 us (12%)
  blocking collectives  26.3 us (9%)
  local copies, waits for them, and re-layouts  10.8 us (4%)
    pallas_call x1, Pallas kernels, per_device(): pl.pallas_call(join_kernel, out_shape=[jax.ShapeDtypeStruct((2 * rows, fe...  120 us
    ppermute x14, waiting for transfers between devices, swapped(): lax.ppermute(value, axis, [(i, i ^ mask) for i in range(lax.axis_size(axi...  41.9 us
    ppermute x14, starting transfers between devices, swapped(): lax.ppermute(value, axis, [(i, i ^ mask) for i in range(lax.axis_size(axi...  19.6 us
    all_to_all x1, blocking collectives, per_device(): terms = lax.all_to_all(parts, 'feat', 0, 0)  15 us
    ppermute x8, waiting for transfers between devices, shifted(): lax.ppermute(value, 'tok', [(i, (i + step * GROUP) % count) for i in rang...  14.8 us
    pallas_call x1, Pallas kernels, early(): pl.pallas_call(functools.partial(early_kernel, z_count=z_count), out_shap...  14.6 us
    ppermute x8, starting transfers between devices, shifted(): lax.ppermute(value, 'tok', [(i, (i + step * GROUP) % count) for i in rang...  13.1 us
    pallas_call x2, Pallas kernels, late(): pl.pallas_call(functools.partial(late_kernel, z_count=blk // share, windo...  11.8 us
  transfers between devices with their start and end apart: 22, of which 8 were waited for; matrix products, arithmetic and copies ran while one was open for 1% of the time, Pallas kernels for 7%

profile of v1, /device:TPU:1, one launch (start us, length us, event | category | flops | bytes accessed | tf_op | source)
XLA Modules:
  0.0 279.7 jit_solution(14387141302008804354)
XLA Ops:
  2.9 3.3 %collective-permute-start = (bf16[2,5,24,384]{3,2,1,0:T(8,128)(2,1)S(1)}, bf16[2,5,24,384]{3,2,1,0:T(8,128)(2,1)S(1)}, u32[]{:S(2)}, u32[]{:S(2)}) collective-permute-start(bf16[2,5,24,384]{3,2,1,0:T(8,128)(2,1)S(1)} %get-tuple-element.41), channel_id=1, source_target_pairs={{0,1},{1,0},{2,3},{3,2},{4,5},{5,4},{6,7},{7,6},{8,9},{9,8},{10,11... | collective-permute-start | bytes 552968 | tf_op jit(solution)/shard_map/ppermute | solution.py:19
  6.2 1.7 collective-permute-start.2
  7.9 4.5 %collective-permute-done.1.refs_2_ = bf16[2,5,24,384]{3,2,1,0:T(8,128)(2,1)S(1)} collective-permute-done((bf16[2,5,24,384]{3,2,1,0:T(8,128)(2,1)S(1)}, bf16[2,5,24,384]{3,2,1,0:T(8,128)(2,1)S(1)}, u32[]{:S(2)}, u32[]{:S(2)}) %collective-permute-start.1) | collective-permute-done | bytes 184352 | tf_op jit(solution)/shard_map/ppermute | solution.py:19
  12.4 4.1 %collective-permute-done.2.refs_3_ = bf16[2,5,24,384]{3,2,1,0:T(8,128)(2,1)S(1)} collective-permute-done((bf16[2,5,24,384]{3,2,1,0:T(8,128)(2,1)S(1)}, bf16[2,5,24,384]{3,2,1,0:T(8,128)(2,1)S(1)}, u32[]{:S(2)}, u32[]{:S(2)}) %collective-permute-start.2) | collective-permute-done | bytes 184352 | tf_op jit(solution)/shard_map/ppermute | solution.py:19
  16.7 5.0 %collective-permute-start.4 = (bf16[2,5,96,384]{3,2,1,0:T(8,128)(2,1)S(1)}, bf16[2,5,96,384]{3,2,1,0:T(8,128)(2,1)}, u32[]{:S(2)}, u32[]{:S(2)}) collective-permute-start(bf16[2,5,96,384]{3,2,1,0:T(8,128)(2,1)S(1)} %bitcast.12), channel_id=1, source_target_pairs={{0,28},{1,29},{2,30},{3,31},{4,0},{5,1},{6,2},{7,3},{8,4},{9,5},{1... | collective-permute-start | bytes 2211848 | tf_op jit(solution)/shard_map/ppermute | solution.py:24
  22.8 3.0 %collective-permute-start.7 = (bf16[256,768]{1,0:T(8,128)(2,1)S(1)}, bf16[256,768]{1,0:T(8,128)(2,1)S(1)}, u32[]{:S(2)}, u32[]{:S(2)}) collective-permute-start(bf16[256,768]{1,0:T(8,128)(2,1)S(1)} %constant_dynamic-slice_fusion.1), channel_id=1, source_target_pairs={{0,128},{32,160},{64,192},{96,224},{128,0},{160,32},{192,64},{224,... | collective-permute-start | bytes 1179656 | tf_op jit(solution)/shard_map/ppermute | solution.py:19
  26.2 8.1 %collective-permute-done.7.refs_5_ = bf16[256,768]{1,0:T(8,128)(2,1)S(1)} collective-permute-done((bf16[256,768]{1,0:T(8,128)(2,1)S(1)}, bf16[256,768]{1,0:T(8,128)(2,1)S(1)}, u32[]{:S(2)}, u32[]{:S(2)}) %collective-permute-start.7) | collective-permute-done | bytes 393248 | tf_op jit(solution)/shard_map/ppermute | solution.py:19
  34.2 8.8 %collective-permute-done.6.refs_3_ = bf16[256,768]{1,0:T(8,128)(2,1)S(1)} collective-permute-done((bf16[256,768]{1,0:T(8,128)(2,1)S(1)}, bf16[256,768]{1,0:T(8,128)(2,1)S(1)}, u32[]{:S(2)}, u32[]{:S(2)}) %collective-permute-start.6) | collective-permute-done | bytes 393248 | tf_op jit(solution)/shard_map/ppermute | solution.py:19
  44.9 2.5 collective-permute-start.10
  47.4 2.7 collective-permute-start.9
  51.7 8.2 %collective-permute-done.12.refs_6_ = bf16[256,768]{1,0:T(8,128)(2,1)S(1)} collective-permute-done((bf16[256,768]{1,0:T(8,128)(2,1)S(1)}, bf16[256,768]{1,0:T(8,128)(2,1)S(1)}, u32[]{:S(2)}, u32[]{:S(2)}) %collective-permute-start.12) | collective-permute-done | bytes 393248 | tf_op jit(solution)/shard_map/ppermute | solution.py:19
  59.8 6.7 %collective-permute-done.11.refs_4_ = bf16[256,768]{1,0:T(8,128)(2,1)S(1)} collective-permute-done((bf16[256,768]{1,0:T(8,128)(2,1)S(1)}, bf16[256,768]{1,0:T(8,128)(2,1)S(1)}, u32[]{:S(2)}, u32[]{:S(2)}) %collective-permute-start.11) | collective-permute-done | bytes 393248 | tf_op jit(solution)/shard_map/ppermute | solution.py:19
  69.0 120.3 %shard_map.106 = (bf16[512,1536]{1,0:T(8,128)(2,1)}, bf16[3,512,768]{2,1,0:T(8,128)(2,1)}) custom-call(bf16[256,1536]{1,0:T(8,128)(2,1)} %refs_0_, bf16[256,1536]{1,0:T(8,128)(2,1)} %collective-permute-done.5.refs_1_, bf16[512,768]{1,0:T(8,128)(2,1)} %collective-permute-done.10.refs_2_, bf16[256,768]{1,0:T(8,128)(2,1)} %copy-done.8, ...), custom_call_target="tpu_custom_call" | custom-call | tf_op jit(solution)/shard_map/pallas_call | solution.py:274
  189.3 3.2 %collective-permute-start.16 = (bf16[3,512,768]{2,1,0:T(8,128)(2,1)}, bf16[3,512,768]{2,1,0:T(8,128)(2,1)}, u32[]{:S(2)}, u32[]{:S(2)}) collective-permute-start(bf16[3,512,768]{2,1,0:T(8,128)(2,1)} %get-tuple-element.70.refs_9_.refs_5_), channel_id=1, source_target_pairs={{0,1},{1,0},{2,3},{3,2},{4,5},{5,4},{6,7},{7,6},{8,9},{9,8},{10,11... | collective-permute-start | bytes 7077896 | tf_op jit(solution)/shard_map/ppermute | solution.py:19
  192.7 2.7 collective-permute-start.14
  197.0 14.8 %collective-permute-done.13.f_ref.refs_5_ = bf16[2,5,96,384]{3,2,1,0:T(8,128)(2,1)S(1)} collective-permute-done((bf16[2,5,96,384]{3,2,1,0:T(8,128)(2,1)}, bf16[2,5,96,384]{3,2,1,0:T(8,128)(2,1)S(1)}, u32[]{:S(2)}, u32[]{:S(2)}) %collective-permute-start.13) | collective-permute-done | bytes 737312 | tf_op jit(solution)/shard_map/ppermute | solution.py:24
  213.1 2.7 collective-permute-start.18
  215.8 14.6 %shard_map.108.refs_2_ = f32[1024,768]{1,0:T(8,128)} custom-call(s32[7]{0:T(128)} %pad_add_fusion.place_ref, f32[5]{0:T(128)} %get-tuple-element.78.gs_ref, f32[5]{0:T(128)} %get-tuple-element.79.us_ref, bf16[2,5,96,384]{3,2,1,0:T(8,128)(2,1)} %bitcast.14, bf16[2,5,96,384]{3,2,1,0:T(8,128)(2,1)} %collective-permute-done.3.refs_1_, ...), custom_call_target="tpu_custom_call" | custom-call | flops 6039797760 | bytes 17825792 | tf_op jit(solution)/shard_map/pallas_call | solution.py:122
  230.4 5.9 %shard_map.110 = (bf16[256,384]{1,0:T(8,128)(2,1)}, bf16[256,384]{1,0:T(8,128)(2,1)}) custom-call(s32[7]{0:T(128)} %pad_add_fusion.place_ref, f32[5]{0:T(128)} %get-tuple-element.78.gs_ref, f32[5]{0:T(128)} %get-tuple-element.79.us_ref, bf16[1,5,96,384]{3,2,1,0:T(8,128)(2,1)} %collective-permute-done.17.refs_0_, ...), custom_call_target="tpu_custom_call" | custom-call | flops 1006632960 | bytes 4194304 | tf_op jit(solution)/shard_map/pallas_call | solution.py:189
  236.4 3.4 %collective-permute-start.21 = (bf16[256,384]{1,0:T(8,128)(2,1)}, bf16[256,384]{1,0:T(8,128)(2,1)S(1)}, u32[]{:S(2)}, u32[]{:S(2)}) collective-permute-start(bf16[256,384]{1,0:T(8,128)(2,1)} %get-tuple-element.75), channel_id=1, source_target_pairs={{0,3},{1,2},{2,1},{3,0},{4,7},{5,6},{6,5},{7,4},{8,11},{9,10},{10,... | collective-permute-start | bytes 589832 | tf_op jit(solution)/shard_map/ppermute | solution.py:19
  239.8 5.9 %shard_map.109 = (bf16[256,384]{1,0:T(8,128)(2,1)}, bf16[256,384]{1,0:T(8,128)(2,1)}) custom-call(s32[7]{0:T(128)} %pad_add_fusion.place_ref, f32[5]{0:T(128)} %get-tuple-element.78.gs_ref, f32[5]{0:T(128)} %get-tuple-element.79.us_ref, bf16[1,5,96,384]{3,2,1,0:T(8,128)(2,1)} %collective-permute-done.17.refs_0_, ...), custom_call_target="tpu_custom_call" | custom-call | flops 1006632960 | bytes 4194304 | tf_op jit(solution)/shard_map/pallas_call | solution.py:189
  247.5 1.7 copy-done.1
  251.6 15.0 %all_to_all.10 = bf16[8,32,768]{2,1,0:T(8,128)(2,1)S(1)} all-to-all(bf16[8,32,768]{2,1,0:T(8,128)(2,1)S(1)} %bitcast.15), channel_id=1, replica_groups=mesh['feat'=8,'tok'=32] {'feat'}, dimensions={0} | all-to-all | bytes 786432 | tf_op jit(solution)/shard_map/all_to_all | solution.py:321
  266.8 11.2 %all_to_all.11 = bf16[8,32,768]{2,1,0:T(8,128)(2,1)S(1)} all-to-all(bf16[8,32,768]{2,1,0:T(8,128)(2,1)S(1)} %broadcast_in_dim.27), channel_id=1, replica_groups=mesh['feat'=8,'tok'=32] {'feat'}, dimensions={0} | all-to-all | bytes 786432 | tf_op jit(solution)/shard_map/all_to_all | solution.py:323
  (75 shorter events, 18.8 us)
Async XLA Ops:
  0.6 277.4 %copy-start = (bf16[768,1536]{1,0:T(8,128)(2,1)S(1)}, bf16[768,1536]{1,0:T(8,128)(2,1)}, u32[]{:S(2)}) copy-start(bf16[768,1536]{1,0:T(8,128)(2,1)} %param.16) | copy-start | bytes 7077892
  2.9 5.1 %collective-permute-start = (bf16[2,5,24,384]{3,2,1,0:T(8,128)(2,1)S(1)}, bf16[2,5,24,384]{3,2,1,0:T(8,128)(2,1)S(1)}, u32[]{:S(2)}, u32[]{:S(2)}) collective-permute-start(bf16[2,5,24,384]{3,2,1,0:T(8,128)(2,1)S(1)} %get-tuple-element.41), channel_id=1, source_target_pairs={{0,1},{1,0},{2,3},{3,2},{4,5},{5,4},{6,7},{7,6},{8,9},{9,8},{10,11... | collective-permute-start | bytes 552968 | tf_op jit(solution)/shard_map/ppermute | solution.py:19
  6.2 6.2 %collective-permute-start.1 = (bf16[2,5,24,384]{3,2,1,0:T(8,128)(2,1)S(1)}, bf16[2,5,24,384]{3,2,1,0:T(8,128)(2,1)S(1)}, u32[]{:S(2)}, u32[]{:S(2)}) collective-permute-start(bf16[2,5,24,384]{3,2,1,0:T(8,128)(2,1)S(1)} %get-tuple-element.42), channel_id=1, source_target_pairs={{0,2},{1,3},{2,0},{3,1},{4,6},{5,7},{6,4},{7,5},{8,10},{9,11},{10,... | collective-permute-start | bytes 552968 | tf_op jit(solution)/shard_map/ppermute | solution.py:19
  6.2 10.3 %collective-permute-start.2 = (bf16[2,5,24,384]{3,2,1,0:T(8,128)(2,1)S(1)}, bf16[2,5,24,384]{3,2,1,0:T(8,128)(2,1)S(1)}, u32[]{:S(2)}, u32[]{:S(2)}) collective-permute-start(bf16[2,5,24,384]{3,2,1,0:T(8,128)(2,1)S(1)} %get-tuple-element.43), channel_id=1, source_target_pairs={{0,3},{1,2},{2,1},{3,0},{4,7},{5,6},{6,5},{7,4},{8,11},{9,10},{10,... | collective-permute-start | bytes 552968 | tf_op jit(solution)/shard_map/ppermute | solution.py:19
  16.6 172.7 %copy-start.2 = (bf16[2,5,4,24,384]{4,3,2,1,0:T(8,128)(2,1)}, bf16[2,5,4,24,384]{4,3,2,1,0:T(8,128)(2,1)S(1)}, u32[]{:S(2)}) copy-start(bf16[2,5,4,24,384]{4,3,2,1,0:T(8,128)(2,1)S(1)} %shard_map.105) | copy-start | bytes 2211844
  16.6 27.1 %collective-permute-start.5 = (bf16[256,1536]{1,0:T(8,128)(2,1)}, bf16[256,1536]{1,0:T(8,128)(2,1)}, u32[]{:S(2)}, u32[]{:S(2)}) collective-permute-start(bf16[256,1536]{1,0:T(8,128)(2,1)} %refs_0_), channel_id=1, source_target_pairs={{0,2},{1,3},{2,0},{3,1},{4,6},{5,7},{6,4},{7,5},{8,10},{9,11},{10,... | collective-permute-start | bytes 2359304 | tf_op jit(solution)/shard_map/ppermute | solution.py:19
  16.7 26.3 %collective-permute-start.4 = (bf16[2,5,96,384]{3,2,1,0:T(8,128)(2,1)S(1)}, bf16[2,5,96,384]{3,2,1,0:T(8,128)(2,1)}, u32[]{:S(2)}, u32[]{:S(2)}) collective-permute-start(bf16[2,5,96,384]{3,2,1,0:T(8,128)(2,1)S(1)} %bitcast.12), channel_id=1, source_target_pairs={{0,28},{1,29},{2,30},{3,31},{4,0},{5,1},{6,2},{7,3},{8,4},{9,5},{1... | collective-permute-start | bytes 2211848 | tf_op jit(solution)/shard_map/ppermute | solution.py:24
  21.7 21.3 %collective-permute-start.3 = (bf16[2,5,96,384]{3,2,1,0:T(8,128)(2,1)S(1)}, bf16[2,5,96,384]{3,2,1,0:T(8,128)(2,1)}, u32[]{:S(2)}, u32[]{:S(2)}) collective-permute-start(bf16[2,5,96,384]{3,2,1,0:T(8,128)(2,1)S(1)} %bitcast.13), channel_id=1, source_target_pairs={{0,4},{1,5},{2,6},{3,7},{4,8},{5,9},{6,10},{7,11},{8,12},{9,13},{1... | collective-permute-start | bytes 2211848 | tf_op jit(solution)/shard_map/ppermute | solution.py:24
  22.8 11.5 %collective-permute-start.7 = (bf16[256,768]{1,0:T(8,128)(2,1)S(1)}, bf16[256,768]{1,0:T(8,128)(2,1)S(1)}, u32[]{:S(2)}, u32[]{:S(2)}) collective-permute-start(bf16[256,768]{1,0:T(8,128)(2,1)S(1)} %constant_dynamic-slice_fusion.1), channel_id=1, source_target_pairs={{0,128},{32,160},{64,192},{96,224},{128,0},{160,32},{192,64},{224,... | collective-permute-start | bytes 1179656 | tf_op jit(solution)/shard_map/ppermute | solution.py:19
  25.8 17.2 %collective-permute-start.6 = (bf16[256,768]{1,0:T(8,128)(2,1)S(1)}, bf16[256,768]{1,0:T(8,128)(2,1)S(1)}, u32[]{:S(2)}, u32[]{:S(2)}) collective-permute-start(bf16[256,768]{1,0:T(8,128)(2,1)S(1)} %constant_dynamic-slice_fusion.1), channel_id=1, source_target_pairs={{0,64},{32,96},{64,0},{96,32},{128,192},{160,224},{192,128},{224,1... | collective-permute-start | bytes 1179656 | tf_op jit(solution)/shard_map/ppermute | solution.py:19
  44.9 24.2 %collective-permute-start.10 = (bf16[512,768]{1,0:T(8,128)(2,1)S(1)}, bf16[512,768]{1,0:T(8,128)(2,1)}, u32[]{:S(2)}, u32[]{:S(2)}) collective-permute-start(bf16[512,768]{1,0:T(8,128)(2,1)S(1)} %pad_maximum_fusion), channel_id=1, source_target_pairs={{0,32},{32,0},{64,96},{96,64},{128,160},{160,128},{192,224},{224,1... | collective-permute-start | bytes 2359304 | tf_op jit(solution)/shard_map/ppermute | solution.py:19
  47.4 19.1 %collective-permute-start.8 = (bf16[2,5,96,384]{3,2,1,0:T(8,128)(2,1)}, bf16[2,5,96,384]{3,2,1,0:T(8,128)(2,1)S(1)}, u32[]{:S(2)}, u32[]{:S(2)}) collective-permute-start(bf16[2,5,96,384]{3,2,1,0:T(8,128)(2,1)} %collective-permute-done.3.refs_1_), channel_id=1, source_target_pairs={{0,4},{1,5},{2,6},{3,7},{4,8},{5,9},{6,10},{7,11},{8,12},{9,13},{1... | collective-permute-start | bytes 2211848 | tf_op jit(solution)/shard_map/ppermute | solution.py:24
  47.4 19.9 %collective-permute-start.9 = (bf16[2,5,96,384]{3,2,1,0:T(8,128)(2,1)}, bf16[2,5,96,384]{3,2,1,0:T(8,128)(2,1)S(1)}, u32[]{:S(2)}, u32[]{:S(2)}) collective-permute-start(bf16[2,5,96,384]{3,2,1,0:T(8,128)(2,1)} %collective-permute-done.4.refs_2_), channel_id=1, source_target_pairs={{0,28},{1,29},{2,30},{3,31},{4,0},{5,1},{6,2},{7,3},{8,4},{9,5},{1... | collective-permute-start | bytes 2211848 | tf_op jit(solution)/shard_map/ppermute | solution.py:24
  50.1 9.7 %collective-permute-start.12 = (bf16[256,768]{1,0:T(8,128)(2,1)S(1)}, bf16[256,768]{1,0:T(8,128)(2,1)S(1)}, u32[]{:S(2)}, u32[]{:S(2)}) collective-permute-start(bf16[256,768]{1,0:T(8,128)(2,1)S(1)} %constant_dynamic-slice_fusion), channel_id=1, source_target_pairs={{0,128},{32,160},{64,192},{96,224},{128,0},{160,32},{192,64},{224,... | collective-permute-start | bytes 1179656 | tf_op jit(solution)/shard_map/ppermute | solution.py:19
  51.7 14.9 %collective-permute-start.11 = (bf16[256,768]{1,0:T(8,128)(2,1)S(1)}, bf16[256,768]{1,0:T(8,128)(2,1)S(1)}, u32[]{:S(2)}, u32[]{:S(2)}) collective-permute-start(bf16[256,768]{1,0:T(8,128)(2,1)S(1)} %constant_dynamic-slice_fusion), channel_id=1, source_target_pairs={{0,64},{32,96},{64,0},{96,32},{128,192},{160,224},{192,128},{224,1... | collective-permute-start | bytes 1179656 | tf_op jit(solution)/shard_map/ppermute | solution.py:19
  189.3 22.4 %collective-permute-start.16 = (bf16[3,512,768]{2,1,0:T(8,128)(2,1)}, bf16[3,512,768]{2,1,0:T(8,128)(2,1)}, u32[]{:S(2)}, u32[]{:S(2)}) collective-permute-start(bf16[3,512,768]{2,1,0:T(8,128)(2,1)} %get-tuple-element.70.refs_9_.refs_5_), channel_id=1, source_target_pairs={{0,1},{1,0},{2,3},{3,2},{4,5},{5,4},{6,7},{7,6},{8,9},{9,8},{10,11... | collective-permute-start | bytes 7077896 | tf_op jit(solution)/shard_map/ppermute | solution.py:19
  192.6 19.2 %collective-permute-start.15 = (bf16[512,1536]{1,0:T(8,128)(2,1)}, bf16[512,1536]{1,0:T(8,128)(2,1)}, u32[]{:S(2)}, u32[]{:S(2)}) collective-permute-start(bf16[512,1536]{1,0:T(8,128)(2,1)} %get-tuple-element.68.refs_7_.refs_3_), channel_id=1, source_target_pairs={{0,1},{1,0},{2,3},{3,2},{4,5},{5,4},{6,7},{7,6},{8,9},{9,8},{10,11... | collective-permute-start | bytes 4718600 | tf_op jit(solution)/shard_map/ppermute | solution.py:19
  192.7 19.1 %collective-permute-start.13 = (bf16[2,5,96,384]{3,2,1,0:T(8,128)(2,1)}, bf16[2,5,96,384]{3,2,1,0:T(8,128)(2,1)S(1)}, u32[]{:S(2)}, u32[]{:S(2)}) collective-permute-start(bf16[2,5,96,384]{3,2,1,0:T(8,128)(2,1)} %copy-done.14), channel_id=1, source_target_pairs={{0,4},{1,5},{2,6},{3,7},{4,8},{5,9},{6,10},{7,11},{8,12},{9,13},{1... | collective-permute-start | bytes 2211848 | tf_op jit(solution)/shard_map/ppermute | solution.py:24
  192.7 19.1 %collective-permute-start.14 = (bf16[2,5,96,384]{3,2,1,0:T(8,128)(2,1)}, bf16[2,5,96,384]{3,2,1,0:T(8,128)(2,1)}, u32[]{:S(2)}, u32[]{:S(2)}) collective-permute-start(bf16[2,5,96,384]{3,2,1,0:T(8,128)(2,1)} %copy-done.15), channel_id=1, source_target_pairs={{0,28},{1,29},{2,30},{3,31},{4,0},{5,1},{6,2},{7,3},{8,4},{9,5},{1... | collective-permute-start | bytes 2211848 | tf_op jit(solution)/shard_map/ppermute | solution.py:24
  213.0 17.3 %collective-permute-start.17 = (bf16[1,5,96,384]{3,2,1,0:T(8,128)(2,1)S(1)}, bf16[1,5,96,384]{3,2,1,0:T(8,128)(2,1)}, u32[]{:S(2)}, u32[]{:S(2)}) collective-permute-start(bf16[1,5,96,384]{3,2,1,0:T(8,128)(2,1)S(1)} %get-tuple-element.66), channel_id=1, source_target_pairs={{0,4},{1,5},{2,6},{3,7},{4,8},{5,9},{6,10},{7,11},{8,12},{9,13},{1... | collective-permute-start | bytes 1105928 | tf_op jit(solution)/shard_map/ppermute | solution.py:24
  213.1 17.3 %collective-permute-start.18 = (bf16[1,5,96,384]{3,2,1,0:T(8,128)(2,1)S(1)}, bf16[1,5,96,384]{3,2,1,0:T(8,128)(2,1)}, u32[]{:S(2)}, u32[]{:S(2)}) collective-permute-start(bf16[1,5,96,384]{3,2,1,0:T(8,128)(2,1)S(1)} %get-tuple-element.67), channel_id=1, source_target_pairs={{0,28},{1,29},{2,30},{3,31},{4,0},{5,1},{6,2},{7,3},{8,4},{9,5},{1... | collective-permute-start | bytes 1105928 | tf_op jit(solution)/shard_map/ppermute | solution.py:24
  236.3 9.5 %collective-permute-start.20 = (bf16[256,384]{1,0:T(8,128)(2,1)}, bf16[256,384]{1,0:T(8,128)(2,1)S(1)}, u32[]{:S(2)}, u32[]{:S(2)}) collective-permute-start(bf16[256,384]{1,0:T(8,128)(2,1)} %get-tuple-element.74), channel_id=1, source_target_pairs={{0,2},{1,3},{2,0},{3,1},{4,6},{5,7},{6,4},{7,5},{8,10},{9,11},{10,... | collective-permute-start | bytes 589832 | tf_op jit(solution)/shard_map/ppermute | solution.py:19
  236.4 11.0 %collective-permute-start.21 = (bf16[256,384]{1,0:T(8,128)(2,1)}, bf16[256,384]{1,0:T(8,128)(2,1)S(1)}, u32[]{:S(2)}, u32[]{:S(2)}) collective-permute-start(bf16[256,384]{1,0:T(8,128)(2,1)} %get-tuple-element.75), channel_id=1, source_target_pairs={{0,3},{1,2},{2,1},{3,0},{4,7},{5,6},{6,5},{7,4},{8,11},{9,10},{10,... | collective-permute-start | bytes 589832 | tf_op jit(solution)/shard_map/ppermute | solution.py:19
  245.7 1.7 collective-permute-start.19
  (15 other events, 657.9 us)

commit v2 on v0

v2 whole, which is shorter than its diff:
```python
import functools
import jax
import jax.numpy as jnp
from jax import lax
from jax.experimental import pallas as pl
from jax.experimental.pallas import tpu as pltpu
from jax.sharding import PartitionSpec as P

GROUP = 4
SMEM = pl.BlockSpec(memory_space=pltpu.SMEM)
VMEM = pl.BlockSpec(memory_space=pltpu.VMEM)
VMEM_BYTES = 30 * 2**20
SMALL_BYTES = 16 * 2**20


def swapped(value, axis, mask):
    return lax.ppermute(value, axis, [(i, i ^ mask) for i in range(lax.axis_size(axis))])


def shifted(value, step):
    count = lax.axis_size("tok")
    return lax.ppermute(value, "tok", [(i, (i + step * GROUP) % count) for i in range(count)])


def pack_kernel(own_ref, gate_ref, up_ref, *out_refs):
    half = gate_ref.shape[3] // 2
    for m in range(4):
        to = own_ref[0] ^ m
        at = pl.ds(pl.multiple_of(to % 2 * half, 128), half)
        for side, ref in enumerate((gate_ref, up_ref)):
            out_refs[m][side] = ref[to // 2, :, :, at]


def place_kernel(own_ref, *refs):
    for m in range(4):
        refs[4][:, :, own_ref[0] ^ m] = refs[m][...]


def halves_kernel(f_ref, b_ref, f_out, b_out):
    f_out[...] = f_ref[...]
    b_out[...] = b_ref[...]


def block_of_rows(own_refs, partner_refs, j, x_lo, rows, start, width):
    blk = partner_refs[0].shape[2]
    if j < 2:
        column = pl.ds(pl.multiple_of((x_lo ^ j) * blk + start, 128), width)
        return jnp.concatenate([ref[rows, column] for ref in own_refs])
    column = pl.ds(pl.multiple_of(start, 128), width)
    return jnp.concatenate([ref[j - 2, rows, column] for ref in partner_refs])


def last_window(z, z_count, share, blk, window):
    row = (z + z_count // 2) % z_count * share
    return row, jnp.minimum(row // 128 * 128, blk - window)


def early_kernel(place_ref, gs_ref, us_ref, *refs, z_count, window):
    n_w = z_count - 1
    w_refs, own_refs, partner_refs = refs[:n_w], refs[n_w : n_w + 2], refs[n_w + 2 : n_w + 4]
    acc, windows, w_mem = refs[n_w + 4 :]
    x_lo, z = place_ref[5], place_ref[6]
    blk, both = w_mem.shape[1:]
    share, width = blk // z_count, both // 2
    row, start = last_window(z, z_count, share, blk, window)
    last = pl.ds(pl.multiple_of(row, 16), share)
    for j in range(5):
        slot = place_ref[j]
        w_mem[j % 2, last] = jnp.zeros((share, both), w_mem.dtype)
        for i, ref in enumerate(w_refs):
            origin = z - (i + 1) // 2 if i % 2 else z + i // 2
            at = pl.ds(pl.multiple_of((origin + z_count) % z_count * share, 16), share)
            for side in range(2):
                w_mem[j % 2, at, side * width : (side + 1) * width] = ref[side, slot]
        windows[j] = block_of_rows(own_refs, partner_refs, j, x_lo, slice(None), start, window)
        x = block_of_rows(own_refs, partner_refs, j, x_lo, slice(None), 0, blk)
        term = jnp.dot(x, w_mem[j % 2], preferred_element_type=jnp.float32)
        g, u = term[:, :width] * gs_ref[slot], term[:, width:] * us_ref[slot]
        if j == 0:
            acc[:, :width] = g
            acc[:, width:] = u
        else:
            acc[:, :width] += g
            acc[:, width:] += u


def early(place, gs, us, weights, own_rows, partner_rows):
    blk = own_rows[0].shape[1] // 2
    rows = 2 * own_rows[0].shape[0]
    _, slots, share, width = weights[0].shape
    window = min(2 * 128 * ((share + 127) // 128), blk)
    return pl.pallas_call(
        functools.partial(early_kernel, z_count=blk // share, window=window),
        out_shape=[
            jax.ShapeDtypeStruct((rows, 2 * width), jnp.float32),
            jax.ShapeDtypeStruct((slots, rows, window), jnp.bfloat16),
        ],
        in_specs=[SMEM] * 3 + [VMEM] * (len(weights) + 4),
        out_specs=[VMEM] * 2,
        scratch_shapes=[pltpu.VMEM((2, blk, 2 * width), jnp.bfloat16)],
        compiler_params=pltpu.CompilerParams(vmem_limit_bytes=VMEM_BYTES),
        cost_estimate=pl.CostEstimate(flops=2**20, bytes_accessed=2**20, transcendentals=0),
    )(place, gs, us, *weights, *own_rows, *partner_rows)


def late_kernel(place_ref, gs_ref, us_ref, *refs, z_count, first):
    w_refs, acc_ref, window_ref, out_refs = refs[:2], refs[2], refs[3], refs[4:6]
    w_mem, acc = refs[6:]
    z = place_ref[6]
    share, width = w_refs[0].shape[2:]
    slots, rows, window = window_ref.shape
    rows //= 4
    row, start = last_window(z, z_count, share, z_count * share, window)
    at = pl.ds(pl.multiple_of(row - start, 16), share)
    w_mem[...] = jnp.zeros_like(w_mem)
    mine = [pl.ds((2 * core + first) * rows, rows) for core in range(2)]
    for core in range(2):
        acc[pl.ds(core * rows, rows)] = acc_ref[mine[core]]
    for j in range(slots):
        slot = place_ref[j]
        for side in range(2):
            w_mem[j, at, side * width : (side + 1) * width] = w_refs[side][0, slot]
        x = jnp.concatenate([window_ref[j, at_core] for at_core in mine])
        term = jnp.dot(x, w_mem[j], preferred_element_type=jnp.float32)
        acc[:, :width] += term[:, :width] * gs_ref[slot]
        acc[:, width:] += term[:, width:] * us_ref[slot]
    g = acc[:, :width]
    out = (g / (1.0 + jnp.exp(-g)) * acc[:, width:]).astype(jnp.bfloat16)
    out_refs[0][...] = out[:rows]
    out_refs[1][...] = out[rows:]


def late(place, gs, us, weights, acc, windows, z_count, first):
    slots, rows, window = windows.shape
    rows //= 4
    width = weights[0].shape[3]
    return pl.pallas_call(
        functools.partial(late_kernel, z_count=z_count, first=first),
        out_shape=[jax.ShapeDtypeStruct((rows, width), jnp.bfloat16)] * 2,
        in_specs=[SMEM] * 3 + [VMEM] * 4,
        out_specs=[VMEM] * 2,
        scratch_shapes=[
            pltpu.VMEM((slots, window, 2 * width), jnp.bfloat16),
            pltpu.VMEM((2 * rows, 2 * width), jnp.float32),
        ],
        compiler_params=pltpu.CompilerParams(vmem_limit_bytes=SMALL_BYTES),
        cost_estimate=pl.CostEstimate(
            flops=2 * 2 * 2 * rows * slots * window * width, bytes_accessed=4 * 2**20, transcendentals=2 * rows * width
        ),
    )(place, gs, us, *weights, acc, windows)


def latent_kernel(own_ref, lin_ref, *refs):
    pieces, hidden_ref, part_ref = refs[:4], refs[4], refs[5]
    width = pieces[0].shape[1]
    total = None
    for m in range(4):
        at = pl.ds(pl.multiple_of((own_ref[0] ^ m) * width, width), width)
        piece = pieces[m][...]
        hidden_ref[:, at] = piece
        term = jnp.dot(piece, lin_ref[at], preferred_element_type=jnp.float32)
        total = term if total is None else total + term
    part_ref[...] = total.astype(jnp.bfloat16)


def per_device(tokens, gate_weight, up_weight, gate_scale, up_scale, partners, latent_in, latent_out):
    rows, features = tokens.shape
    blocks, slots, share, blk = gate_weight.shape
    feat_count = lax.axis_size("feat")
    half = blk // 2
    feat, tok = lax.axis_index("feat"), lax.axis_index("tok")
    member, z = tok % GROUP, tok // GROUP
    x_lo, core = member // 2, member % 2
    block_id = feat * blocks + x_lo

    own = member[None].astype(jnp.int32)
    packed = pl.pallas_call(
        pack_kernel,
        out_shape=[jax.ShapeDtypeStruct((2, slots, share, half), jnp.bfloat16)] * 4,
        in_specs=[SMEM, VMEM, VMEM],
        out_specs=[VMEM] * 4,
        compiler_params=pltpu.CompilerParams(vmem_limit_bytes=SMALL_BYTES),
    )(own, gate_weight, up_weight)

    def place(got):
        shape = got[0].shape
        out = pl.pallas_call(
            place_kernel,
            out_shape=jax.ShapeDtypeStruct(shape[:2] + (4,) + shape[2:], jnp.bfloat16),
            in_specs=[SMEM] + [VMEM] * 4,
            out_specs=VMEM,
            compiler_params=pltpu.CompilerParams(vmem_limit_bytes=SMALL_BYTES),
        )(own, *got)
        return out.reshape(shape[:2] + (4 * shape[2],) + shape[3:])

    def block_of(value):
        return lax.dynamic_slice(value, (0, x_lo * blk), (rows, blk))

    def step(forward, back):
        return shifted(forward, 1), shifted(back, -1)

    far = [swapped(packed[m], "tok", m) for m in (2, 3)]
    near = swapped(packed[1], "tok", 1)
    w0 = place([packed[0], near, *far])
    barrier = lax.optimization_barrier
    first = block_of(tokens)
    p0_y1, p0_y2 = swapped(first, "feat", 2), swapped(first, "feat", 4)
    w0, later = barrier((w0, tokens))
    w1 = step(w0, w0)
    s2 = swapped(later, "tok", 2)
    w1, s2, first, later = barrier((w1, s2, first, later))
    w2 = step(*w1)
    second = block_of(s2)
    p_x = swapped(jnp.concatenate([first, second]), "feat", 1)
    second, p0_y1, p0_y2 = barrier((second, p0_y1, p0_y2))
    p2_y1, p2_y2 = swapped(second, "feat", 2), swapped(second, "feat", 4)
    w2, p_x, p2_y1, p2_y2, p0_y1, p0_y2, s2, later = barrier((w2, p_x, p2_y1, p2_y2, p0_y1, p0_y2, s2, later))
    w3 = step(*w2)
    own0 = jnp.concatenate([later, s2])
    partner0 = jnp.stack([p_x, jnp.concatenate([p0_y1, p2_y1]), jnp.concatenate([p0_y2, p2_y2])])
    own1, partner1 = swapped(own0, "tok", 1), swapped(partner0, "tok", 1)
    w3, own0, own1, partner0, partner1 = barrier((w3, own0, own1, partner0, partner1))
    half_shape = (1,) + w3[0].shape[1:]
    cut = pl.pallas_call(
        halves_kernel,
        grid=(1,),
        out_shape=[jax.ShapeDtypeStruct(half_shape, jnp.bfloat16)] * 2,
        in_specs=[pl.BlockSpec(half_shape, lambda i: (0, 0, 0, 0)), pl.BlockSpec(half_shape, lambda i: (1, 0, 0, 0))],
        out_specs=[pl.BlockSpec(half_shape, lambda i: (0, 0, 0, 0))] * 2,
        compiler_params=pltpu.CompilerParams(vmem_limit_bytes=SMALL_BYTES),
    )(*w3)
    w4 = step(*cut)

    wanted = lax.dynamic_index_in_dim(partners, block_id, 0, keepdims=False)
    labels = block_id ^ jnp.array([0, 1, 2, 4, 8], jnp.int32)
    order = jnp.sum(jnp.where(labels[:, None] == wanted[None, :], jnp.arange(5, dtype=jnp.int32)[None, :], 0), axis=1)
    here = jnp.concatenate([order, jnp.stack([x_lo, z]).astype(jnp.int32)])
    gs = lax.dynamic_index_in_dim(gate_scale, x_lo, 0, keepdims=False)
    us = lax.dynamic_index_in_dim(up_scale, x_lo, 0, keepdims=False)

    acc, windows = early(here, gs, us, (w0, *w1, *w2, *w3), (own0, own1), (partner0, partner1))
    z_count = lax.axis_size("tok") // GROUP
    made = late(here, gs, us, w4, acc, windows, z_count, 1)
    far_hidden = [swapped(v, "tok", mask) for v, mask in zip(made, (2, 3))]
    made = late(here, gs, us, w4, acc, windows, z_count, 0)
    hidden_pieces = [made[0], swapped(made[1], "tok", 1), *far_hidden]
    hidden, part = pl.pallas_call(
        latent_kernel,
        out_shape=(
            jax.ShapeDtypeStruct((rows, features), jnp.bfloat16),
            jax.ShapeDtypeStruct((rows, latent_in.shape[1]), jnp.bfloat16),
        ),
        in_specs=[SMEM] + [VMEM] * 5,
        out_specs=(VMEM, VMEM),
        compiler_params=pltpu.CompilerParams(vmem_limit_bytes=SMALL_BYTES),
        cost_estimate=pl.CostEstimate(flops=2 * rows * features * latent_in.shape[1], bytes_accessed=4 * 2**20, transcendentals=0),
    )(own, latent_in, *hidden_pieces)

    parts = part.reshape(feat_count, rows // feat_count, -1)
    terms = lax.all_to_all(parts, "feat", 0, 0)
    mine = jnp.sum(terms.astype(jnp.float32), axis=0).astype(jnp.bfloat16)
    latent = lax.all_to_all(jnp.broadcast_to(mine[None], parts.shape), "feat", 0, 0).reshape(rows, -1)
    rank_term = jnp.dot(latent, latent_out, preferred_element_type=jnp.float32).astype(jnp.bfloat16)
    return hidden, rank_term


def solution(mesh):
    placed = (
        P("tok", "feat"),
        P("feat", None, "tok", None),
        P("feat", None, "tok", None),
        P("feat", None),
        P("feat", None),
        P(),
        P("feat", None),
        P(None, "feat"),
    )
    return jax.shard_map(
        per_device,
        mesh=mesh,
        in_specs=placed,
        out_specs=(P("tok", "feat"), P("tok", "feat")),
        check_vma=False,
    )
```

time: 170 us -> 153 us (0.900)
  starting transfers between devices: 42.3 us -> 34.6 us
  local copies, waits for them, and re-layouts: 15.3 us -> 8.61 us
  Pallas kernels: 22.8 us -> 20.1 us
  waiting for transfers between devices: 61.1 us -> 58.9 us
    ppermute x21 -> x14, waiting for transfers between devices: 45.6 us -> 28.3 us  [swapped(): lax.ppermute(value, axis, [(i, i ^ mask) for i in range(lax.axis_size(axi...]
    ppermute x8, waiting for transfers between devices: 15.5 us -> 30.5 us  [shifted(): lax.ppermute(value, 'tok', [(i, (i + step * GROUP) % count) for i in rang...]
    unnamed x36 -> x17, local copies, waits for them, and re-layouts: 8.63 us -> 4.22 us
    ppermute x21 -> x14, starting transfers between devices: 25.9 us -> 21.5 us  [swapped(): lax.ppermute(value, axis, [(i, i ^ mask) for i in range(lax.axis_size(axi...]
    slice x2 -> x0, local copies, waits for them, and re-layouts: 3.58 us -> none  [per_device(): w4 = step(w3[0][:1], w3[1][1:])]
    ppermute x8, starting transfers between devices: 16.4 us -> 13.1 us  [shifted(): lax.ppermute(value, 'tok', [(i, (i + step * GROUP) % count) for i in rang...]
    pallas_call x1, Pallas kernels: 2.2 us -> 0.07 us  [per_device(): pl.pallas_call(pack_kernel, out_shape=[jax.ShapeDtypeStruct((2, slots, sh...]
    concatenate x0 -> x1, local copies, waits for them, and re-layouts: none -> 2.13 us  [per_device(): own0 = jnp.concatenate([later, s2])]
  transfers between devices with their start and end apart: 29 -> 22, of which waited for: 12 -> 8; matrix products, arithmetic and copies ran while one was open for 3% -> 4% of each run, Pallas kernels for 11% -> 9%
where the time goes in v2:
time: 153 us; the launch traced here: 152 us
  waiting for transfers between devices  58.9 us (38%)
  starting transfers between devices  34.6 us (23%)
  blocking collectives  25.5 us (17%)
  Pallas kernels  20.1 us (13%)
  local copies, waits for them, and re-layouts  8.61 us (6%)
  other arithmetic  2.16 us (1%)
  matrix products  1.66 us (1%)
    ppermute x8, waiting for transfers between devices, shifted(): lax.ppermute(value, 'tok', [(i, (i + step * GROUP) % count) for i in rang...  30.5 us
    ppermute x14, waiting for transfers between devices, swapped(): lax.ppermute(value, axis, [(i, i ^ mask) for i in range(lax.axis_size(axi...  28.3 us
    ppermute x14, starting transfers between devices, swapped(): lax.ppermute(value, axis, [(i, i ^ mask) for i in range(lax.axis_size(axi...  21.5 us
    all_to_all x1, blocking collectives, per_device(): terms = lax.all_to_all(parts, 'feat', 0, 0)  13.7 us
    ppermute x8, starting transfers between devices, shifted(): lax.ppermute(value, 'tok', [(i, (i + step * GROUP) % count) for i in rang...  13.1 us
    all_to_all x1, blocking collectives, per_device(): lax.all_to_all(jnp.broadcast_to(mine[None], parts.shape), 'feat', 0, 0)  11.8 us
    pallas_call x1, Pallas kernels, early(): pl.pallas_call(functools.partial(early_kernel, z_count=blk // share, wind...  11.3 us
    pallas_call x2, Pallas kernels, late(): pl.pallas_call(functools.partial(late_kernel, z_count=z_count, first=firs...  5.09 us
  transfers between devices with their start and end apart: 22, of which 8 were waited for; matrix products, arithmetic and copies ran while one was open for 4% of the time, Pallas kernels for 9%

profile of v2, /device:TPU:1, one launch (start us, length us, event | category | flops | bytes accessed | tf_op | source)
XLA Modules:
  0.0 152.3 jit_solution(575455375536363086)
XLA Ops:
  2.9 3.3 %collective-permute-start = (bf16[2,5,24,384]{3,2,1,0:T(8,128)(2,1)S(1)}, bf16[2,5,24,384]{3,2,1,0:T(8,128)(2,1)S(1)}, u32[]{:S(2)}, u32[]{:S(2)}) collective-permute-start(bf16[2,5,24,384]{3,2,1,0:T(8,128)(2,1)S(1)} %get-tuple-element.42), channel_id=1, source_target_pairs={{0,1},{1,0},{2,3},{3,2},{4,5},{5,4},{6,7},{7,6},{8,9},{9,8},{10,11... | collective-permute-start | bytes 552968 | tf_op jit(solution)/shard_map/ppermute | solution.py:17
  7.9 4.5 %collective-permute-done.1.refs_2_ = bf16[2,5,24,384]{3,2,1,0:T(8,128)(2,1)S(1)} collective-permute-done((bf16[2,5,24,384]{3,2,1,0:T(8,128)(2,1)S(1)}, bf16[2,5,24,384]{3,2,1,0:T(8,128)(2,1)S(1)}, u32[]{:S(2)}, u32[]{:S(2)}) %collective-permute-start.1) | collective-permute-done | bytes 184352 | tf_op jit(solution)/shard_map/ppermute | solution.py:17
  12.4 4.1 %collective-permute-done.2.refs_3_ = bf16[2,5,24,384]{3,2,1,0:T(8,128)(2,1)S(1)} collective-permute-done((bf16[2,5,24,384]{3,2,1,0:T(8,128)(2,1)S(1)}, bf16[2,5,24,384]{3,2,1,0:T(8,128)(2,1)S(1)}, u32[]{:S(2)}, u32[]{:S(2)}) %collective-permute-start.2) | collective-permute-done | bytes 184352 | tf_op jit(solution)/shard_map/ppermute | solution.py:17
  16.7 5.0 %collective-permute-start.4 = (bf16[2,5,96,384]{3,2,1,0:T(8,128)(2,1)S(1)}, bf16[2,5,96,384]{3,2,1,0:T(8,128)(2,1)}, u32[]{:S(2)}, u32[]{:S(2)}) collective-permute-start(bf16[2,5,96,384]{3,2,1,0:T(8,128)(2,1)S(1)} %bitcast.17), channel_id=1, source_target_pairs={{0,28},{1,29},{2,30},{3,31},{4,0},{5,1},{6,2},{7,3},{8,4},{9,5},{1... | collective-permute-start | bytes 2211848 | tf_op jit(solution)/shard_map/ppermute | solution.py:22
  22.8 3.0 %collective-permute-start.10 = (bf16[256,768]{1,0:T(8,128)(2,1)S(1)}, bf16[256,768]{1,0:T(8,128)(2,1)S(1)}, u32[]{:S(2)}, u32[]{:S(2)}) collective-permute-start(bf16[256,768]{1,0:T(8,128)(2,1)S(1)} %constant_dynamic-slice_fusion.1), channel_id=1, source_target_pairs={{0,128},{32,160},{64,192},{96,224},{128,0},{160,32},{192,64},{224,... | collective-permute-start | bytes 1179656 | tf_op jit(solution)/shard_map/ppermute | solution.py:17
  26.2 10.9 %collective-permute-done.4.refs_2_ = bf16[2,5,96,384]{3,2,1,0:T(8,128)(2,1)} collective-permute-done((bf16[2,5,96,384]{3,2,1,0:T(8,128)(2,1)S(1)}, bf16[2,5,96,384]{3,2,1,0:T(8,128)(2,1)}, u32[]{:S(2)}, u32[]{:S(2)}) %collective-permute-start.4) | collective-permute-done | bytes 737312 | tf_op jit(solution)/shard_map/ppermute | solution.py:22
  37.1 3.2 %collective-permute-done.3.refs_1_ = bf16[2,5,96,384]{3,2,1,0:T(8,128)(2,1)} collective-permute-done((bf16[2,5,96,384]{3,2,1,0:T(8,128)(2,1)S(1)}, bf16[2,5,96,384]{3,2,1,0:T(8,128)(2,1)}, u32[]{:S(2)}, u32[]{:S(2)}) %collective-permute-start.3) | collective-permute-done | bytes 737312 | tf_op jit(solution)/shard_map/ppermute | solution.py:22
  41.4 2.5 %collective-permute-start.8 = (bf16[512,768]{1,0:T(8,128)(2,1)S(1)}, bf16[512,768]{1,0:T(8,128)(2,1)S(1)}, u32[]{:S(2)}, u32[]{:S(2)}) collective-permute-start(bf16[512,768]{1,0:T(8,128)(2,1)S(1)} %pad_maximum_fusion.1), channel_id=1, source_target_pairs={{0,32},{32,0},{64,96},{96,64},{128,160},{160,128},{192,224},{224,1... | collective-permute-start | bytes 2359304 | tf_op jit(solution)/shard_map/ppermute | solution.py:17
  43.9 2.7 %collective-permute-start.7 = (bf16[2,5,96,384]{3,2,1,0:T(8,128)(2,1)}, bf16[2,5,96,384]{3,2,1,0:T(8,128)(2,1)}, u32[]{:S(2)}, u32[]{:S(2)}) collective-permute-start(bf16[2,5,96,384]{3,2,1,0:T(8,128)(2,1)} %collective-permute-done.4.refs_2_), channel_id=1, source_target_pairs={{0,28},{1,29},{2,30},{3,31},{4,0},{5,1},{6,2},{7,3},{8,4},{9,5},{1... | collective-permute-start | bytes 2211848 | tf_op jit(solution)/shard_map/ppermute | solution.py:22
  46.6 2.9 %collective-permute-start.12 = (bf16[256,768]{1,0:T(8,128)(2,1)S(1)}, bf16[256,768]{1,0:T(8,128)(2,1)S(1)}, u32[]{:S(2)}, u32[]{:S(2)}) collective-permute-start(bf16[256,768]{1,0:T(8,128)(2,1)S(1)} %constant_dynamic-slice_fusion), channel_id=1, source_target_pairs={{0,128},{32,160},{64,192},{96,224},{128,0},{160,32},{192,64},{224,... | collective-permute-start | bytes 1179656 | tf_op jit(solution)/shard_map/ppermute | solution.py:17
  49.9 6.3 %collective-permute-done.12 = bf16[256,768]{1,0:T(8,128)(2,1)S(1)} collective-permute-done((bf16[256,768]{1,0:T(8,128)(2,1)S(1)}, bf16[256,768]{1,0:T(8,128)(2,1)S(1)}, u32[]{:S(2)}, u32[]{:S(2)}) %collective-permute-start.12) | collective-permute-done | bytes 393248 | tf_op jit(solution)/shard_map/ppermute | solution.py:17
  56.2 8.8 %collective-permute-done.11 = bf16[256,768]{1,0:T(8,128)(2,1)S(1)} collective-permute-done((bf16[256,768]{1,0:T(8,128)(2,1)S(1)}, bf16[256,768]{1,0:T(8,128)(2,1)S(1)}, u32[]{:S(2)}, u32[]{:S(2)}) %collective-permute-start.11) | collective-permute-done | bytes 393248 | tf_op jit(solution)/shard_map/ppermute | solution.py:17
  66.8 3.4 %collective-permute-start.16 = (bf16[3,512,768]{2,1,0:T(8,128)(2,1)}, bf16[3,512,768]{2,1,0:T(8,128)(2,1)}, u32[]{:S(2)}, u32[]{:S(2)}) collective-permute-start(bf16[3,512,768]{2,1,0:T(8,128)(2,1)} %pad_maximum_fusion.refs_9_), channel_id=1, source_target_pairs={{0,1},{1,0},{2,3},{3,2},{4,5},{5,4},{6,7},{7,6},{8,9},{9,8},{10,11... | collective-permute-start | bytes 7077896 | tf_op jit(solution)/shard_map/ppermute | solution.py:17
  72.3 2.1 %constant_dynamic-update-slice_fusion.refs_7_ = bf16[512,1536]{1,0:T(8,128)(2,1)} fusion(bf16[512,1536]{1,0:T(8,128)(2,1)} %constant_dynamic-update-slice_fusion.1, bf16[256,1536]{1,0:T(8,128)(2,1)} %collective-permute-done.5), kind=kLoop, calls=%fused_computation.5 | loop fusion | bytes 1572864 | tf_op jit(solution)/shard_map/concatenate | solution.py:219
  74.4 2.7 %collective-permute-start.14 = (bf16[2,5,96,384]{3,2,1,0:T(8,128)(2,1)}, bf16[2,5,96,384]{3,2,1,0:T(8,128)(2,1)}, u32[]{:S(2)}, u32[]{:S(2)}) collective-permute-start(bf16[2,5,96,384]{3,2,1,0:T(8,128)(2,1)} %collective-permute-done.7.refs_4_), channel_id=1, source_target_pairs={{0,28},{1,29},{2,30},{3,31},{4,0},{5,1},{6,2},{7,3},{8,4},{9,5},{1... | collective-permute-start | bytes 2211848 | tf_op jit(solution)/shard_map/ppermute | solution.py:22
  77.1 16.4 %collective-permute-done.13.f_ref.refs_5_ = bf16[2,5,96,384]{3,2,1,0:T(8,128)(2,1)} collective-permute-done((bf16[2,5,96,384]{3,2,1,0:T(8,128)(2,1)}, bf16[2,5,96,384]{3,2,1,0:T(8,128)(2,1)}, u32[]{:S(2)}, u32[]{:S(2)}) %collective-permute-start.13) | collective-permute-done | bytes 737312 | tf_op jit(solution)/shard_map/ppermute | solution.py:22
  95.5 2.7 %collective-permute-start.18 = (bf16[1,5,96,384]{3,2,1,0:T(8,128)(2,1)}, bf16[1,5,96,384]{3,2,1,0:T(8,128)(2,1)}, u32[]{:S(2)}, u32[]{:S(2)}) collective-permute-start(bf16[1,5,96,384]{3,2,1,0:T(8,128)(2,1)} %get-tuple-element.67), channel_id=1, source_target_pairs={{0,28},{1,29},{2,30},{3,31},{4,0},{5,1},{6,2},{7,3},{8,4},{9,5},{1... | collective-permute-start | bytes 1105928 | tf_op jit(solution)/shard_map/ppermute | solution.py:22
  98.7 11.3 %shard_map.107 = (f32[1024,768]{1,0:T(8,128)S(1)}, bf16[5,1024,256]{2,1,0:T(8,128)(2,1)S(1)}) custom-call(s32[7]{0:T(128)S(1)} %pad_add_fusion.place_ref, f32[5]{0:T(128)S(1)} %get-tuple-element.80.gs_ref, f32[5]{0:T(128)S(1)} %get-tuple-element.81.us_ref, bf16[2,5,96,384]{3,2,1,0:T(8,128)(2,1)S(1)} %bitcast.19, ...), custom_call_target="tpu_custom_call" | custom-call | flops 1048576 | bytes 1048576 | tf_op jit(solution)/shard_map/pallas_call | solution.py:92
  110.0 2.5 %shard_map.109 = (bf16[256,384]{1,0:T(8,128)(2,1)S(1)}, bf16[256,384]{1,0:T(8,128)(2,1)S(1)}) custom-call(s32[7]{0:T(128)S(1)} %pad_add_fusion.place_ref, f32[5]{0:T(128)S(1)} %get-tuple-element.80.gs_ref, f32[5]{0:T(128)S(1)} %get-tuple-element.81.us_ref, bf16[1,5,96,384]{3,2,1,0:T(8,128)(2,1)S(1)} %collective-permute-done.17.refs_0_, ...), custom_call_target="tpu_custom_call" | custom-call | flops 1006632960 | bytes 4194304 | tf_op jit(solution)/shard_map/pallas_call | solution.py:137
  112.7 3.5 %collective-permute-start.21 = (bf16[256,384]{1,0:T(8,128)(2,1)S(1)}, bf16[256,384]{1,0:T(8,128)(2,1)S(1)}, u32[]{:S(2)}, u32[]{:S(2)}) collective-permute-start(bf16[256,384]{1,0:T(8,128)(2,1)S(1)} %get-tuple-element.77), channel_id=1, source_target_pairs={{0,3},{1,2},{2,1},{3,0},{4,7},{5,6},{6,5},{7,4},{8,11},{9,10},{10,... | collective-permute-start | bytes 589832 | tf_op jit(solution)/shard_map/ppermute | solution.py:17
  116.2 2.5 %shard_map.108 = (bf16[256,384]{1,0:T(8,128)(2,1)S(1)}, bf16[256,384]{1,0:T(8,128)(2,1)S(1)}) custom-call(s32[7]{0:T(128)S(1)} %pad_add_fusion.place_ref, f32[5]{0:T(128)S(1)} %get-tuple-element.80.gs_ref, f32[5]{0:T(128)S(1)} %get-tuple-element.81.us_ref, bf16[1,5,96,384]{3,2,1,0:T(8,128)(2,1)S(1)} %collective-permute-done.17.refs_0_, ...), custom_call_target="tpu_custom_call" | custom-call | flops 1006632960 | bytes 4194304 | tf_op jit(solution)/shard_map/pallas_call | solution.py:137
  118.8 4.6 %collective-permute-done.21.refs_3_ = bf16[256,384]{1,0:T(8,128)(2,1)S(1)} collective-permute-done((bf16[256,384]{1,0:T(8,128)(2,1)S(1)}, bf16[256,384]{1,0:T(8,128)(2,1)S(1)}, u32[]{:S(2)}, u32[]{:S(2)}) %collective-permute-start.21) | collective-permute-done | bytes 196640 | tf_op jit(solution)/shard_map/ppermute | solution.py:17
  125.1 13.7 %all_to_all.10 = bf16[8,32,768]{2,1,0:T(8,128)(2,1)S(1)} all-to-all(bf16[8,32,768]{2,1,0:T(8,128)(2,1)S(1)} %bitcast.20), channel_id=1, replica_groups=mesh['feat'=8,'tok'=32] {'feat'}, dimensions={0} | all-to-all | bytes 786432 | tf_op jit(solution)/shard_map/all_to_all | solution.py:260
  138.9 11.8 %all_to_all.11 = bf16[8,32,768]{2,1,0:T(8,128)(2,1)S(1)} all-to-all(bf16[8,32,768]{2,1,0:T(8,128)(2,1)S(1)} %broadcast_in_dim.27), channel_id=1, replica_groups=mesh['feat'=8,'tok'=32] {'feat'}, dimensions={0} | all-to-all | bytes 786432 | tf_op jit(solution)/shard_map/all_to_all | solution.py:262
  (60 shorter events, 16.9 us)
Async XLA Ops:
  0.6 150.0 %copy-start = (bf16[768,1536]{1,0:T(8,128)(2,1)S(1)}, bf16[768,1536]{1,0:T(8,128)(2,1)}, u32[]{:S(2)}) copy-start(bf16[768,1536]{1,0:T(8,128)(2,1)} %param.16) | copy-start | bytes 7077892
  2.9 5.1 %collective-permute-start = (bf16[2,5,24,384]{3,2,1,0:T(8,128)(2,1)S(1)}, bf16[2,5,24,384]{3,2,1,0:T(8,128)(2,1)S(1)}, u32[]{:S(2)}, u32[]{:S(2)}) collective-permute-start(bf16[2,5,24,384]{3,2,1,0:T(8,128)(2,1)S(1)} %get-tuple-element.42), channel_id=1, source_target_pairs={{0,1},{1,0},{2,3},{3,2},{4,5},{5,4},{6,7},{7,6},{8,9},{9,8},{10,11... | collective-permute-start | bytes 552968 | tf_op jit(solution)/shard_map/ppermute | solution.py:17
  6.2 6.2 %collective-permute-start.1 = (bf16[2,5,24,384]{3,2,1,0:T(8,128)(2,1)S(1)}, bf16[2,5,24,384]{3,2,1,0:T(8,128)(2,1)S(1)}, u32[]{:S(2)}, u32[]{:S(2)}) collective-permute-start(bf16[2,5,24,384]{3,2,1,0:T(8,128)(2,1)S(1)} %get-tuple-element.43), channel_id=1, source_target_pairs={{0,2},{1,3},{2,0},{3,1},{4,6},{5,7},{6,4},{7,5},{8,10},{9,11},{10,... | collective-permute-start | bytes 552968 | tf_op jit(solution)/shard_map/ppermute | solution.py:17
  6.2 10.3 %collective-permute-start.2 = (bf16[2,5,24,384]{3,2,1,0:T(8,128)(2,1)S(1)}, bf16[2,5,24,384]{3,2,1,0:T(8,128)(2,1)S(1)}, u32[]{:S(2)}, u32[]{:S(2)}) collective-permute-start(bf16[2,5,24,384]{3,2,1,0:T(8,128)(2,1)S(1)} %get-tuple-element.44), channel_id=1, source_target_pairs={{0,3},{1,2},{2,1},{3,0},{4,7},{5,6},{6,5},{7,4},{8,11},{9,10},{10,... | collective-permute-start | bytes 552968 | tf_op jit(solution)/shard_map/ppermute | solution.py:17
  16.6 23.7 %collective-permute-start.5 = (bf16[256,1536]{1,0:T(8,128)(2,1)}, bf16[256,1536]{1,0:T(8,128)(2,1)}, u32[]{:S(2)}, u32[]{:S(2)}) collective-permute-start(bf16[256,1536]{1,0:T(8,128)(2,1)} %param.9), channel_id=1, source_target_pairs={{0,2},{1,3},{2,0},{3,1},{4,6},{5,7},{6,4},{7,5},{8,10},{9,11},{10,... | collective-permute-start | bytes 2359304 | tf_op jit(solution)/shard_map/ppermute | solution.py:17
  16.7 20.4 %collective-permute-start.4 = (bf16[2,5,96,384]{3,2,1,0:T(8,128)(2,1)S(1)}, bf16[2,5,96,384]{3,2,1,0:T(8,128)(2,1)}, u32[]{:S(2)}, u32[]{:S(2)}) collective-permute-start(bf16[2,5,96,384]{3,2,1,0:T(8,128)(2,1)S(1)} %bitcast.17), channel_id=1, source_target_pairs={{0,28},{1,29},{2,30},{3,31},{4,0},{5,1},{6,2},{7,3},{8,4},{9,5},{1... | collective-permute-start | bytes 2211848 | tf_op jit(solution)/shard_map/ppermute | solution.py:22
  21.7 18.6 %collective-permute-start.3 = (bf16[2,5,96,384]{3,2,1,0:T(8,128)(2,1)S(1)}, bf16[2,5,96,384]{3,2,1,0:T(8,128)(2,1)}, u32[]{:S(2)}, u32[]{:S(2)}) collective-permute-start(bf16[2,5,96,384]{3,2,1,0:T(8,128)(2,1)S(1)} %bitcast.18), channel_id=1, source_target_pairs={{0,4},{1,5},{2,6},{3,7},{4,8},{5,9},{6,10},{7,11},{8,12},{9,13},{1... | collective-permute-start | bytes 2211848 | tf_op jit(solution)/shard_map/ppermute | solution.py:22
  22.8 23.8 %collective-permute-start.10 = (bf16[256,768]{1,0:T(8,128)(2,1)S(1)}, bf16[256,768]{1,0:T(8,128)(2,1)S(1)}, u32[]{:S(2)}, u32[]{:S(2)}) collective-permute-start(bf16[256,768]{1,0:T(8,128)(2,1)S(1)} %constant_dynamic-slice_fusion.1), channel_id=1, source_target_pairs={{0,128},{32,160},{64,192},{96,224},{128,0},{160,32},{192,64},{224,... | collective-permute-start | bytes 1179656 | tf_op jit(solution)/shard_map/ppermute | solution.py:17
  25.8 20.8 %collective-permute-start.9 = (bf16[256,768]{1,0:T(8,128)(2,1)S(1)}, bf16[256,768]{1,0:T(8,128)(2,1)S(1)}, u32[]{:S(2)}, u32[]{:S(2)}) collective-permute-start(bf16[256,768]{1,0:T(8,128)(2,1)S(1)} %constant_dynamic-slice_fusion.1), channel_id=1, source_target_pairs={{0,64},{32,96},{64,0},{96,32},{128,192},{160,224},{192,128},{224,1... | collective-permute-start | bytes 1179656 | tf_op jit(solution)/shard_map/ppermute | solution.py:17
  41.4 23.6 %collective-permute-start.8 = (bf16[512,768]{1,0:T(8,128)(2,1)S(1)}, bf16[512,768]{1,0:T(8,128)(2,1)S(1)}, u32[]{:S(2)}, u32[]{:S(2)}) collective-permute-start(bf16[512,768]{1,0:T(8,128)(2,1)S(1)} %pad_maximum_fusion.1), channel_id=1, source_target_pairs={{0,32},{32,0},{64,96},{96,64},{128,160},{160,128},{192,224},{224,1... | collective-permute-start | bytes 2359304 | tf_op jit(solution)/shard_map/ppermute | solution.py:17
  43.9 21.1 %collective-permute-start.6 = (bf16[2,5,96,384]{3,2,1,0:T(8,128)(2,1)}, bf16[2,5,96,384]{3,2,1,0:T(8,128)(2,1)}, u32[]{:S(2)}, u32[]{:S(2)}) collective-permute-start(bf16[2,5,96,384]{3,2,1,0:T(8,128)(2,1)} %collective-permute-done.3.refs_1_), channel_id=1, source_target_pairs={{0,4},{1,5},{2,6},{3,7},{4,8},{5,9},{6,10},{7,11},{8,12},{9,13},{1... | collective-permute-start | bytes 2211848 | tf_op jit(solution)/shard_map/ppermute | solution.py:22
  43.9 21.1 %collective-permute-start.7 = (bf16[2,5,96,384]{3,2,1,0:T(8,128)(2,1)}, bf16[2,5,96,384]{3,2,1,0:T(8,128)(2,1)}, u32[]{:S(2)}, u32[]{:S(2)}) collective-permute-start(bf16[2,5,96,384]{3,2,1,0:T(8,128)(2,1)} %collective-permute-done.4.refs_2_), channel_id=1, source_target_pairs={{0,28},{1,29},{2,30},{3,31},{4,0},{5,1},{6,2},{7,3},{8,4},{9,5},{1... | collective-permute-start | bytes 2211848 | tf_op jit(solution)/shard_map/ppermute | solution.py:22
  46.6 9.6 %collective-permute-start.12 = (bf16[256,768]{1,0:T(8,128)(2,1)S(1)}, bf16[256,768]{1,0:T(8,128)(2,1)S(1)}, u32[]{:S(2)}, u32[]{:S(2)}) collective-permute-start(bf16[256,768]{1,0:T(8,128)(2,1)S(1)} %constant_dynamic-slice_fusion), channel_id=1, source_target_pairs={{0,128},{32,160},{64,192},{96,224},{128,0},{160,32},{192,64},{224,... | collective-permute-start | bytes 1179656 | tf_op jit(solution)/shard_map/ppermute | solution.py:17
  49.5 15.5 %collective-permute-start.11 = (bf16[256,768]{1,0:T(8,128)(2,1)S(1)}, bf16[256,768]{1,0:T(8,128)(2,1)S(1)}, u32[]{:S(2)}, u32[]{:S(2)}) collective-permute-start(bf16[256,768]{1,0:T(8,128)(2,1)S(1)} %constant_dynamic-slice_fusion), channel_id=1, source_target_pairs={{0,64},{32,96},{64,0},{96,32},{128,192},{160,224},{192,128},{224,1... | collective-permute-start | bytes 1179656 | tf_op jit(solution)/shard_map/ppermute | solution.py:17
  66.8 26.7 %collective-permute-start.16 = (bf16[3,512,768]{2,1,0:T(8,128)(2,1)}, bf16[3,512,768]{2,1,0:T(8,128)(2,1)}, u32[]{:S(2)}, u32[]{:S(2)}) collective-permute-start(bf16[3,512,768]{2,1,0:T(8,128)(2,1)} %pad_maximum_fusion.refs_9_), channel_id=1, source_target_pairs={{0,1},{1,0},{2,3},{3,2},{4,5},{5,4},{6,7},{7,6},{8,9},{9,8},{10,11... | collective-permute-start | bytes 7077896 | tf_op jit(solution)/shard_map/ppermute | solution.py:17
  72.3 26.4 %copy-start.6 = (f32[2,5]{1,0:T(2,128)S(1)}, f32[2,5]{1,0:T(2,128)}, u32[]{:S(2)}) copy-start(f32[2,5]{1,0:T(2,128)} %param.13) | copy-start | bytes 124
  74.4 19.1 %collective-permute-start.15 = (bf16[512,1536]{1,0:T(8,128)(2,1)}, bf16[512,1536]{1,0:T(8,128)(2,1)}, u32[]{:S(2)}, u32[]{:S(2)}) collective-permute-start(bf16[512,1536]{1,0:T(8,128)(2,1)} %constant_dynamic-update-slice_fusion.refs_7_), channel_id=1, source_target_pairs={{0,1},{1,0},{2,3},{3,2},{4,5},{5,4},{6,7},{7,6},{8,9},{9,8},{10,11... | collective-permute-start | bytes 4718600 | tf_op jit(solution)/shard_map/ppermute | solution.py:17
  74.4 19.1 %collective-permute-start.13 = (bf16[2,5,96,384]{3,2,1,0:T(8,128)(2,1)}, bf16[2,5,96,384]{3,2,1,0:T(8,128)(2,1)}, u32[]{:S(2)}, u32[]{:S(2)}) collective-permute-start(bf16[2,5,96,384]{3,2,1,0:T(8,128)(2,1)} %collective-permute-done.6.refs_3_), channel_id=1, source_target_pairs={{0,4},{1,5},{2,6},{3,7},{4,8},{5,9},{6,10},{7,11},{8,12},{9,13},{1... | collective-permute-start | bytes 2211848 | tf_op jit(solution)/shard_map/ppermute | solution.py:22
  74.4 19.1 %collective-permute-start.14 = (bf16[2,5,96,384]{3,2,1,0:T(8,128)(2,1)}, bf16[2,5,96,384]{3,2,1,0:T(8,128)(2,1)}, u32[]{:S(2)}, u32[]{:S(2)}) collective-permute-start(bf16[2,5,96,384]{3,2,1,0:T(8,128)(2,1)} %collective-permute-done.7.refs_4_), channel_id=1, source_target_pairs={{0,28},{1,29},{2,30},{3,31},{4,0},{5,1},{6,2},{7,3},{8,4},{9,5},{1... | collective-permute-start | bytes 2211848 | tf_op jit(solution)/shard_map/ppermute | solution.py:22
  95.5 14.5 %collective-permute-start.17 = (bf16[1,5,96,384]{3,2,1,0:T(8,128)(2,1)}, bf16[1,5,96,384]{3,2,1,0:T(8,128)(2,1)S(1)}, u32[]{:S(2)}, u32[]{:S(2)}) collective-permute-start(bf16[1,5,96,384]{3,2,1,0:T(8,128)(2,1)} %get-tuple-element.66), channel_id=1, source_target_pairs={{0,4},{1,5},{2,6},{3,7},{4,8},{5,9},{6,10},{7,11},{8,12},{9,13},{1... | collective-permute-start | bytes 1105928 | tf_op jit(solution)/shard_map/ppermute | solution.py:22
  95.5 14.5 %collective-permute-start.18 = (bf16[1,5,96,384]{3,2,1,0:T(8,128)(2,1)}, bf16[1,5,96,384]{3,2,1,0:T(8,128)(2,1)}, u32[]{:S(2)}, u32[]{:S(2)}) collective-permute-start(bf16[1,5,96,384]{3,2,1,0:T(8,128)(2,1)} %get-tuple-element.67), channel_id=1, source_target_pairs={{0,28},{1,29},{2,30},{3,31},{4,0},{5,1},{6,2},{7,3},{8,4},{9,5},{1... | collective-permute-start | bytes 1105928 | tf_op jit(solution)/shard_map/ppermute | solution.py:22
  112.5 6.3 %collective-permute-start.20 = (bf16[256,384]{1,0:T(8,128)(2,1)S(1)}, bf16[256,384]{1,0:T(8,128)(2,1)S(1)}, u32[]{:S(2)}, u32[]{:S(2)}) collective-permute-start(bf16[256,384]{1,0:T(8,128)(2,1)S(1)} %get-tuple-element.76), channel_id=1, source_target_pairs={{0,2},{1,3},{2,0},{3,1},{4,6},{5,7},{6,4},{7,5},{8,10},{9,11},{10,... | collective-permute-start | bytes 589832 | tf_op jit(solution)/shard_map/ppermute | solution.py:17
  112.7 10.8 %collective-permute-start.21 = (bf16[256,384]{1,0:T(8,128)(2,1)S(1)}, bf16[256,384]{1,0:T(8,128)(2,1)S(1)}, u32[]{:S(2)}, u32[]{:S(2)}) collective-permute-start(bf16[256,384]{1,0:T(8,128)(2,1)S(1)} %get-tuple-element.77), channel_id=1, source_target_pairs={{0,3},{1,2},{2,1},{3,0},{4,7},{5,6},{6,5},{7,4},{8,11},{9,10},{10,... | collective-permute-start | bytes 589832 | tf_op jit(solution)/shard_map/ppermute | solution.py:17
  118.7 4.7 %collective-permute-start.19 = (bf16[256,384]{1,0:T(8,128)(2,1)S(1)}, bf16[256,384]{1,0:T(8,128)(2,1)S(1)}, u32[]{:S(2)}, u32[]{:S(2)}) collective-permute-start(bf16[256,384]{1,0:T(8,128)(2,1)S(1)} %get-tuple-element.75), channel_id=1, source_target_pairs={{0,1},{1,0},{2,3},{3,2},{4,5},{5,4},{6,7},{7,6},{8,9},{9,8},{10,11... | collective-permute-start | bytes 589832 | tf_op jit(solution)/shard_map/ppermute | solution.py:17
  (6 other events, 91.1 us)

commit v3 on v2

--- a/solution.py
+++ b/solution.py
@@ -41,13 +41,15 @@
     b_out[...] = b_ref[...]
 
 
-def block_of_rows(own_refs, partner_refs, j, x_lo, rows, start, width):
-    blk = partner_refs[0].shape[2]
+def block_of_rows(own_refs, partner_refs, j, m, x_lo, start, width):
+    blk = partner_refs[0].shape[1]
+    rows = own_refs[0].shape[0]
+    if j < 2 and m < 2:
+        return own_refs[m][:, pl.ds(pl.multiple_of((x_lo ^ j) * blk + start, 128), width)]
+    column = pl.ds(pl.multiple_of(start, 128), width)
     if j < 2:
-        column = pl.ds(pl.multiple_of((x_lo ^ j) * blk + start, 128), width)
-        return jnp.concatenate([ref[rows, column] for ref in own_refs])
-    column = pl.ds(pl.multiple_of(start, 128), width)
-    return jnp.concatenate([ref[j - 2, rows, column] for ref in partner_refs])
+        return own_refs[2 * m - 2 + j][:, column]
+    return partner_refs[m % 2 * 3 + j - 2][pl.ds(m // 2 * rows, rows), column]
 
 
 def last_window(z, z_count, share, blk, window):
@@ -57,8 +59,8 @@
 
 def early_kernel(place_ref, gs_ref, us_ref, *refs, z_count, window):
     n_w = z_count - 1
-    w_refs, own_refs, partner_refs = refs[:n_w], refs[n_w : n_w + 2], refs[n_w + 2 : n_w + 4]
-    acc, windows, w_mem = refs[n_w + 4 :]
+    w_refs, own_refs, partner_refs = refs[:n_w], refs[n_w : n_w + 6], refs[n_w + 6 : n_w + 12]
+    acc, windows, w_mem = refs[n_w + 12 :]
     x_lo, z = place_ref[5], place_ref[6]
     blk, both = w_mem.shape[1:]
     share, width = blk // z_count, both // 2
@@ -72,8 +74,10 @@
             at = pl.ds(pl.multiple_of((origin + z_count) % z_count * share, 16), share)
             for side in range(2):
                 w_mem[j % 2, at, side * width : (side + 1) * width] = ref[side, slot]
-        windows[j] = block_of_rows(own_refs, partner_refs, j, x_lo, slice(None), start, window)
-        x = block_of_rows(own_refs, partner_refs, j, x_lo, slice(None), 0, blk)
+        for m in range(4):
+            at = pl.ds(m * own_refs[0].shape[0], own_refs[0].shape[0])
+            windows[j, at] = block_of_rows(own_refs, partner_refs, j, m, x_lo, start, window)
+        x = jnp.concatenate([block_of_rows(own_refs, partner_refs, j, m, x_lo, 0, blk) for m in range(4)])
         term = jnp.dot(x, w_mem[j % 2], preferred_element_type=jnp.float32)
         g, u = term[:, :width] * gs_ref[slot], term[:, width:] * us_ref[slot]
         if j == 0:
@@ -86,7 +90,7 @@
 
 def early(place, gs, us, weights, own_rows, partner_rows):
     blk = own_rows[0].shape[1] // 2
-    rows = 2 * own_rows[0].shape[0]
+    rows = 4 * own_rows[0].shape[0]
     _, slots, share, width = weights[0].shape
     window = min(2 * 128 * ((share + 127) // 128), blk)
     return pl.pallas_call(
@@ -95,11 +99,11 @@
             jax.ShapeDtypeStruct((rows, 2 * width), jnp.float32),
             jax.ShapeDtypeStruct((slots, rows, window), jnp.bfloat16),
         ],
-        in_specs=[SMEM] * 3 + [VMEM] * (len(weights) + 4),
+        in_specs=[SMEM] * 3 + [VMEM] * (len(weights) + 12),
         out_specs=[VMEM] * 2,
         scratch_shapes=[pltpu.VMEM((2, blk, 2 * width), jnp.bfloat16)],
         compiler_params=pltpu.CompilerParams(vmem_limit_bytes=VMEM_BYTES),
-        cost_estimate=pl.CostEstimate(flops=2**20, bytes_accessed=2**20, transcendentals=0),
+        cost_estimate=pl.CostEstimate(flops=2**33, bytes_accessed=2**20, transcendentals=0),
     )(place, gs, us, *weights, *own_rows, *partner_rows)
 
 
@@ -113,7 +117,7 @@
     row, start = last_window(z, z_count, share, z_count * share, window)
     at = pl.ds(pl.multiple_of(row - start, 16), share)
     w_mem[...] = jnp.zeros_like(w_mem)
-    mine = [pl.ds((2 * core + first) * rows, rows) for core in range(2)]
+    mine = [pl.ds((2 * first + core) * rows, rows) for core in range(2)]
     for core in range(2):
         acc[pl.ds(core * rows, rows)] = acc_ref[mine[core]]
     for j in range(slots):
@@ -193,8 +197,8 @@
         )(own, *got)
         return out.reshape(shape[:2] + (4 * shape[2],) + shape[3:])
 
-    def block_of(value):
-        return lax.dynamic_slice(value, (0, x_lo * blk), (rows, blk))
+    def block_of(value, which):
+        return lax.dynamic_slice(value, (0, which * blk), (rows, blk))
 
     def step(forward, back):
         return shifted(forward, 1), shifted(back, -1)
@@ -203,23 +207,33 @@
     near = swapped(packed[1], "tok", 1)
     w0 = place([packed[0], near, *far])
     barrier = lax.optimization_barrier
-    first = block_of(tokens)
+    first, other = block_of(tokens, x_lo), block_of(tokens, 1 - x_lo)
     p0_y1, p0_y2 = swapped(first, "feat", 2), swapped(first, "feat", 4)
-    w0, later = barrier((w0, tokens))
+    w0, other, later = barrier((w0, other, tokens))
     w1 = step(w0, w0)
-    s2 = swapped(later, "tok", 2)
-    w1, s2, first, later = barrier((w1, s2, first, later))
+    s2_own = swapped(other, "tok", 2)
+    first, s2_own, p0_y1, p0_y2 = barrier((first, s2_own, p0_y1, p0_y2))
+    s2_other = swapped(first, "tok", 2)
+    p2_y1 = swapped(s2_own, "feat", 2)
+    w1, s2_own, s2_other, p0_y1, p0_y2, p2_y1, first, later = barrier(
+        (w1, s2_own, s2_other, p0_y1, p0_y2, p2_y1, first, later)
+    )
     w2 = step(*w1)
-    second = block_of(s2)
-    p_x = swapped(jnp.concatenate([first, second]), "feat", 1)
-    second, p0_y1, p0_y2 = barrier((second, p0_y1, p0_y2))
-    p2_y1, p2_y2 = swapped(second, "feat", 2), swapped(second, "feat", 4)
-    w2, p_x, p2_y1, p2_y2, p0_y1, p0_y2, s2, later = barrier((w2, p_x, p2_y1, p2_y2, p0_y1, p0_y2, s2, later))
+    p_x = swapped(jnp.concatenate([first, s2_own]), "feat", 1)
+    p2_y2 = swapped(s2_own, "feat", 4)
+    s1 = swapped(later, "tok", 1)
+    s1, s2_other = barrier((s1, s2_other))
+    s3_other = swapped(s2_other, "tok", 1)
+    p_y1 = jnp.concatenate([p0_y1, p2_y1])
+    w2, p_x, p2_y2, p0_y2, p_y1, s2_own, s1, s3_other = barrier((w2, p_x, p2_y2, p0_y2, p_y1, s2_own, s1, s3_other))
     w3 = step(*w2)
-    own0 = jnp.concatenate([later, s2])
-    partner0 = jnp.stack([p_x, jnp.concatenate([p0_y1, p2_y1]), jnp.concatenate([p0_y2, p2_y2])])
-    own1, partner1 = swapped(own0, "tok", 1), swapped(partner0, "tok", 1)
-    w3, own0, own1, partner0, partner1 = barrier((w3, own0, own1, partner0, partner1))
+    p_y2 = jnp.concatenate([p0_y2, p2_y2])
+    q_y1 = swapped(p_y1, "tok", 1)
+    q_y1, s2_own = barrier((q_y1, s2_own))
+    s3_own = swapped(s2_own, "tok", 1)
+    partner_rows = [p_x, p_y1, p_y2, swapped(p_x, "tok", 1), q_y1, swapped(p_y2, "tok", 1)]
+    own_rows = [later, s1, s2_own, s2_other, s3_own, s3_other]
+    w3, own_rows, partner_rows = barrier((w3, own_rows, partner_rows))
     half_shape = (1,) + w3[0].shape[1:]
     cut = pl.pallas_call(
         halves_kernel,
@@ -238,7 +252,7 @@
     gs = lax.dynamic_index_in_dim(gate_scale, x_lo, 0, keepdims=False)
     us = lax.dynamic_index_in_dim(up_scale, x_lo, 0, keepdims=False)
 
-    acc, windows = early(here, gs, us, (w0, *w1, *w2, *w3), (own0, own1), (partner0, partner1))
+    acc, windows = early(here, gs, us, (w0, *w1, *w2, *w3), own_rows, partner_rows)
     z_count = lax.axis_size("tok") // GROUP
     made = late(here, gs, us, w4, acc, windows, z_count, 1)
     far_hidden = [swapped(v, "tok", mask) for v, mask in zip(made, (2, 3))]

time: 153 us -> 154 us (level)
  local copies, waits for them, and re-layouts: 8.61 us -> 12.7 us
  waiting for transfers between devices: 58.9 us -> 56.1 us
    unnamed x17 -> x45, local copies, waits for them, and re-layouts: 4.22 us -> 10.6 us
    ppermute x14 -> x19, waiting for transfers between devices: 28.3 us -> 25.3 us  [swapped(): lax.ppermute(value, axis, [(i, i ^ mask) for i in range(lax.axis_size(axi...]
    another operation x2 -> x0, other arithmetic: 1.79 us -> none  [per_device(): jnp.stack([p_x, jnp.concatenate([p0_y1, p2_y1]), jnp.concatenate([p0_y2,...]
    ppermute x14 -> x19, starting transfers between devices: 21.5 us -> 21.7 us  [swapped(): lax.ppermute(value, axis, [(i, i ^ mask) for i in range(lax.axis_size(axi...]
  transfers between devices with their start and end apart: 22 -> 27, of which waited for: 8 -> 10; matrix products, arithmetic and copies ran while one was open for 4% -> 3% of each run, Pallas kernels for 9% -> 8%
where the time goes in v3:
time: 154 us
  waiting for transfers between devices  56.1 us (36%)
  starting transfers between devices  35.2 us (23%)
  blocking collectives  26.7 us (17%)
  Pallas kernels  18.7 us (12%)
  local copies, waits for them, and re-layouts  12.7 us (8%)
  matrix products  1.66 us (1%)
  other arithmetic  1.59 us (1%)
    ppermute x8, waiting for transfers between devices, shifted(): lax.ppermute(value, 'tok', [(i, (i + step * GROUP) % count) for i in rang...  30.8 us
    ppermute x19, waiting for transfers between devices, swapped(): lax.ppermute(value, axis, [(i, i ^ mask) for i in range(lax.axis_size(axi...  25.3 us
    ppermute x19, starting transfers between devices, swapped(): lax.ppermute(value, axis, [(i, i ^ mask) for i in range(lax.axis_size(axi...  21.7 us
    all_to_all x1, blocking collectives, per_device(): terms = lax.all_to_all(parts, 'feat', 0, 0)  14.9 us
    ppermute x8, starting transfers between devices, shifted(): lax.ppermute(value, 'tok', [(i, (i + step * GROUP) % count) for i in rang...  13.5 us
    all_to_all x1, blocking collectives, per_device(): lax.all_to_all(jnp.broadcast_to(mine[None], parts.shape), 'feat', 0, 0)  11.8 us
    unnamed x45, local copies, waits for them, and re-layouts  10.6 us
    pallas_call x1, Pallas kernels, early(): pl.pallas_call(functools.partial(early_kernel, z_count=blk // share, wind...  9.81 us
  transfers between devices with their start and end apart: 27, of which 10 were waited for; matrix products, arithmetic and copies ran while one was open for 3% of the time, Pallas kernels for 8%

profile of v3, /device:TPU:1, one launch (start us, length us, event | category | flops | bytes accessed | tf_op | source)
XLA Modules:
  0.0 153.5 jit_solution(9749170848308299378)
XLA Ops:
  3.7 3.2 %collective-permute-start = (bf16[2,5,24,384]{3,2,1,0:T(8,128)(2,1)}, bf16[2,5,24,384]{3,2,1,0:T(8,128)(2,1)S(1)}, u32[]{:S(2)}, u32[]{:S(2)}) collective-permute-start(bf16[2,5,24,384]{3,2,1,0:T(8,128)(2,1)} %get-tuple-element.60), channel_id=1, source_target_pairs={{0,1},{1,0},{2,3},{3,2},{4,5},{5,4},{6,7},{7,6},{8,9},{9,8},{10,11... | collective-permute-start | bytes 552968 | tf_op jit(solution)/shard_map/ppermute | solution.py:17
  6.9 1.6 %collective-permute-start.2 = (bf16[2,5,24,384]{3,2,1,0:T(8,128)(2,1)}, bf16[2,5,24,384]{3,2,1,0:T(8,128)(2,1)}, u32[]{:S(2)}, u32[]{:S(2)}) collective-permute-start(bf16[2,5,24,384]{3,2,1,0:T(8,128)(2,1)} %get-tuple-element.62), channel_id=1, source_target_pairs={{0,3},{1,2},{2,1},{3,0},{4,7},{5,6},{6,5},{7,4},{8,11},{9,10},{10,... | collective-permute-start | bytes 552968 | tf_op jit(solution)/shard_map/ppermute | solution.py:17
  11.4 2.1 %collective-permute-done.1.refs_2_ = bf16[2,5,24,384]{3,2,1,0:T(8,128)(2,1)} collective-permute-done((bf16[2,5,24,384]{3,2,1,0:T(8,128)(2,1)}, bf16[2,5,24,384]{3,2,1,0:T(8,128)(2,1)}, u32[]{:S(2)}, u32[]{:S(2)}) %collective-permute-start.1) | collective-permute-done | bytes 184352 | tf_op jit(solution)/shard_map/ppermute | solution.py:17
  13.5 4.2 %collective-permute-done.2.refs_3_ = bf16[2,5,24,384]{3,2,1,0:T(8,128)(2,1)} collective-permute-done((bf16[2,5,24,384]{3,2,1,0:T(8,128)(2,1)}, bf16[2,5,24,384]{3,2,1,0:T(8,128)(2,1)}, u32[]{:S(2)}, u32[]{:S(2)}) %collective-permute-start.2) | collective-permute-done | bytes 184352 | tf_op jit(solution)/shard_map/ppermute | solution.py:17
  19.0 5.1 %collective-permute-start.4 = (bf16[2,5,96,384]{3,2,1,0:T(8,128)(2,1)S(1)}, bf16[2,5,96,384]{3,2,1,0:T(8,128)(2,1)S(1)}, u32[]{:S(2)}, u32[]{:S(2)}) collective-permute-start(bf16[2,5,96,384]{3,2,1,0:T(8,128)(2,1)S(1)} %bitcast.12), channel_id=1, source_target_pairs={{0,28},{1,29},{2,30},{3,31},{4,0},{5,1},{6,2},{7,3},{8,4},{9,5},{1... | collective-permute-start | bytes 2211848 | tf_op jit(solution)/shard_map/ppermute | solution.py:22
  24.0 4.8 %collective-permute-done.6 = bf16[256,768]{1,0:T(8,128)(2,1)S(1)} collective-permute-done((bf16[256,768]{1,0:T(8,128)(2,1)S(1)}, bf16[256,768]{1,0:T(8,128)(2,1)S(1)}, u32[]{:S(2)}, u32[]{:S(2)}) %collective-permute-start.6) | collective-permute-done | bytes 393248 | tf_op jit(solution)/shard_map/ppermute | solution.py:17
  31.1 8.4 %collective-permute-done.4.refs_2_ = bf16[2,5,96,384]{3,2,1,0:T(8,128)(2,1)S(1)} collective-permute-done((bf16[2,5,96,384]{3,2,1,0:T(8,128)(2,1)S(1)}, bf16[2,5,96,384]{3,2,1,0:T(8,128)(2,1)S(1)}, u32[]{:S(2)}, u32[]{:S(2)}) %collective-permute-start.4) | collective-permute-done | bytes 737312 | tf_op jit(solution)/shard_map/ppermute | solution.py:22
  39.5 3.1 %collective-permute-done.3.refs_1_ = bf16[2,5,96,384]{3,2,1,0:T(8,128)(2,1)S(1)} collective-permute-done((bf16[2,5,96,384]{3,2,1,0:T(8,128)(2,1)S(1)}, bf16[2,5,96,384]{3,2,1,0:T(8,128)(2,1)S(1)}, u32[]{:S(2)}, u32[]{:S(2)}) %collective-permute-start.3) | collective-permute-done | bytes 737312 | tf_op jit(solution)/shard_map/ppermute | solution.py:22
  44.3 2.5 %collective-permute-start.12 = (bf16[512,768]{1,0:T(8,128)(2,1)S(1)}, bf16[512,768]{1,0:T(8,128)(2,1)}, u32[]{:S(2)}, u32[]{:S(2)}) collective-permute-start(bf16[512,768]{1,0:T(8,128)(2,1)S(1)} %pad_maximum_fusion), channel_id=1, source_target_pairs={{0,32},{32,0},{64,96},{96,64},{128,160},{160,128},{192,224},{224,1... | collective-permute-start | bytes 2359304 | tf_op jit(solution)/shard_map/ppermute | solution.py:17
  46.9 3.0 %collective-permute-start.11 = (bf16[2,5,96,384]{3,2,1,0:T(8,128)(2,1)S(1)}, bf16[2,5,96,384]{3,2,1,0:T(8,128)(2,1)}, u32[]{:S(2)}, u32[]{:S(2)}) collective-permute-start(bf16[2,5,96,384]{3,2,1,0:T(8,128)(2,1)S(1)} %collective-permute-done.4.refs_2_), channel_id=1, source_target_pairs={{0,28},{1,29},{2,30},{3,31},{4,0},{5,1},{6,2},{7,3},{8,4},{9,5},{1... | collective-permute-start | bytes 2211848 | tf_op jit(solution)/shard_map/ppermute | solution.py:22
  49.9 2.6 %collective-permute-start.13 = (bf16[256,768]{1,0:T(8,128)(2,1)S(1)}, bf16[256,768]{1,0:T(8,128)(2,1)S(1)}, u32[]{:S(2)}, u32[]{:S(2)}) collective-permute-start(bf16[256,768]{1,0:T(8,128)(2,1)S(1)} %collective-permute-done.5.refs_9_), channel_id=1, source_target_pairs={{0,128},{32,160},{64,192},{96,224},{128,0},{160,32},{192,64},{224,... | collective-permute-start | bytes 1179656 | tf_op jit(solution)/shard_map/ppermute | solution.py:17
  53.7 8.0 %collective-permute-done.13 = bf16[256,768]{1,0:T(8,128)(2,1)S(1)} collective-permute-done((bf16[256,768]{1,0:T(8,128)(2,1)S(1)}, bf16[256,768]{1,0:T(8,128)(2,1)S(1)}, u32[]{:S(2)}, u32[]{:S(2)}) %collective-permute-start.13) | collective-permute-done | bytes 393248 | tf_op jit(solution)/shard_map/ppermute | solution.py:17
  61.6 5.0 %collective-permute-done.10.refs_3_ = bf16[2,5,96,384]{3,2,1,0:T(8,128)(2,1)} collective-permute-done((bf16[2,5,96,384]{3,2,1,0:T(8,128)(2,1)S(1)}, bf16[2,5,96,384]{3,2,1,0:T(8,128)(2,1)}, u32[]{:S(2)}, u32[]{:S(2)}) %collective-permute-start.10) | collective-permute-done | bytes 737312 | tf_op jit(solution)/shard_map/ppermute | solution.py:22
  69.7 2.7 %collective-permute-start.17 = (bf16[2,5,96,384]{3,2,1,0:T(8,128)(2,1)}, bf16[2,5,96,384]{3,2,1,0:T(8,128)(2,1)}, u32[]{:S(2)}, u32[]{:S(2)}) collective-permute-start(bf16[2,5,96,384]{3,2,1,0:T(8,128)(2,1)} %collective-permute-done.11.refs_4_), channel_id=1, source_target_pairs={{0,28},{1,29},{2,30},{3,31},{4,0},{5,1},{6,2},{7,3},{8,4},{9,5},{1... | collective-permute-start | bytes 2211848 | tf_op jit(solution)/shard_map/ppermute | solution.py:22
  74.8 14.2 %collective-permute-done.16.f_ref.refs_5_ = bf16[2,5,96,384]{3,2,1,0:T(8,128)(2,1)} collective-permute-done((bf16[2,5,96,384]{3,2,1,0:T(8,128)(2,1)}, bf16[2,5,96,384]{3,2,1,0:T(8,128)(2,1)}, u32[]{:S(2)}, u32[]{:S(2)}) %collective-permute-start.16) | collective-permute-done | bytes 737312 | tf_op jit(solution)/shard_map/ppermute | solution.py:22
  90.2 2.2 %collective-permute-start.22 = (bf16[1,5,96,384]{3,2,1,0:T(8,128)(2,1)S(1)}, bf16[1,5,96,384]{3,2,1,0:T(8,128)(2,1)S(1)}, u32[]{:S(2)}, u32[]{:S(2)}) collective-permute-start(bf16[1,5,96,384]{3,2,1,0:T(8,128)(2,1)S(1)} %get-tuple-element.94), channel_id=1, source_target_pairs={{0,4},{1,5},{2,6},{3,7},{4,8},{5,9},{6,10},{7,11},{8,12},{9,13},{1... | collective-permute-start | bytes 1105928 | tf_op jit(solution)/shard_map/ppermute | solution.py:22
  100.6 9.8 %shard_map.107 = (f32[1024,768]{1,0:T(8,128)S(1)}, bf16[5,1024,256]{2,1,0:T(8,128)(2,1)S(1)}) custom-call(s32[7]{0:T(128)S(1)} %pad_add_fusion.place_ref, f32[5]{0:T(128)S(1)} %get-tuple-element.118.gs_ref, f32[5]{0:T(128)S(1)} %get-tuple-element.119.us_ref, bf16[2,5,96,384]{3,2,1,0:T(8,128)(2,1)S(1)} %bitcast.14, bf16[2,5,96,384]{3,2,1,0:T(8,128)(2,1)S(1)} %copy-done.13, ...), custom_call_target="tpu_custom_call" | custom-call | flops 8589934592 | bytes 1048576 | tf_op jit(solution)/shard_map/pallas_call | solution.py:96
  110.4 2.1 %shard_map.109 = (bf16[256,384]{1,0:T(8,128)(2,1)S(1)}, bf16[256,384]{1,0:T(8,128)(2,1)S(1)}) custom-call(s32[7]{0:T(128)S(1)} %pad_add_fusion.place_ref, f32[5]{0:T(128)S(1)} %get-tuple-element.118.gs_ref, f32[5]{0:T(128)S(1)} %get-tuple-element.119.us_ref, bf16[1,5,96,384]{3,2,1,0:T(8,128)(2,1)S(1)} %collective-permute-done.22.refs_0_, ...), custom_call_target="tpu_custom_call" | custom-call | flops 1006632960 | bytes 4194304 | tf_op jit(solution)/shard_map/pallas_call | solution.py:141
  112.9 3.0 %collective-permute-start.26 = (bf16[256,384]{1,0:T(8,128)(2,1)S(1)}, bf16[256,384]{1,0:T(8,128)(2,1)S(1)}, u32[]{:S(2)}, u32[]{:S(2)}) collective-permute-start(bf16[256,384]{1,0:T(8,128)(2,1)S(1)} %get-tuple-element.113), channel_id=1, source_target_pairs={{0,3},{1,2},{2,1},{3,0},{4,7},{5,6},{6,5},{7,4},{8,11},{9,10},{10,... | collective-permute-start | bytes 589832 | tf_op jit(solution)/shard_map/ppermute | solution.py:17
  115.9 2.1 %shard_map.108 = (bf16[256,384]{1,0:T(8,128)(2,1)S(1)}, bf16[256,384]{1,0:T(8,128)(2,1)S(1)}) custom-call(s32[7]{0:T(128)S(1)} %pad_add_fusion.place_ref, f32[5]{0:T(128)S(1)} %get-tuple-element.118.gs_ref, f32[5]{0:T(128)S(1)} %get-tuple-element.119.us_ref, bf16[1,5,96,384]{3,2,1,0:T(8,128)(2,1)S(1)} %collective-permute-done.22.refs_0_, ...), custom_call_target="tpu_custom_call" | custom-call | flops 1006632960 | bytes 4194304 | tf_op jit(solution)/shard_map/pallas_call | solution.py:141
  118.1 5.3 %collective-permute-done.26.refs_3_ = bf16[256,384]{1,0:T(8,128)(2,1)S(1)} collective-permute-done((bf16[256,384]{1,0:T(8,128)(2,1)S(1)}, bf16[256,384]{1,0:T(8,128)(2,1)S(1)}, u32[]{:S(2)}, u32[]{:S(2)}) %collective-permute-start.26) | collective-permute-done | bytes 196640 | tf_op jit(solution)/shard_map/ppermute | solution.py:17
  125.1 14.9 %all_to_all.10 = bf16[8,32,768]{2,1,0:T(8,128)(2,1)S(1)} all-to-all(bf16[8,32,768]{2,1,0:T(8,128)(2,1)S(1)} %bitcast.15), channel_id=1, replica_groups=mesh['feat'=8,'tok'=32] {'feat'}, dimensions={0} | all-to-all | bytes 786432 | tf_op jit(solution)/shard_map/all_to_all | solution.py:274
  140.0 11.8 %all_to_all.11 = bf16[8,32,768]{2,1,0:T(8,128)(2,1)S(1)} all-to-all(bf16[8,32,768]{2,1,0:T(8,128)(2,1)S(1)} %broadcast_in_dim.27), channel_id=1, replica_groups=mesh['feat'=8,'tok'=32] {'feat'}, dimensions={0} | all-to-all | bytes 786432 | tf_op jit(solution)/shard_map/all_to_all | solution.py:276
  151.8 1.7 %convolution_convert_fusion = bf16[256,1536]{1,0:T(8,128)(2,1)} fusion(bf16[256,768]{1,0:T(8,128)(2,1)S(1)} %bitcast.16, bf16[768,1536]{1,0:T(8,128)(2,1)S(1)} %copy-done), kind=kOutput, calls=%fused_computation | convolution fusion | flops 604372992 | bytes 3538944 | tf_op jit(solution)/shard_map/dot_general | solution.py:277
  (96 shorter events, 29.1 us)
Async XLA Ops:
  3.7 7.7 %collective-permute-start = (bf16[2,5,24,384]{3,2,1,0:T(8,128)(2,1)}, bf16[2,5,24,384]{3,2,1,0:T(8,128)(2,1)S(1)}, u32[]{:S(2)}, u32[]{:S(2)}) collective-permute-start(bf16[2,5,24,384]{3,2,1,0:T(8,128)(2,1)} %get-tuple-element.60), channel_id=1, source_target_pairs={{0,1},{1,0},{2,3},{3,2},{4,5},{5,4},{6,7},{7,6},{8,9},{9,8},{10,11... | collective-permute-start | bytes 552968 | tf_op jit(solution)/shard_map/ppermute | solution.py:17
  6.9 6.6 %collective-permute-start.1 = (bf16[2,5,24,384]{3,2,1,0:T(8,128)(2,1)}, bf16[2,5,24,384]{3,2,1,0:T(8,128)(2,1)}, u32[]{:S(2)}, u32[]{:S(2)}) collective-permute-start(bf16[2,5,24,384]{3,2,1,0:T(8,128)(2,1)} %get-tuple-element.61), channel_id=1, source_target_pairs={{0,2},{1,3},{2,0},{3,1},{4,6},{5,7},{6,4},{7,5},{8,10},{9,11},{10,... | collective-permute-start | bytes 552968 | tf_op jit(solution)/shard_map/ppermute | solution.py:17
  6.9 10.8 %collective-permute-start.2 = (bf16[2,5,24,384]{3,2,1,0:T(8,128)(2,1)}, bf16[2,5,24,384]{3,2,1,0:T(8,128)(2,1)}, u32[]{:S(2)}, u32[]{:S(2)}) collective-permute-start(bf16[2,5,24,384]{3,2,1,0:T(8,128)(2,1)} %get-tuple-element.62), channel_id=1, source_target_pairs={{0,3},{1,2},{2,1},{3,0},{4,7},{5,6},{6,5},{7,4},{8,11},{9,10},{10,... | collective-permute-start | bytes 552968 | tf_op jit(solution)/shard_map/ppermute | solution.py:17
  9.7 14.3 %collective-permute-start.7 = (bf16[256,768]{1,0:T(8,128)(2,1)S(1)}, bf16[256,768]{1,0:T(8,128)(2,1)S(1)}, u32[]{:S(2)}, u32[]{:S(2)}) collective-permute-start(bf16[256,768]{1,0:T(8,128)(2,1)S(1)} %get-tuple-element.72), channel_id=1, source_target_pairs={{0,128},{32,160},{64,192},{96,224},{128,0},{160,32},{192,64},{224,... | collective-permute-start | bytes 1179656 | tf_op jit(solution)/shard_map/ppermute | solution.py:17
  11.0 17.8 %collective-permute-start.6 = (bf16[256,768]{1,0:T(8,128)(2,1)S(1)}, bf16[256,768]{1,0:T(8,128)(2,1)S(1)}, u32[]{:S(2)}, u32[]{:S(2)}) collective-permute-start(bf16[256,768]{1,0:T(8,128)(2,1)S(1)} %get-tuple-element.72), channel_id=1, source_target_pairs={{0,64},{32,96},{64,0},{96,32},{128,192},{160,224},{192,128},{224,1... | collective-permute-start | bytes 1179656 | tf_op jit(solution)/shard_map/ppermute | solution.py:17
  18.9 10.8 %collective-permute-start.5 = (bf16[256,768]{1,0:T(8,128)(2,1)S(1)}, bf16[256,768]{1,0:T(8,128)(2,1)S(1)}, u32[]{:S(2)}, u32[]{:S(2)}) collective-permute-start(bf16[256,768]{1,0:T(8,128)(2,1)S(1)} %get-tuple-element.64), channel_id=1, source_target_pairs={{0,2},{1,3},{2,0},{3,1},{4,6},{5,7},{6,4},{7,5},{8,10},{9,11},{10,... | collective-permute-start | bytes 1179656 | tf_op jit(solution)/shard_map/ppermute | solution.py:17
  19.0 20.6 %collective-permute-start.4 = (bf16[2,5,96,384]{3,2,1,0:T(8,128)(2,1)S(1)}, bf16[2,5,96,384]{3,2,1,0:T(8,128)(2,1)S(1)}, u32[]{:S(2)}, u32[]{:S(2)}) collective-permute-start(bf16[2,5,96,384]{3,2,1,0:T(8,128)(2,1)S(1)} %bitcast.12), channel_id=1, source_target_pairs={{0,28},{1,29},{2,30},{3,31},{4,0},{5,1},{6,2},{7,3},{8,4},{9,5},{1... | collective-permute-start | bytes 2211848 | tf_op jit(solution)/shard_map/ppermute | solution.py:22
  24.0 18.6 %collective-permute-start.3 = (bf16[2,5,96,384]{3,2,1,0:T(8,128)(2,1)S(1)}, bf16[2,5,96,384]{3,2,1,0:T(8,128)(2,1)S(1)}, u32[]{:S(2)}, u32[]{:S(2)}) collective-permute-start(bf16[2,5,96,384]{3,2,1,0:T(8,128)(2,1)S(1)} %bitcast.13), channel_id=1, source_target_pairs={{0,4},{1,5},{2,6},{3,7},{4,8},{5,9},{6,10},{7,11},{8,12},{9,13},{1... | collective-permute-start | bytes 2211848 | tf_op jit(solution)/shard_map/ppermute | solution.py:22
  29.6 13.0 %collective-permute-start.9 = (bf16[256,768]{1,0:T(8,128)(2,1)S(1)}, bf16[256,768]{1,0:T(8,128)(2,1)S(1)}, u32[]{:S(2)}, u32[]{:S(2)}) collective-permute-start(bf16[256,768]{1,0:T(8,128)(2,1)S(1)} %collective-permute-done.5.refs_9_), channel_id=1, source_target_pairs={{0,64},{32,96},{64,0},{96,32},{128,192},{160,224},{192,128},{224,1... | collective-permute-start | bytes 1179656 | tf_op jit(solution)/shard_map/ppermute | solution.py:17
  29.9 12.8 %collective-permute-start.8 = (bf16[256,768]{1,0:T(8,128)(2,1)S(1)}, bf16[256,768]{1,0:T(8,128)(2,1)S(1)}, u32[]{:S(2)}, u32[]{:S(2)}) collective-permute-start(bf16[256,768]{1,0:T(8,128)(2,1)S(1)} %get-tuple-element.72), channel_id=1, source_target_pairs={{0,2},{1,3},{2,0},{3,1},{4,6},{5,7},{6,4},{7,5},{8,10},{9,11},{10,... | collective-permute-start | bytes 1179656 | tf_op jit(solution)/shard_map/ppermute | solution.py:17
  42.7 9.8 %collective-permute-start.14 = (bf16[256,1536]{1,0:T(8,128)(2,1)S(1)}, bf16[256,1536]{1,0:T(8,128)(2,1)S(1)}, u32[]{:S(2)}, u32[]{:S(2)}) collective-permute-start(bf16[256,1536]{1,0:T(8,128)(2,1)S(1)} %copy-done.2), channel_id=1, source_target_pairs={{0,1},{1,0},{2,3},{3,2},{4,5},{5,4},{6,7},{7,6},{8,9},{9,8},{10,11... | collective-permute-start | bytes 2359304 | tf_op jit(solution)/shard_map/ppermute | solution.py:17
  44.3 22.3 %collective-permute-start.12 = (bf16[512,768]{1,0:T(8,128)(2,1)S(1)}, bf16[512,768]{1,0:T(8,128)(2,1)}, u32[]{:S(2)}, u32[]{:S(2)}) collective-permute-start(bf16[512,768]{1,0:T(8,128)(2,1)S(1)} %pad_maximum_fusion), channel_id=1, source_target_pairs={{0,32},{32,0},{64,96},{96,64},{128,160},{160,128},{192,224},{224,1... | collective-permute-start | bytes 2359304 | tf_op jit(solution)/shard_map/ppermute | solution.py:17
  46.9 19.8 %collective-permute-start.10 = (bf16[2,5,96,384]{3,2,1,0:T(8,128)(2,1)S(1)}, bf16[2,5,96,384]{3,2,1,0:T(8,128)(2,1)}, u32[]{:S(2)}, u32[]{:S(2)}) collective-permute-start(bf16[2,5,96,384]{3,2,1,0:T(8,128)(2,1)S(1)} %collective-permute-done.3.refs_1_), channel_id=1, source_target_pairs={{0,4},{1,5},{2,6},{3,7},{4,8},{5,9},{6,10},{7,11},{8,12},{9,13},{1... | collective-permute-start | bytes 2211848 | tf_op jit(solution)/shard_map/ppermute | solution.py:22
  46.9 19.8 %collective-permute-start.11 = (bf16[2,5,96,384]{3,2,1,0:T(8,128)(2,1)S(1)}, bf16[2,5,96,384]{3,2,1,0:T(8,128)(2,1)}, u32[]{:S(2)}, u32[]{:S(2)}) collective-permute-start(bf16[2,5,96,384]{3,2,1,0:T(8,128)(2,1)S(1)} %collective-permute-done.4.refs_2_), channel_id=1, source_target_pairs={{0,28},{1,29},{2,30},{3,31},{4,0},{5,1},{6,2},{7,3},{8,4},{9,5},{1... | collective-permute-start | bytes 2211848 | tf_op jit(solution)/shard_map/ppermute | solution.py:22
  49.9 11.7 %collective-permute-start.13 = (bf16[256,768]{1,0:T(8,128)(2,1)S(1)}, bf16[256,768]{1,0:T(8,128)(2,1)S(1)}, u32[]{:S(2)}, u32[]{:S(2)}) collective-permute-start(bf16[256,768]{1,0:T(8,128)(2,1)S(1)} %collective-permute-done.5.refs_9_), channel_id=1, source_target_pairs={{0,128},{32,160},{64,192},{96,224},{128,0},{160,32},{192,64},{224,... | collective-permute-start | bytes 1179656 | tf_op jit(solution)/shard_map/ppermute | solution.py:17
  52.5 14.2 %collective-permute-start.15 = (bf16[256,768]{1,0:T(8,128)(2,1)S(1)}, bf16[256,768]{1,0:T(8,128)(2,1)S(1)}, u32[]{:S(2)}, u32[]{:S(2)}) collective-permute-start(bf16[256,768]{1,0:T(8,128)(2,1)S(1)} %collective-permute-done.8.refs_10_), channel_id=1, source_target_pairs={{0,1},{1,0},{2,3},{3,2},{4,5},{5,4},{6,7},{7,6},{8,9},{9,8},{10,11... | collective-permute-start | bytes 1179656 | tf_op jit(solution)/shard_map/ppermute | solution.py:17
  69.1 20.0 %collective-permute-start.21 = (bf16[512,768]{1,0:T(8,128)(2,1)}, bf16[512,768]{1,0:T(8,128)(2,1)}, u32[]{:S(2)}, u32[]{:S(2)}) collective-permute-start(bf16[512,768]{1,0:T(8,128)(2,1)} %constant_dynamic-update-slice_fusion.refs_15_), channel_id=1, source_target_pairs={{0,1},{1,0},{2,3},{3,2},{4,5},{5,4},{6,7},{7,6},{8,9},{9,8},{10,11... | collective-permute-start | bytes 2359304 | tf_op jit(solution)/shard_map/ppermute | solution.py:17
  69.2 19.9 %collective-permute-start.20 = (bf16[512,768]{1,0:T(8,128)(2,1)}, bf16[512,768]{1,0:T(8,128)(2,1)}, u32[]{:S(2)}, u32[]{:S(2)}) collective-permute-start(bf16[512,768]{1,0:T(8,128)(2,1)} %collective-permute-done.12.refs_13_), channel_id=1, source_target_pairs={{0,1},{1,0},{2,3},{3,2},{4,5},{5,4},{6,7},{7,6},{8,9},{9,8},{10,11... | collective-permute-start | bytes 2359304 | tf_op jit(solution)/shard_map/ppermute | solution.py:17
  69.7 19.3 %collective-permute-start.16 = (bf16[2,5,96,384]{3,2,1,0:T(8,128)(2,1)}, bf16[2,5,96,384]{3,2,1,0:T(8,128)(2,1)}, u32[]{:S(2)}, u32[]{:S(2)}) collective-permute-start(bf16[2,5,96,384]{3,2,1,0:T(8,128)(2,1)} %collective-permute-done.10.refs_3_), channel_id=1, source_target_pairs={{0,4},{1,5},{2,6},{3,7},{4,8},{5,9},{6,10},{7,11},{8,12},{9,13},{1... | collective-permute-start | bytes 2211848 | tf_op jit(solution)/shard_map/ppermute | solution.py:22
  69.7 19.3 %collective-permute-start.17 = (bf16[2,5,96,384]{3,2,1,0:T(8,128)(2,1)}, bf16[2,5,96,384]{3,2,1,0:T(8,128)(2,1)}, u32[]{:S(2)}, u32[]{:S(2)}) collective-permute-start(bf16[2,5,96,384]{3,2,1,0:T(8,128)(2,1)} %collective-permute-done.11.refs_4_), channel_id=1, source_target_pairs={{0,28},{1,29},{2,30},{3,31},{4,0},{5,1},{6,2},{7,3},{8,4},{9,5},{1... | collective-permute-start | bytes 2211848 | tf_op jit(solution)/shard_map/ppermute | solution.py:22
  72.4 16.7 %collective-permute-start.19 = (bf16[256,768]{1,0:T(8,128)(2,1)S(1)}, bf16[256,768]{1,0:T(8,128)(2,1)}, u32[]{:S(2)}, u32[]{:S(2)}) collective-permute-start(bf16[256,768]{1,0:T(8,128)(2,1)S(1)} %collective-permute-done.5.refs_9_), channel_id=1, source_target_pairs={{0,1},{1,0},{2,3},{3,2},{4,5},{5,4},{6,7},{7,6},{8,9},{9,8},{10,11... | collective-permute-start | bytes 1179656 | tf_op jit(solution)/shard_map/ppermute | solution.py:17
  90.2 20.2 %collective-permute-start.22 = (bf16[1,5,96,384]{3,2,1,0:T(8,128)(2,1)S(1)}, bf16[1,5,96,384]{3,2,1,0:T(8,128)(2,1)S(1)}, u32[]{:S(2)}, u32[]{:S(2)}) collective-permute-start(bf16[1,5,96,384]{3,2,1,0:T(8,128)(2,1)S(1)} %get-tuple-element.94), channel_id=1, source_target_pairs={{0,4},{1,5},{2,6},{3,7},{4,8},{5,9},{6,10},{7,11},{8,12},{9,13},{1... | collective-permute-start | bytes 1105928 | tf_op jit(solution)/shard_map/ppermute | solution.py:22
  92.5 17.9 %collective-permute-start.23 = (bf16[1,5,96,384]{3,2,1,0:T(8,128)(2,1)S(1)}, bf16[1,5,96,384]{3,2,1,0:T(8,128)(2,1)S(1)}, u32[]{:S(2)}, u32[]{:S(2)}) collective-permute-start(bf16[1,5,96,384]{3,2,1,0:T(8,128)(2,1)S(1)} %get-tuple-element.95), channel_id=1, source_target_pairs={{0,28},{1,29},{2,30},{3,31},{4,0},{5,1},{6,2},{7,3},{8,4},{9,5},{1... | collective-permute-start | bytes 1105928 | tf_op jit(solution)/shard_map/ppermute | solution.py:22
  112.9 10.5 %collective-permute-start.26 = (bf16[256,384]{1,0:T(8,128)(2,1)S(1)}, bf16[256,384]{1,0:T(8,128)(2,1)S(1)}, u32[]{:S(2)}, u32[]{:S(2)}) collective-permute-start(bf16[256,384]{1,0:T(8,128)(2,1)S(1)} %get-tuple-element.113), channel_id=1, source_target_pairs={{0,3},{1,2},{2,1},{3,0},{4,7},{5,6},{6,5},{7,4},{8,11},{9,10},{10,... | collective-permute-start | bytes 589832 | tf_op jit(solution)/shard_map/ppermute | solution.py:17
  (25 other events, 604.1 us)

commit v4 on v3

--- a/solution.py
+++ b/solution.py
@@ -9,7 +9,7 @@
 GROUP = 4
 SMEM = pl.BlockSpec(memory_space=pltpu.SMEM)
 VMEM = pl.BlockSpec(memory_space=pltpu.VMEM)
-VMEM_BYTES = 30 * 2**20
+VMEM_BYTES = 60 * 2**20
 SMALL_BYTES = 16 * 2**20
 
 
@@ -57,97 +57,119 @@
     return row, jnp.minimum(row // 128 * 128, blk - window)
 
 
-def early_kernel(place_ref, gs_ref, us_ref, *refs, z_count, window):
-    n_w = z_count - 1
-    w_refs, own_refs, partner_refs = refs[:n_w], refs[n_w : n_w + 6], refs[n_w + 6 : n_w + 12]
-    acc, windows, w_mem = refs[n_w + 12 :]
+def lay_kernel(place_ref, *refs, z_count, share):
+    own_refs, partner_refs, x_ref, windows = refs[:6], refs[6:12], refs[12], refs[13]
     x_lo, z = place_ref[5], place_ref[6]
-    blk, both = w_mem.shape[1:]
-    share, width = blk // z_count, both // 2
-    row, start = last_window(z, z_count, share, blk, window)
-    last = pl.ds(pl.multiple_of(row, 16), share)
+    rows, (blk, window) = own_refs[0].shape[0], (x_ref.shape[2], windows.shape[2])
+    _, start = last_window(z, z_count, share, blk, window)
     for j in range(5):
-        slot = place_ref[j]
-        w_mem[j % 2, last] = jnp.zeros((share, both), w_mem.dtype)
-        for i, ref in enumerate(w_refs):
-            origin = z - (i + 1) // 2 if i % 2 else z + i // 2
-            at = pl.ds(pl.multiple_of((origin + z_count) % z_count * share, 16), share)
-            for side in range(2):
-                w_mem[j % 2, at, side * width : (side + 1) * width] = ref[side, slot]
         for m in range(4):
-            at = pl.ds(m * own_refs[0].shape[0], own_refs[0].shape[0])
+            at = pl.ds(m * rows, rows)
+            x_ref[j, at] = block_of_rows(own_refs, partner_refs, j, m, x_lo, 0, blk)
             windows[j, at] = block_of_rows(own_refs, partner_refs, j, m, x_lo, start, window)
-        x = jnp.concatenate([block_of_rows(own_refs, partner_refs, j, m, x_lo, 0, blk) for m in range(4)])
-        term = jnp.dot(x, w_mem[j % 2], preferred_element_type=jnp.float32)
-        g, u = term[:, :width] * gs_ref[slot], term[:, width:] * us_ref[slot]
-        if j == 0:
-            acc[:, :width] = g
-            acc[:, width:] = u
-        else:
-            acc[:, :width] += g
-            acc[:, width:] += u
-
-
-def early(place, gs, us, weights, own_rows, partner_rows):
-    blk = own_rows[0].shape[1] // 2
-    rows = 4 * own_rows[0].shape[0]
-    _, slots, share, width = weights[0].shape
+
+
+def lay(place, own_rows, partner_rows, share):
+    rows, features = own_rows[0].shape
+    blk = features // 2
     window = min(2 * 128 * ((share + 127) // 128), blk)
     return pl.pallas_call(
-        functools.partial(early_kernel, z_count=blk // share, window=window),
-        out_shape=[
-            jax.ShapeDtypeStruct((rows, 2 * width), jnp.float32),
-            jax.ShapeDtypeStruct((slots, rows, window), jnp.bfloat16),
-        ],
-        in_specs=[SMEM] * 3 + [VMEM] * (len(weights) + 12),
+        functools.partial(lay_kernel, z_count=blk // share, share=share),
+        out_shape=[jax.ShapeDtypeStruct((5, 4 * rows, w), jnp.bfloat16) for w in (blk, window)],
+        in_specs=[SMEM] + [VMEM] * 12,
         out_specs=[VMEM] * 2,
-        scratch_shapes=[pltpu.VMEM((2, blk, 2 * width), jnp.bfloat16)],
         compiler_params=pltpu.CompilerParams(vmem_limit_bytes=VMEM_BYTES),
-        cost_estimate=pl.CostEstimate(flops=2**33, bytes_accessed=2**20, transcendentals=0),
-    )(place, gs, us, *weights, *own_rows, *partner_rows)
-
-
-def late_kernel(place_ref, gs_ref, us_ref, *refs, z_count, first):
-    w_refs, acc_ref, window_ref, out_refs = refs[:2], refs[2], refs[3], refs[4:6]
-    w_mem, acc = refs[6:]
+        cost_estimate=pl.CostEstimate(flops=2**20, bytes_accessed=2**20, transcendentals=0),
+    )(place, *own_rows, *partner_rows)
+
+
+def early_kernel(place_ref, gs_ref, us_ref, x_ref, *refs, z_count):
+    w_refs, acc, w_mem = refs[: z_count - 1], refs[z_count - 1], refs[z_count]
+    j = pl.program_id(0)
+    z, slot = place_ref[6], place_ref[j]
+    blk, both = w_mem.shape
+    share, width = blk // z_count, both // 2
+    w_mem[pl.ds(pl.multiple_of((z + z_count // 2) % z_count * share, 16), share)] = jnp.zeros((share, both), w_mem.dtype)
+    for i, ref in enumerate(w_refs):
+        origin = z - (i + 1) // 2 if i % 2 else z + i // 2
+        at = pl.ds(pl.multiple_of((origin + z_count) % z_count * share, 16), share)
+        for side in range(2):
+            w_mem[at, side * width : (side + 1) * width] = ref[side, 0]
+    term = jnp.dot(x_ref[0], w_mem[...], preferred_element_type=jnp.float32)
+    g, u = term[:, :width] * gs_ref[slot], term[:, width:] * us_ref[slot]
+
+    @pl.when(j == 0)
+    def _():
+        acc[:, :width] = g
+        acc[:, width:] = u
+
+    @pl.when(j > 0)
+    def _():
+        acc[:, :width] += g
+        acc[:, width:] += u
+
+
+def early(place, gs, us, weights, x):
+    slots, rows, blk = x.shape
+    share, width = weights[0].shape[2:]
+    return pl.pallas_call(
+        functools.partial(early_kernel, z_count=blk // share),
+        out_shape=jax.ShapeDtypeStruct((rows, 2 * width), jnp.float32),
+        grid_spec=pltpu.PrefetchScalarGridSpec(
+            num_scalar_prefetch=3,
+            grid=(slots,),
+            in_specs=[pl.BlockSpec((1, rows, blk), lambda j, place, *_: (j, 0, 0))]
+            + [pl.BlockSpec((2, 1, share, width), lambda j, place, *_: (0, place[j], 0, 0))] * len(weights),
+            out_specs=pl.BlockSpec((rows, 2 * width), lambda j, *_: (0, 0)),
+            scratch_shapes=[pltpu.VMEM((blk, 2 * width), jnp.bfloat16)],
+        ),
+        compiler_params=pltpu.CompilerParams(vmem_limit_bytes=VMEM_BYTES),
+        cost_estimate=pl.CostEstimate(flops=2**20, bytes_accessed=2**20, transcendentals=0),
+    )(place, gs, us, x, *weights)
+
+
+def late_kernel(place_ref, gs_ref, us_ref, g_ref, u_ref, acc_ref, window_ref, near_ref, far_ref, w_mem, acc, *, z_count):
     z = place_ref[6]
-    share, width = w_refs[0].shape[2:]
+    share, width = g_ref.shape[2:]
     slots, rows, window = window_ref.shape
-    rows //= 4
+    rows //= 2
     row, start = last_window(z, z_count, share, z_count * share, window)
     at = pl.ds(pl.multiple_of(row - start, 16), share)
     w_mem[...] = jnp.zeros_like(w_mem)
-    mine = [pl.ds((2 * first + core) * rows, rows) for core in range(2)]
-    for core in range(2):
-        acc[pl.ds(core * rows, rows)] = acc_ref[mine[core]]
     for j in range(slots):
         slot = place_ref[j]
-        for side in range(2):
-            w_mem[j, at, side * width : (side + 1) * width] = w_refs[side][0, slot]
-        x = jnp.concatenate([window_ref[j, at_core] for at_core in mine])
-        term = jnp.dot(x, w_mem[j], preferred_element_type=jnp.float32)
-        acc[:, :width] += term[:, :width] * gs_ref[slot]
-        acc[:, width:] += term[:, width:] * us_ref[slot]
+        w_mem[j, at, :width] = g_ref[0, slot]
+        w_mem[j, at, width:] = u_ref[0, slot]
+        term = jnp.dot(window_ref[j], w_mem[j], preferred_element_type=jnp.float32)
+        before = acc_ref if j == 0 else acc
+        acc[:, :width] = before[:, :width] + term[:, :width] * gs_ref[slot]
+        acc[:, width:] = before[:, width:] + term[:, width:] * us_ref[slot]
     g = acc[:, :width]
     out = (g / (1.0 + jnp.exp(-g)) * acc[:, width:]).astype(jnp.bfloat16)
-    out_refs[0][...] = out[:rows]
-    out_refs[1][...] = out[rows:]
+    near_ref[...] = out[:rows]
+    far_ref[...] = out[rows:]
 
 
 def late(place, gs, us, weights, acc, windows, z_count, first):
     slots, rows, window = windows.shape
     rows //= 4
-    width = weights[0].shape[3]
+    share, width = weights[0].shape[2:]
     return pl.pallas_call(
-        functools.partial(late_kernel, z_count=z_count, first=first),
+        functools.partial(late_kernel, z_count=z_count),
         out_shape=[jax.ShapeDtypeStruct((rows, width), jnp.bfloat16)] * 2,
-        in_specs=[SMEM] * 3 + [VMEM] * 4,
-        out_specs=[VMEM] * 2,
+        grid=(1,),
+        in_specs=[SMEM] * 3
+        + [pl.BlockSpec((1, slots, share, width), lambda i: (0, 0, 0, 0))] * 2
+        + [
+            pl.BlockSpec((2 * rows, 2 * width), lambda i: (first, 0)),
+            pl.BlockSpec((slots, 2 * rows, window), lambda i: (0, first, 0)),
+        ],
+        out_specs=[pl.BlockSpec((rows, width), lambda i: (0, 0))] * 2,
         scratch_shapes=[
             pltpu.VMEM((slots, window, 2 * width), jnp.bfloat16),
             pltpu.VMEM((2 * rows, 2 * width), jnp.float32),
         ],
-        compiler_params=pltpu.CompilerParams(vmem_limit_bytes=SMALL_BYTES),
+        compiler_params=pltpu.CompilerParams(vmem_limit_bytes=VMEM_BYTES),
         cost_estimate=pl.CostEstimate(
             flops=2 * 2 * 2 * rows * slots * window * width, bytes_accessed=4 * 2**20, transcendentals=2 * rows * width
         ),
@@ -176,6 +198,13 @@
     member, z = tok % GROUP, tok // GROUP
     x_lo, core = member // 2, member % 2
     block_id = feat * blocks + x_lo
+
+    wanted = lax.dynamic_index_in_dim(partners, block_id, 0, keepdims=False)
+    labels = block_id ^ jnp.array([0, 1, 2, 4, 8], jnp.int32)
+    order = jnp.sum(jnp.where(labels[:, None] == wanted[None, :], jnp.arange(5, dtype=jnp.int32)[None, :], 0), axis=1)
+    here = jnp.concatenate([order, jnp.stack([x_lo, z]).astype(jnp.int32)])
+    gs = lax.dynamic_index_in_dim(gate_scale, x_lo, 0, keepdims=False)
+    us = lax.dynamic_index_in_dim(up_scale, x_lo, 0, keepdims=False)
 
     own = member[None].astype(jnp.int32)
     packed = pl.pallas_call(
@@ -233,7 +262,8 @@
     s3_own = swapped(s2_own, "tok", 1)
     partner_rows = [p_x, p_y1, p_y2, swapped(p_x, "tok", 1), q_y1, swapped(p_y2, "tok", 1)]
     own_rows = [later, s1, s2_own, s2_other, s3_own, s3_other]
-    w3, own_rows, partner_rows = barrier((w3, own_rows, partner_rows))
+    x, windows = lay(here, own_rows, partner_rows, w0.shape[2])
+    w3, x, windows = barrier((w3, x, windows))
     half_shape = (1,) + w3[0].shape[1:]
     cut = pl.pallas_call(
         halves_kernel,
@@ -245,14 +275,7 @@
     )(*w3)
     w4 = step(*cut)
 
-    wanted = lax.dynamic_index_in_dim(partners, block_id, 0, keepdims=False)
-    labels = block_id ^ jnp.array([0, 1, 2, 4, 8], jnp.int32)
-    order = jnp.sum(jnp.where(labels[:, None] == wanted[None, :], jnp.arange(5, dtype=jnp.int32)[None, :], 0), axis=1)
-    here = jnp.concatenate([order, jnp.stack([x_lo, z]).astype(jnp.int32)])
-    gs = lax.dynamic_index_in_dim(gate_scale, x_lo, 0, keepdims=False)
-    us = lax.dynamic_index_in_dim(up_scale, x_lo, 0, keepdims=False)
-
-    acc, windows = early(here, gs, us, (w0, *w1, *w2, *w3), own_rows, partner_rows)
+    acc = early(here, gs, us, (w0, *w1, *w2, *w3), x)
     z_count = lax.axis_size("tok") // GROUP
     made = late(here, gs, us, w4, acc, windows, z_count, 1)
     far_hidden = [swapped(v, "tok", mask) for v, mask in zip(made, (2, 3))]

time: 154 us -> 157 us (1.019)
  Pallas kernels: 18.7 us -> 34.4 us
  waiting for transfers between devices: 56.1 us -> 42.6 us
    pallas_call x3 -> x4, Pallas kernels: 14 us -> 30 us  [the longest x1 13.6 us: early(): pl.pallas_call(functools.partial(early_kernel, z_count=blk // share), out...]
    ppermute x8, waiting for transfers between devices: 30.8 us -> 20.6 us  [shifted(): lax.ppermute(value, 'tok', [(i, (i + step * GROUP) % count) for i in rang...]
    ppermute x19, waiting for transfers between devices: 25.3 us -> 21.9 us  [swapped(): lax.ppermute(value, axis, [(i, i ^ mask) for i in range(lax.axis_size(axi...]
    ppermute x8, starting transfers between devices: 13.5 us -> 15.4 us  [shifted(): lax.ppermute(value, 'tok', [(i, (i + step * GROUP) % count) for i in rang...]
    unnamed x45 -> x47, local copies, waits for them, and re-layouts: 10.6 us -> 9.46 us
  transfers between devices with their start and end apart: 27 -> 27, of which waited for: 10 -> 10; matrix products, arithmetic and copies ran while one was open for 3% -> 3% of each run, Pallas kernels for 8% -> 16%
where the time goes in v4:
time: 157 us
  waiting for transfers between devices  42.6 us (27%)
  starting transfers between devices  35.9 us (23%)
  Pallas kernels  34.4 us (22%)
  blocking collectives  27.2 us (17%)
  local copies, waits for them, and re-layouts  12.3 us (8%)
  other arithmetic  1.83 us (1%)
  matrix products  1.66 us (1%)
    ppermute x19, waiting for transfers between devices, swapped(): lax.ppermute(value, axis, [(i, i ^ mask) for i in range(lax.axis_size(axi...  21.9 us
    ppermute x8, waiting for transfers between devices, shifted(): lax.ppermute(value, 'tok', [(i, (i + step * GROUP) % count) for i in rang...  20.6 us
    ppermute x19, starting transfers between devices, swapped(): lax.ppermute(value, axis, [(i, i ^ mask) for i in range(lax.axis_size(axi...  20.5 us
    all_to_all x1, blocking collectives, per_device(): terms = lax.all_to_all(parts, 'feat', 0, 0)  15.5 us
    ppermute x8, starting transfers between devices, shifted(): lax.ppermute(value, 'tok', [(i, (i + step * GROUP) % count) for i in rang...  15.4 us
    pallas_call x1, Pallas kernels, early(): pl.pallas_call(functools.partial(early_kernel, z_count=blk // share), out...  13.6 us
    all_to_all x1, blocking collectives, per_device(): lax.all_to_all(jnp.broadcast_to(mine[None], parts.shape), 'feat', 0, 0)  11.7 us
    unnamed x47, local copies, waits for them, and re-layouts  9.46 us
  transfers between devices with their start and end apart: 27, of which 10 were waited for; matrix products, arithmetic and copies ran while one was open for 3% of the time, Pallas kernels for 16%

profile of v4, /device:TPU:1, one launch (start us, length us, event | category | flops | bytes accessed | tf_op | source)
XLA Modules:
  0.0 156.7 jit_solution(10959244313254743296)
XLA Ops:
  3.5 3.2 %collective-permute-start = (bf16[2,5,24,384]{3,2,1,0:T(8,128)(2,1)}, bf16[2,5,24,384]{3,2,1,0:T(8,128)(2,1)S(1)}, u32[]{:S(2)}, u32[]{:S(2)}) collective-permute-start(bf16[2,5,24,384]{3,2,1,0:T(8,128)(2,1)} %get-tuple-element.50), channel_id=1, source_target_pairs={{0,1},{1,0},{2,3},{3,2},{4,5},{5,4},{6,7},{7,6},{8,9},{9,8},{10,11... | collective-permute-start | bytes 552968 | tf_op jit(solution)/shard_map/ppermute | solution.py:17
  9.7 2.2 %collective-permute-start.7 = (bf16[256,768]{1,0:T(8,128)(2,1)S(1)}, bf16[256,768]{1,0:T(8,128)(2,1)S(1)}, u32[]{:S(2)}, u32[]{:S(2)}) collective-permute-start(bf16[256,768]{1,0:T(8,128)(2,1)S(1)} %get-tuple-element.62), channel_id=1, source_target_pairs={{0,128},{32,160},{64,192},{96,224},{128,0},{160,32},{192,64},{224,... | collective-permute-start | bytes 1179656 | tf_op jit(solution)/shard_map/ppermute | solution.py:17
  13.7 3.7 %collective-permute-done.2.refs_3_ = bf16[2,5,24,384]{3,2,1,0:T(8,128)(2,1)S(1)} collective-permute-done((bf16[2,5,24,384]{3,2,1,0:T(8,128)(2,1)S(1)}, bf16[2,5,24,384]{3,2,1,0:T(8,128)(2,1)S(1)}, u32[]{:S(2)}, u32[]{:S(2)}) %collective-permute-start.2) | collective-permute-done | bytes 184352 | tf_op jit(solution)/shard_map/ppermute | solution.py:17
  21.2 3.9 %collective-permute-start.4 = (bf16[2,5,96,384]{3,2,1,0:T(8,128)(2,1)S(1)}, bf16[2,5,96,384]{3,2,1,0:T(8,128)(2,1)S(1)}, u32[]{:S(2)}, u32[]{:S(2)}) collective-permute-start(bf16[2,5,96,384]{3,2,1,0:T(8,128)(2,1)S(1)} %bitcast.13), channel_id=1, source_target_pairs={{0,28},{1,29},{2,30},{3,31},{4,0},{5,1},{6,2},{7,3},{8,4},{9,5},{1... | collective-permute-start | bytes 2211848 | tf_op jit(solution)/shard_map/ppermute | solution.py:22
  25.1 4.2 %collective-permute-done.7 = bf16[256,768]{1,0:T(8,128)(2,1)S(1)} collective-permute-done((bf16[256,768]{1,0:T(8,128)(2,1)S(1)}, bf16[256,768]{1,0:T(8,128)(2,1)S(1)}, u32[]{:S(2)}, u32[]{:S(2)}) %collective-permute-start.7) | collective-permute-done | bytes 393248 | tf_op jit(solution)/shard_map/ppermute | solution.py:17
  31.6 10.2 %collective-permute-done.3.refs_1_ = bf16[2,5,96,384]{3,2,1,0:T(8,128)(2,1)S(1)} collective-permute-done((bf16[2,5,96,384]{3,2,1,0:T(8,128)(2,1)S(1)}, bf16[2,5,96,384]{3,2,1,0:T(8,128)(2,1)S(1)}, u32[]{:S(2)}, u32[]{:S(2)}) %collective-permute-start.3) | collective-permute-done | bytes 737312 | tf_op jit(solution)/shard_map/ppermute | solution.py:22
  42.8 2.5 %collective-permute-start.12 = (bf16[512,768]{1,0:T(8,128)(2,1)S(1)}, bf16[512,768]{1,0:T(8,128)(2,1)}, u32[]{:S(2)}, u32[]{:S(2)}) collective-permute-start(bf16[512,768]{1,0:T(8,128)(2,1)S(1)} %pad_maximum_fusion), channel_id=1, source_target_pairs={{0,32},{32,0},{64,96},{96,64},{128,160},{160,128},{192,224},{224,1... | collective-permute-start | bytes 2359304 | tf_op jit(solution)/shard_map/ppermute | solution.py:17
  46.3 3.9 %collective-permute-start.11 = (bf16[2,5,96,384]{3,2,1,0:T(8,128)(2,1)S(1)}, bf16[2,5,96,384]{3,2,1,0:T(8,128)(2,1)}, u32[]{:S(2)}, u32[]{:S(2)}) collective-permute-start(bf16[2,5,96,384]{3,2,1,0:T(8,128)(2,1)S(1)} %collective-permute-done.4.refs_2_), channel_id=1, source_target_pairs={{0,28},{1,29},{2,30},{3,31},{4,0},{5,1},{6,2},{7,3},{8,4},{9,5},{1... | collective-permute-start | bytes 2211848 | tf_op jit(solution)/shard_map/ppermute | solution.py:22
  50.3 2.6 %collective-permute-start.13 = (bf16[256,768]{1,0:T(8,128)(2,1)S(1)}, bf16[256,768]{1,0:T(8,128)(2,1)S(1)}, u32[]{:S(2)}, u32[]{:S(2)}) collective-permute-start(bf16[256,768]{1,0:T(8,128)(2,1)S(1)} %collective-permute-done.5.refs_2_), channel_id=1, source_target_pairs={{0,128},{32,160},{64,192},{96,224},{128,0},{160,32},{192,64},{224,... | collective-permute-start | bytes 1179656 | tf_op jit(solution)/shard_map/ppermute | solution.py:17
  54.7 7.3 %collective-permute-done.13 = bf16[256,768]{1,0:T(8,128)(2,1)S(1)} collective-permute-done((bf16[256,768]{1,0:T(8,128)(2,1)S(1)}, bf16[256,768]{1,0:T(8,128)(2,1)S(1)}, u32[]{:S(2)}, u32[]{:S(2)}) %collective-permute-start.13) | collective-permute-done | bytes 393248 | tf_op jit(solution)/shard_map/ppermute | solution.py:17
  62.0 5.0 %collective-permute-done.10.refs_3_ = bf16[2,5,96,384]{3,2,1,0:T(8,128)(2,1)} collective-permute-done((bf16[2,5,96,384]{3,2,1,0:T(8,128)(2,1)S(1)}, bf16[2,5,96,384]{3,2,1,0:T(8,128)(2,1)}, u32[]{:S(2)}, u32[]{:S(2)}) %collective-permute-start.10) | collective-permute-done | bytes 737312 | tf_op jit(solution)/shard_map/ppermute | solution.py:22
  70.1 2.7 %collective-permute-start.17 = (bf16[2,5,96,384]{3,2,1,0:T(8,128)(2,1)}, bf16[2,5,96,384]{3,2,1,0:T(8,128)(2,1)}, u32[]{:S(2)}, u32[]{:S(2)}) collective-permute-start(bf16[2,5,96,384]{3,2,1,0:T(8,128)(2,1)} %collective-permute-done.11.refs_4_), channel_id=1, source_target_pairs={{0,28},{1,29},{2,30},{3,31},{4,0},{5,1},{6,2},{7,3},{8,4},{9,5},{1... | collective-permute-start | bytes 2211848 | tf_op jit(solution)/shard_map/ppermute | solution.py:22
  76.0 8.0 %shard_map.106 = (bf16[5,1024,768]{2,1,0:T(8,128)(2,1)}, bf16[5,1024,256]{2,1,0:T(8,128)(2,1)}) custom-call(s32[7]{0:T(128)} %pad_add_fusion.place_ref, bf16[256,1536]{1,0:T(8,128)(2,1)} %refs_0_, bf16[256,1536]{1,0:T(8,128)(2,1)} %copy-done.13, bf16[256,768]{1,0:T(8,128)(2,1)} %copy-done.12, bf16[256,768]{1,0:T(8,128)(2,1)} %copy-done.16, ...), custom_call_target="tpu_custom_call" | custom-call | flops 1048576 | bytes 1048576 | tf_op jit(solution)/shard_map/pallas_call | solution.py:76
  84.0 5.4 %collective-permute-done.16.f_ref.refs_5_ = bf16[2,5,96,384]{3,2,1,0:T(8,128)(2,1)S(1)} collective-permute-done((bf16[2,5,96,384]{3,2,1,0:T(8,128)(2,1)}, bf16[2,5,96,384]{3,2,1,0:T(8,128)(2,1)S(1)}, u32[]{:S(2)}, u32[]{:S(2)}) %collective-permute-start.16) | collective-permute-done | bytes 737312 | tf_op jit(solution)/shard_map/ppermute | solution.py:22
  89.4 2.0 %shard_map.107 = (bf16[1,5,96,384]{3,2,1,0:T(8,128)(2,1)}, bf16[1,5,96,384]{3,2,1,0:T(8,128)(2,1)S(1)}) custom-call(bf16[2,5,96,384]{3,2,1,0:T(8,128)(2,1)S(1)} %collective-permute-done.16.f_ref.refs_5_, bf16[2,5,96,384]{3,2,1,0:T(8,128)(2,1)} %collective-permute-done.17.b_ref.refs_6_), custom_call_target="tpu_custom_call" | custom-call | tf_op jit(solution)/shard_map/pallas_call | solution.py:268
  91.4 2.0 %collective-permute-start.22 = (bf16[1,5,96,384]{3,2,1,0:T(8,128)(2,1)}, bf16[1,5,96,384]{3,2,1,0:T(8,128)(2,1)}, u32[]{:S(2)}, u32[]{:S(2)}) collective-permute-start(bf16[1,5,96,384]{3,2,1,0:T(8,128)(2,1)} %get-tuple-element.86), channel_id=1, source_target_pairs={{0,4},{1,5},{2,6},{3,7},{4,8},{5,9},{6,10},{7,11},{8,12},{9,13},{1... | collective-permute-start | bytes 1105928 | tf_op jit(solution)/shard_map/ppermute | solution.py:22
  94.7 13.6 %shard_map.108.acc_ref = f32[1024,768]{1,0:T(8,128)} custom-call(s32[7]{0:T(128)} %pad_add_fusion.place_ref, f32[5]{0:T(128)} %get-tuple-element.98.gs_ref, f32[5]{0:T(128)} %get-tuple-element.99.us_ref, bf16[5,1024,768]{2,1,0:T(8,128)(2,1)} %get-tuple-element.88.x_ref, bf16[2,5,96,384]{3,2,1,0:T(8,128)(2,1)} %bitcast.14, ...), custom_call_target="tpu_custom_call" | custom-call | flops 1048576 | bytes 1048576 | tf_op jit(solution)/shard_map/pallas_call | solution.py:115
  108.3 4.2 %shard_map.110 = (bf16[256,384]{1,0:T(8,128)(2,1)}, bf16[256,384]{1,0:T(8,128)(2,1)}) custom-call(s32[7]{0:T(128)} %pad_add_fusion.place_ref, f32[5]{0:T(128)} %get-tuple-element.98.gs_ref, f32[5]{0:T(128)} %get-tuple-element.99.us_ref, bf16[1,5,96,384]{3,2,1,0:T(8,128)(2,1)} %collective-permute-done.22.g_ref, ...), custom_call_target="tpu_custom_call" | custom-call | flops 1006632960 | bytes 4194304 | tf_op jit(solution)/shard_map/pallas_call | solution.py:157
  112.5 3.3 %collective-permute-start.26 = (bf16[256,384]{1,0:T(8,128)(2,1)}, bf16[256,384]{1,0:T(8,128)(2,1)S(1)}, u32[]{:S(2)}, u32[]{:S(2)}) collective-permute-start(bf16[256,384]{1,0:T(8,128)(2,1)} %get-tuple-element.93), channel_id=1, source_target_pairs={{0,3},{1,2},{2,1},{3,0},{4,7},{5,6},{6,5},{7,4},{8,11},{9,10},{10,... | collective-permute-start | bytes 589832 | tf_op jit(solution)/shard_map/ppermute | solution.py:17
  115.8 4.2 %shard_map.109 = (bf16[256,384]{1,0:T(8,128)(2,1)}, bf16[256,384]{1,0:T(8,128)(2,1)}) custom-call(s32[7]{0:T(128)} %pad_add_fusion.place_ref, f32[5]{0:T(128)} %get-tuple-element.98.gs_ref, f32[5]{0:T(128)} %get-tuple-element.99.us_ref, bf16[1,5,96,384]{3,2,1,0:T(8,128)(2,1)} %collective-permute-done.22.g_ref, ...), custom_call_target="tpu_custom_call" | custom-call | flops 1006632960 | bytes 4194304 | tf_op jit(solution)/shard_map/pallas_call | solution.py:157
  120.0 3.6 %collective-permute-done.26.refs_3_ = bf16[256,384]{1,0:T(8,128)(2,1)S(1)} collective-permute-done((bf16[256,384]{1,0:T(8,128)(2,1)}, bf16[256,384]{1,0:T(8,128)(2,1)S(1)}, u32[]{:S(2)}, u32[]{:S(2)}) %collective-permute-start.26) | collective-permute-done | bytes 196640 | tf_op jit(solution)/shard_map/ppermute | solution.py:17
  123.6 1.7 %copy-done.3 = bf16[1536,768]{1,0:T(8,128)(2,1)S(1)} copy-done((bf16[1536,768]{1,0:T(8,128)(2,1)S(1)}, bf16[1536,768]{1,0:T(8,128)(2,1)}, u32[]{:S(2)}) %copy-start.3) | copy-done | bytes 2359320
  127.7 15.5 %all_to_all.10 = bf16[8,32,768]{2,1,0:T(8,128)(2,1)S(1)} all-to-all(bf16[8,32,768]{2,1,0:T(8,128)(2,1)S(1)} %bitcast.15), channel_id=1, replica_groups=mesh['feat'=8,'tok'=32] {'feat'}, dimensions={0} | all-to-all | bytes 786432 | tf_op jit(solution)/shard_map/all_to_all | solution.py:297
  143.3 11.7 %all_to_all.11 = bf16[8,32,768]{2,1,0:T(8,128)(2,1)S(1)} all-to-all(bf16[8,32,768]{2,1,0:T(8,128)(2,1)S(1)} %broadcast_in_dim.27), channel_id=1, replica_groups=mesh['feat'=8,'tok'=32] {'feat'}, dimensions={0} | all-to-all | bytes 786432 | tf_op jit(solution)/shard_map/all_to_all | solution.py:299
  (99 shorter events, 29.2 us)
Async XLA Ops:
  3.5 8.4 %collective-permute-start = (bf16[2,5,24,384]{3,2,1,0:T(8,128)(2,1)}, bf16[2,5,24,384]{3,2,1,0:T(8,128)(2,1)S(1)}, u32[]{:S(2)}, u32[]{:S(2)}) collective-permute-start(bf16[2,5,24,384]{3,2,1,0:T(8,128)(2,1)} %get-tuple-element.50), channel_id=1, source_target_pairs={{0,1},{1,0},{2,3},{3,2},{4,5},{5,4},{6,7},{7,6},{8,9},{9,8},{10,11... | collective-permute-start | bytes 552968 | tf_op jit(solution)/shard_map/ppermute | solution.py:17
  6.8 6.3 %collective-permute-start.1 = (bf16[2,5,24,384]{3,2,1,0:T(8,128)(2,1)S(1)}, bf16[2,5,24,384]{3,2,1,0:T(8,128)(2,1)S(1)}, u32[]{:S(2)}, u32[]{:S(2)}) collective-permute-start(bf16[2,5,24,384]{3,2,1,0:T(8,128)(2,1)S(1)} %get-tuple-element.51), channel_id=1, source_target_pairs={{0,2},{1,3},{2,0},{3,1},{4,6},{5,7},{6,4},{7,5},{8,10},{9,11},{10,... | collective-permute-start | bytes 552968 | tf_op jit(solution)/shard_map/ppermute | solution.py:17
  6.8 10.6 %collective-permute-start.2 = (bf16[2,5,24,384]{3,2,1,0:T(8,128)(2,1)S(1)}, bf16[2,5,24,384]{3,2,1,0:T(8,128)(2,1)S(1)}, u32[]{:S(2)}, u32[]{:S(2)}) collective-permute-start(bf16[2,5,24,384]{3,2,1,0:T(8,128)(2,1)S(1)} %get-tuple-element.52), channel_id=1, source_target_pairs={{0,3},{1,2},{2,1},{3,0},{4,7},{5,6},{6,5},{7,4},{8,11},{9,10},{10,... | collective-permute-start | bytes 552968 | tf_op jit(solution)/shard_map/ppermute | solution.py:17
  9.6 15.5 %collective-permute-start.6 = (bf16[256,768]{1,0:T(8,128)(2,1)S(1)}, bf16[256,768]{1,0:T(8,128)(2,1)S(1)}, u32[]{:S(2)}, u32[]{:S(2)}) collective-permute-start(bf16[256,768]{1,0:T(8,128)(2,1)S(1)} %get-tuple-element.62), channel_id=1, source_target_pairs={{0,64},{32,96},{64,0},{96,32},{128,192},{160,224},{192,128},{224,1... | collective-permute-start | bytes 1179656 | tf_op jit(solution)/shard_map/ppermute | solution.py:17
  9.7 19.6 %collective-permute-start.7 = (bf16[256,768]{1,0:T(8,128)(2,1)S(1)}, bf16[256,768]{1,0:T(8,128)(2,1)S(1)}, u32[]{:S(2)}, u32[]{:S(2)}) collective-permute-start(bf16[256,768]{1,0:T(8,128)(2,1)S(1)} %get-tuple-element.62), channel_id=1, source_target_pairs={{0,128},{32,160},{64,192},{96,224},{128,0},{160,32},{192,64},{224,... | collective-permute-start | bytes 1179656 | tf_op jit(solution)/shard_map/ppermute | solution.py:17
  20.0 10.8 %collective-permute-start.5 = (bf16[256,768]{1,0:T(8,128)(2,1)S(1)}, bf16[256,768]{1,0:T(8,128)(2,1)S(1)}, u32[]{:S(2)}, u32[]{:S(2)}) collective-permute-start(bf16[256,768]{1,0:T(8,128)(2,1)S(1)} %get-tuple-element.54), channel_id=1, source_target_pairs={{0,2},{1,3},{2,0},{3,1},{4,6},{5,7},{6,4},{7,5},{8,10},{9,11},{10,... | collective-permute-start | bytes 1179656 | tf_op jit(solution)/shard_map/ppermute | solution.py:17
  20.1 21.7 %collective-permute-start.3 = (bf16[2,5,96,384]{3,2,1,0:T(8,128)(2,1)S(1)}, bf16[2,5,96,384]{3,2,1,0:T(8,128)(2,1)S(1)}, u32[]{:S(2)}, u32[]{:S(2)}) collective-permute-start(bf16[2,5,96,384]{3,2,1,0:T(8,128)(2,1)S(1)} %bitcast.12), channel_id=1, source_target_pairs={{0,4},{1,5},{2,6},{3,7},{4,8},{5,9},{6,10},{7,11},{8,12},{9,13},{1... | collective-permute-start | bytes 2211848 | tf_op jit(solution)/shard_map/ppermute | solution.py:22
  21.2 20.6 %collective-permute-start.4 = (bf16[2,5,96,384]{3,2,1,0:T(8,128)(2,1)S(1)}, bf16[2,5,96,384]{3,2,1,0:T(8,128)(2,1)S(1)}, u32[]{:S(2)}, u32[]{:S(2)}) collective-permute-start(bf16[2,5,96,384]{3,2,1,0:T(8,128)(2,1)S(1)} %bitcast.13), channel_id=1, source_target_pairs={{0,28},{1,29},{2,30},{3,31},{4,0},{5,1},{6,2},{7,3},{8,4},{9,5},{1... | collective-permute-start | bytes 2211848 | tf_op jit(solution)/shard_map/ppermute | solution.py:22
  30.8 11.0 %collective-permute-start.8 = (bf16[256,768]{1,0:T(8,128)(2,1)S(1)}, bf16[256,768]{1,0:T(8,128)(2,1)S(1)}, u32[]{:S(2)}, u32[]{:S(2)}) collective-permute-start(bf16[256,768]{1,0:T(8,128)(2,1)S(1)} %get-tuple-element.62), channel_id=1, source_target_pairs={{0,2},{1,3},{2,0},{3,1},{4,6},{5,7},{6,4},{7,5},{8,10},{9,11},{10,... | collective-permute-start | bytes 1179656 | tf_op jit(solution)/shard_map/ppermute | solution.py:17
  30.8 11.0 %collective-permute-start.9 = (bf16[256,768]{1,0:T(8,128)(2,1)S(1)}, bf16[256,768]{1,0:T(8,128)(2,1)S(1)}, u32[]{:S(2)}, u32[]{:S(2)}) collective-permute-start(bf16[256,768]{1,0:T(8,128)(2,1)S(1)} %collective-permute-done.5.refs_2_), channel_id=1, source_target_pairs={{0,64},{32,96},{64,0},{96,32},{128,192},{160,224},{192,128},{224,1... | collective-permute-start | bytes 1179656 | tf_op jit(solution)/shard_map/ppermute | solution.py:17
  41.8 11.1 %collective-permute-start.14 = (bf16[256,1536]{1,0:T(8,128)(2,1)S(1)}, bf16[256,1536]{1,0:T(8,128)(2,1)S(1)}, u32[]{:S(2)}, u32[]{:S(2)}) collective-permute-start(bf16[256,1536]{1,0:T(8,128)(2,1)S(1)} %copy-done.11), channel_id=1, source_target_pairs={{0,1},{1,0},{2,3},{3,2},{4,5},{5,4},{6,7},{7,6},{8,9},{9,8},{10,11... | collective-permute-start | bytes 2359304 | tf_op jit(solution)/shard_map/ppermute | solution.py:17
  42.8 24.3 %collective-permute-start.12 = (bf16[512,768]{1,0:T(8,128)(2,1)S(1)}, bf16[512,768]{1,0:T(8,128)(2,1)}, u32[]{:S(2)}, u32[]{:S(2)}) collective-permute-start(bf16[512,768]{1,0:T(8,128)(2,1)S(1)} %pad_maximum_fusion), channel_id=1, source_target_pairs={{0,32},{32,0},{64,96},{96,64},{128,160},{160,128},{192,224},{224,1... | collective-permute-start | bytes 2359304 | tf_op jit(solution)/shard_map/ppermute | solution.py:17
  45.3 21.7 %collective-permute-start.10 = (bf16[2,5,96,384]{3,2,1,0:T(8,128)(2,1)S(1)}, bf16[2,5,96,384]{3,2,1,0:T(8,128)(2,1)}, u32[]{:S(2)}, u32[]{:S(2)}) collective-permute-start(bf16[2,5,96,384]{3,2,1,0:T(8,128)(2,1)S(1)} %collective-permute-done.3.refs_1_), channel_id=1, source_target_pairs={{0,4},{1,5},{2,6},{3,7},{4,8},{5,9},{6,10},{7,11},{8,12},{9,13},{1... | collective-permute-start | bytes 2211848 | tf_op jit(solution)/shard_map/ppermute | solution.py:22
  46.3 20.7 %collective-permute-start.11 = (bf16[2,5,96,384]{3,2,1,0:T(8,128)(2,1)S(1)}, bf16[2,5,96,384]{3,2,1,0:T(8,128)(2,1)}, u32[]{:S(2)}, u32[]{:S(2)}) collective-permute-start(bf16[2,5,96,384]{3,2,1,0:T(8,128)(2,1)S(1)} %collective-permute-done.4.refs_2_), channel_id=1, source_target_pairs={{0,28},{1,29},{2,30},{3,31},{4,0},{5,1},{6,2},{7,3},{8,4},{9,5},{1... | collective-permute-start | bytes 2211848 | tf_op jit(solution)/shard_map/ppermute | solution.py:22
  50.3 11.7 %collective-permute-start.13 = (bf16[256,768]{1,0:T(8,128)(2,1)S(1)}, bf16[256,768]{1,0:T(8,128)(2,1)S(1)}, u32[]{:S(2)}, u32[]{:S(2)}) collective-permute-start(bf16[256,768]{1,0:T(8,128)(2,1)S(1)} %collective-permute-done.5.refs_2_), channel_id=1, source_target_pairs={{0,128},{32,160},{64,192},{96,224},{128,0},{160,32},{192,64},{224,... | collective-permute-start | bytes 1179656 | tf_op jit(solution)/shard_map/ppermute | solution.py:17
  52.9 14.1 %collective-permute-start.15 = (bf16[256,768]{1,0:T(8,128)(2,1)S(1)}, bf16[256,768]{1,0:T(8,128)(2,1)S(1)}, u32[]{:S(2)}, u32[]{:S(2)}) collective-permute-start(bf16[256,768]{1,0:T(8,128)(2,1)S(1)} %collective-permute-done.8.refs_3_), channel_id=1, source_target_pairs={{0,1},{1,0},{2,3},{3,2},{4,5},{5,4},{6,7},{7,6},{8,9},{9,8},{10,11... | collective-permute-start | bytes 1179656 | tf_op jit(solution)/shard_map/ppermute | solution.py:17
  67.1 5.9 %collective-permute-start.18 = (bf16[512,768]{1,0:T(8,128)(2,1)}, bf16[512,768]{1,0:T(8,128)(2,1)}, u32[]{:S(2)}, u32[]{:S(2)}) collective-permute-start(bf16[512,768]{1,0:T(8,128)(2,1)} %pad_maximum_fusion.1.refs_7_), channel_id=1, source_target_pairs={{0,1},{1,0},{2,3},{3,2},{4,5},{5,4},{6,7},{7,6},{8,9},{9,8},{10,11... | collective-permute-start | bytes 2359304 | tf_op jit(solution)/shard_map/ppermute | solution.py:17
  69.5 5.2 %collective-permute-start.21 = (bf16[512,768]{1,0:T(8,128)(2,1)}, bf16[512,768]{1,0:T(8,128)(2,1)}, u32[]{:S(2)}, u32[]{:S(2)}) collective-permute-start(bf16[512,768]{1,0:T(8,128)(2,1)} %constant_dynamic-update-slice_fusion.refs_8_), channel_id=1, source_target_pairs={{0,1},{1,0},{2,3},{3,2},{4,5},{5,4},{6,7},{7,6},{8,9},{9,8},{10,11... | collective-permute-start | bytes 2359304 | tf_op jit(solution)/shard_map/ppermute | solution.py:17
  70.1 19.2 %collective-permute-start.16 = (bf16[2,5,96,384]{3,2,1,0:T(8,128)(2,1)}, bf16[2,5,96,384]{3,2,1,0:T(8,128)(2,1)S(1)}, u32[]{:S(2)}, u32[]{:S(2)}) collective-permute-start(bf16[2,5,96,384]{3,2,1,0:T(8,128)(2,1)} %collective-permute-done.10.refs_3_), channel_id=1, source_target_pairs={{0,4},{1,5},{2,6},{3,7},{4,8},{5,9},{6,10},{7,11},{8,12},{9,13},{1... | collective-permute-start | bytes 2211848 | tf_op jit(solution)/shard_map/ppermute | solution.py:22
  70.1 19.2 %collective-permute-start.17 = (bf16[2,5,96,384]{3,2,1,0:T(8,128)(2,1)}, bf16[2,5,96,384]{3,2,1,0:T(8,128)(2,1)}, u32[]{:S(2)}, u32[]{:S(2)}) collective-permute-start(bf16[2,5,96,384]{3,2,1,0:T(8,128)(2,1)} %collective-permute-done.11.refs_4_), channel_id=1, source_target_pairs={{0,28},{1,29},{2,30},{3,31},{4,0},{5,1},{6,2},{7,3},{8,4},{9,5},{1... | collective-permute-start | bytes 2211848 | tf_op jit(solution)/shard_map/ppermute | solution.py:22
  91.4 16.9 %collective-permute-start.22 = (bf16[1,5,96,384]{3,2,1,0:T(8,128)(2,1)}, bf16[1,5,96,384]{3,2,1,0:T(8,128)(2,1)}, u32[]{:S(2)}, u32[]{:S(2)}) collective-permute-start(bf16[1,5,96,384]{3,2,1,0:T(8,128)(2,1)} %get-tuple-element.86), channel_id=1, source_target_pairs={{0,4},{1,5},{2,6},{3,7},{4,8},{5,9},{6,10},{7,11},{8,12},{9,13},{1... | collective-permute-start | bytes 1105928 | tf_op jit(solution)/shard_map/ppermute | solution.py:22
  93.4 14.9 %collective-permute-start.23 = (bf16[1,5,96,384]{3,2,1,0:T(8,128)(2,1)S(1)}, bf16[1,5,96,384]{3,2,1,0:T(8,128)(2,1)}, u32[]{:S(2)}, u32[]{:S(2)}) collective-permute-start(bf16[1,5,96,384]{3,2,1,0:T(8,128)(2,1)S(1)} %get-tuple-element.87), channel_id=1, source_target_pairs={{0,28},{1,29},{2,30},{3,31},{4,0},{5,1},{6,2},{7,3},{8,4},{9,5},{1... | collective-permute-start | bytes 1105928 | tf_op jit(solution)/shard_map/ppermute | solution.py:22
  112.5 7.5 %collective-permute-start.25 = (bf16[256,384]{1,0:T(8,128)(2,1)}, bf16[256,384]{1,0:T(8,128)(2,1)S(1)}, u32[]{:S(2)}, u32[]{:S(2)}) collective-permute-start(bf16[256,384]{1,0:T(8,128)(2,1)} %get-tuple-element.92), channel_id=1, source_target_pairs={{0,2},{1,3},{2,0},{3,1},{4,6},{5,7},{6,4},{7,5},{8,10},{9,11},{10,... | collective-permute-start | bytes 589832 | tf_op jit(solution)/shard_map/ppermute | solution.py:17
  112.5 11.0 %collective-permute-start.26 = (bf16[256,384]{1,0:T(8,128)(2,1)}, bf16[256,384]{1,0:T(8,128)(2,1)S(1)}, u32[]{:S(2)}, u32[]{:S(2)}) collective-permute-start(bf16[256,384]{1,0:T(8,128)(2,1)} %get-tuple-element.93), channel_id=1, source_target_pairs={{0,3},{1,2},{2,1},{3,0},{4,7},{5,6},{6,5},{7,4},{8,11},{9,10},{10,... | collective-permute-start | bytes 589832 | tf_op jit(solution)/shard_map/ppermute | solution.py:17
  (26 other events, 552.7 us)

commit v5 on v4

--- a/solution.py
+++ b/solution.py
@@ -7,9 +7,11 @@
 from jax.sharding import PartitionSpec as P
 
 GROUP = 4
+ANY = pl.BlockSpec(memory_space=pl.ANY)
 SMEM = pl.BlockSpec(memory_space=pltpu.SMEM)
 VMEM = pl.BlockSpec(memory_space=pltpu.VMEM)
-VMEM_BYTES = 60 * 2**20
+VMEM_BYTES = 44 * 2**20
+LAY_BYTES = 60 * 2**20
 SMALL_BYTES = 16 * 2**20
 
 
@@ -57,9 +59,16 @@
     return row, jnp.minimum(row // 128 * 128, blk - window)
 
 
-def lay_kernel(place_ref, *refs, z_count, share):
-    own_refs, partner_refs, x_ref, windows = refs[:6], refs[6:12], refs[12], refs[13]
+def ring_row(i, z, z_count, share):
+    origin = z - (i + 1) // 2 if i % 2 else z + i // 2
+    return pl.ds(pl.multiple_of((origin + z_count) % z_count * share, 16), share)
+
+
+def lay_kernel(place_ref, *refs, z_count, n_w):
+    w_refs, own_refs, partner_refs = refs[:n_w], refs[n_w : n_w + 6], refs[n_w + 6 : n_w + 12]
+    x_ref, windows, w_out = refs[n_w + 12 :]
     x_lo, z = place_ref[5], place_ref[6]
+    share, width = w_refs[0].shape[2:]
     rows, (blk, window) = own_refs[0].shape[0], (x_ref.shape[2], windows.shape[2])
     _, start = last_window(z, z_count, share, blk, window)
     for j in range(5):
@@ -67,65 +76,74 @@
             at = pl.ds(m * rows, rows)
             x_ref[j, at] = block_of_rows(own_refs, partner_refs, j, m, x_lo, 0, blk)
             windows[j, at] = block_of_rows(own_refs, partner_refs, j, m, x_lo, start, window)
-
-
-def lay(place, own_rows, partner_rows, share):
+        for i in range(z_count):
+            at = ring_row(i, z, z_count, share)
+            for side in range(2):
+                piece = w_refs[i][side, place_ref[j]] if i < n_w else jnp.zeros((share, width), w_out.dtype)
+                w_out[j, at, side * width : (side + 1) * width] = piece
+
+
+def lay(place, weights, own_rows, partner_rows):
     rows, features = own_rows[0].shape
     blk = features // 2
+    share, width = weights[0].shape[2:]
     window = min(2 * 128 * ((share + 127) // 128), blk)
+    shapes = [(5, 4 * rows, blk), (5, 4 * rows, window), (5, blk, 2 * width)]
     return pl.pallas_call(
-        functools.partial(lay_kernel, z_count=blk // share, share=share),
-        out_shape=[jax.ShapeDtypeStruct((5, 4 * rows, w), jnp.bfloat16) for w in (blk, window)],
-        in_specs=[SMEM] + [VMEM] * 12,
-        out_specs=[VMEM] * 2,
-        compiler_params=pltpu.CompilerParams(vmem_limit_bytes=VMEM_BYTES),
+        functools.partial(lay_kernel, z_count=blk // share, n_w=len(weights)),
+        out_shape=[jax.ShapeDtypeStruct(shape, jnp.bfloat16) for shape in shapes],
+        in_specs=[SMEM] + [VMEM] * (len(weights) + 12),
+        out_specs=[VMEM] * 3,
+        compiler_params=pltpu.CompilerParams(vmem_limit_bytes=LAY_BYTES),
         cost_estimate=pl.CostEstimate(flops=2**20, bytes_accessed=2**20, transcendentals=0),
-    )(place, *own_rows, *partner_rows)
-
-
-def early_kernel(place_ref, gs_ref, us_ref, x_ref, *refs, z_count):
-    w_refs, acc, w_mem = refs[: z_count - 1], refs[z_count - 1], refs[z_count]
-    j = pl.program_id(0)
-    z, slot = place_ref[6], place_ref[j]
-    blk, both = w_mem.shape
+    )(place, *weights, *own_rows, *partner_rows)
+
+
+def early_kernel(place_ref, gs_ref, us_ref, x_ref, w_ref, below_ref, above_ref, acc, x_mem, w_mem, x_sem, w_sem, *, z_count):
+    z = place_ref[6]
+    blk, both = w_mem.shape[1:]
     share, width = blk // z_count, both // 2
-    w_mem[pl.ds(pl.multiple_of((z + z_count // 2) % z_count * share, 16), share)] = jnp.zeros((share, both), w_mem.dtype)
-    for i, ref in enumerate(w_refs):
-        origin = z - (i + 1) // 2 if i % 2 else z + i // 2
-        at = pl.ds(pl.multiple_of((origin + z_count) % z_count * share, 16), share)
-        for side in range(2):
-            w_mem[at, side * width : (side + 1) * width] = ref[side, 0]
-    term = jnp.dot(x_ref[0], w_mem[...], preferred_element_type=jnp.float32)
-    g, u = term[:, :width] * gs_ref[slot], term[:, width:] * us_ref[slot]
-
-    @pl.when(j == 0)
-    def _():
-        acc[:, :width] = g
-        acc[:, width:] = u
-
-    @pl.when(j > 0)
-    def _():
-        acc[:, :width] += g
-        acc[:, width:] += u
-
-
-def early(place, gs, us, weights, x):
+    copies = []
+    for j in range(5):
+        copies.append(pltpu.make_async_copy(w_ref.at[j], w_mem.at[j], w_sem.at[j]))
+        copies.append(pltpu.make_async_copy(x_ref.at[j], x_mem.at[j], x_sem.at[j]))
+    for copy in copies:
+        copy.start()
+    for j in range(5):
+        slot = place_ref[j]
+        copies[2 * j].wait()
+        for i, ref in ((z_count - 3, below_ref), (z_count - 2, above_ref)):
+            at = ring_row(i, z, z_count, share)
+            for side in range(2):
+                w_mem[j, at, side * width : (side + 1) * width] = ref[side, slot]
+        copies[2 * j + 1].wait()
+        term = jnp.dot(x_mem[j], w_mem[j], preferred_element_type=jnp.float32)
+        g, u = term[:, :width] * gs_ref[slot], term[:, width:] * us_ref[slot]
+        if j == 0:
+            acc[:, :width] = g
+            acc[:, width:] = u
+        else:
+            acc[:, :width] += g
+            acc[:, width:] += u
+
+
+def early(place, gs, us, x, weights, below, above):
     slots, rows, blk = x.shape
-    share, width = weights[0].shape[2:]
+    share, width = below.shape[2:]
     return pl.pallas_call(
         functools.partial(early_kernel, z_count=blk // share),
         out_shape=jax.ShapeDtypeStruct((rows, 2 * width), jnp.float32),
-        grid_spec=pltpu.PrefetchScalarGridSpec(
-            num_scalar_prefetch=3,
-            grid=(slots,),
-            in_specs=[pl.BlockSpec((1, rows, blk), lambda j, place, *_: (j, 0, 0))]
-            + [pl.BlockSpec((2, 1, share, width), lambda j, place, *_: (0, place[j], 0, 0))] * len(weights),
-            out_specs=pl.BlockSpec((rows, 2 * width), lambda j, *_: (0, 0)),
-            scratch_shapes=[pltpu.VMEM((blk, 2 * width), jnp.bfloat16)],
-        ),
+        in_specs=[SMEM] * 3 + [ANY] * 2 + [VMEM] * 2,
+        out_specs=VMEM,
+        scratch_shapes=[
+            pltpu.VMEM(x.shape, jnp.bfloat16),
+            pltpu.VMEM(weights.shape, jnp.bfloat16),
+            pltpu.SemaphoreType.DMA((slots,)),
+            pltpu.SemaphoreType.DMA((slots,)),
+        ],
         compiler_params=pltpu.CompilerParams(vmem_limit_bytes=VMEM_BYTES),
         cost_estimate=pl.CostEstimate(flops=2**20, bytes_accessed=2**20, transcendentals=0),
-    )(place, gs, us, x, *weights)
+    )(place, gs, us, x, weights, below, above)
 
 
 def late_kernel(place_ref, gs_ref, us_ref, g_ref, u_ref, acc_ref, window_ref, near_ref, far_ref, w_mem, acc, *, z_count):
@@ -177,16 +195,21 @@
 
 
 def latent_kernel(own_ref, lin_ref, *refs):
-    pieces, hidden_ref, part_ref = refs[:4], refs[4], refs[5]
-    width = pieces[0].shape[1]
-    total = None
+    pieces, hidden_ref, part_ref, total = refs[:4], refs[4], refs[5], refs[6]
+    step = pl.program_id(0)
     for m in range(4):
-        at = pl.ds(pl.multiple_of((own_ref[0] ^ m) * width, width), width)
-        piece = pieces[m][...]
-        hidden_ref[:, at] = piece
-        term = jnp.dot(piece, lin_ref[at], preferred_element_type=jnp.float32)
-        total = term if total is None else total + term
-    part_ref[...] = total.astype(jnp.bfloat16)
+
+        @pl.when(step == m)
+        def _(m=m):
+            piece = pieces[m][...]
+            hidden_ref[...] = piece
+            term = jnp.dot(piece, lin_ref[...], preferred_element_type=jnp.float32)
+            if m > 0:
+                term += total[...]
+            if m < 3:
+                total[...] = term
+            else:
+                part_ref[...] = term.astype(jnp.bfloat16)
 
 
 def per_device(tokens, gate_weight, up_weight, gate_scale, up_scale, partners, latent_in, latent_out):
@@ -212,7 +235,7 @@
         out_shape=[jax.ShapeDtypeStruct((2, slots, share, half), jnp.bfloat16)] * 4,
         in_specs=[SMEM, VMEM, VMEM],
         out_specs=[VMEM] * 4,
-        compiler_params=pltpu.CompilerParams(vmem_limit_bytes=SMALL_BYTES),
+        compiler_params=pltpu.CompilerParams(vmem_limit_bytes=LAY_BYTES),
     )(own, gate_weight, up_weight)
 
     def place(got):
@@ -222,7 +245,7 @@
             out_shape=jax.ShapeDtypeStruct(shape[:2] + (4,) + shape[2:], jnp.bfloat16),
             in_specs=[SMEM] + [VMEM] * 4,
             out_specs=VMEM,
-            compiler_params=pltpu.CompilerParams(vmem_limit_bytes=SMALL_BYTES),
+            compiler_params=pltpu.CompilerParams(vmem_limit_bytes=LAY_BYTES),
         )(own, *got)
         return out.reshape(shape[:2] + (4 * shape[2],) + shape[3:])
 
@@ -262,8 +285,8 @@
     s3_own = swapped(s2_own, "tok", 1)
     partner_rows = [p_x, p_y1, p_y2, swapped(p_x, "tok", 1), q_y1, swapped(p_y2, "tok", 1)]
     own_rows = [later, s1, s2_own, s2_other, s3_own, s3_other]
-    x, windows = lay(here, own_rows, partner_rows, w0.shape[2])
-    w3, x, windows = barrier((w3, x, windows))
+    x, windows, w_laid = lay(here, (w0, *w1, *w2), own_rows, partner_rows)
+    w3, x, windows, w_laid = barrier((w3, x, windows, w_laid))
     half_shape = (1,) + w3[0].shape[1:]
     cut = pl.pallas_call(
         halves_kernel,
@@ -275,22 +298,32 @@
     )(*w3)
     w4 = step(*cut)
 
-    acc = early(here, gs, us, (w0, *w1, *w2, *w3), x)
+    acc = early(here, gs, us, x, w_laid, *w3)
     z_count = lax.axis_size("tok") // GROUP
     made = late(here, gs, us, w4, acc, windows, z_count, 1)
     far_hidden = [swapped(v, "tok", mask) for v, mask in zip(made, (2, 3))]
     made = late(here, gs, us, w4, acc, windows, z_count, 0)
     hidden_pieces = [made[0], swapped(made[1], "tok", 1), *far_hidden]
+    rank = latent_in.shape[1]
     hidden, part = pl.pallas_call(
         latent_kernel,
         out_shape=(
             jax.ShapeDtypeStruct((rows, features), jnp.bfloat16),
-            jax.ShapeDtypeStruct((rows, latent_in.shape[1]), jnp.bfloat16),
+            jax.ShapeDtypeStruct((rows, rank), jnp.bfloat16),
         ),
-        in_specs=[SMEM] + [VMEM] * 5,
-        out_specs=(VMEM, VMEM),
-        compiler_params=pltpu.CompilerParams(vmem_limit_bytes=SMALL_BYTES),
-        cost_estimate=pl.CostEstimate(flops=2 * rows * features * latent_in.shape[1], bytes_accessed=4 * 2**20, transcendentals=0),
+        grid_spec=pltpu.PrefetchScalarGridSpec(
+            num_scalar_prefetch=1,
+            grid=(4,),
+            in_specs=[pl.BlockSpec((half, rank), lambda m, own: (own[0] ^ m, 0))]
+            + [pl.BlockSpec((rows, half), lambda m, own: (0, 0))] * 4,
+            out_specs=[
+                pl.BlockSpec((rows, half), lambda m, own: (0, own[0] ^ m)),
+                pl.BlockSpec((rows, rank), lambda m, own: (0, 0)),
+            ],
+            scratch_shapes=[pltpu.VMEM((rows, rank), jnp.float32)],
+        ),
+        compiler_params=pltpu.CompilerParams(vmem_limit_bytes=VMEM_BYTES),
+        cost_estimate=pl.CostEstimate(flops=2 * rows * features * rank, bytes_accessed=4 * 2**20, transcendentals=0),
     )(own, latent_in, *hidden_pieces)
 
     parts = part.reshape(feat_count, rows // feat_count, -1)

time: 157 us -> 152 us (0.968)
  local copies, waits for them, and re-layouts: 12.3 us -> 5.54 us
  Pallas kernels: 34.4 us -> 36.4 us
    unnamed x47 -> x37, local copies, waits for them, and re-layouts: 9.46 us -> 2.63 us
    pallas_call x2, Pallas kernels: 8.4 us -> 5.09 us  [late(): pl.pallas_call(functools.partial(late_kernel, z_count=z_count), out_shape...]
    ppermute x8, waiting for transfers between devices: 20.6 us -> 17.8 us  [shifted(): lax.ppermute(value, 'tok', [(i, (i + step * GROUP) % count) for i in rang...]
    pallas_call x1, Pallas kernels: 7.95 us -> 10.6 us  [lay(): pl.pallas_call(functools.partial(lay_kernel, z_count=blk // share, n_w=le...]
    pallas_call x1, Pallas kernels: 0.07 us -> 2.14 us  [place(): pl.pallas_call(place_kernel, out_shape=jax.ShapeDtypeStruct(shape[:2] + (...]
    ppermute x19, waiting for transfers between devices: 21.9 us -> 23.6 us  [swapped(): lax.ppermute(value, axis, [(i, i ^ mask) for i in range(lax.axis_size(axi...]
    pallas_call x1, Pallas kernels: 13.6 us -> 12 us  [early(): pl.pallas_call(functools.partial(early_kernel, z_count=blk // share), out...]
  transfers between devices with their start and end apart: 27 -> 27, of which waited for: 10 -> 10; matrix products, arithmetic and copies ran while one was open for 3% -> 5% of each run, Pallas kernels for 16% -> 18%
where the time goes in v5:
time: 152 us; the launch traced here: 151 us
  waiting for transfers between devices  41.4 us (27%)
  Pallas kernels  36.4 us (24%)
  starting transfers between devices  36 us (24%)
  blocking collectives  26.4 us (17%)
  local copies, waits for them, and re-layouts  5.54 us (4%)
  other arithmetic  2.81 us (2%)
  matrix products  1.66 us (1%)
    ppermute x19, waiting for transfers between devices, swapped(): lax.ppermute(value, axis, [(i, i ^ mask) for i in range(lax.axis_size(axi...  23.6 us
    ppermute x19, starting transfers between devices, swapped(): lax.ppermute(value, axis, [(i, i ^ mask) for i in range(lax.axis_size(axi...  20 us
    ppermute x8, waiting for transfers between devices, shifted(): lax.ppermute(value, 'tok', [(i, (i + step * GROUP) % count) for i in rang...  17.8 us
    ppermute x8, starting transfers between devices, shifted(): lax.ppermute(value, 'tok', [(i, (i + step * GROUP) % count) for i in rang...  16 us
    all_to_all x1, blocking collectives, per_device(): terms = lax.all_to_all(parts, 'feat', 0, 0)  14.6 us
    pallas_call x1, Pallas kernels, early(): pl.pallas_call(functools.partial(early_kernel, z_count=blk // share), out...  12 us
    all_to_all x1, blocking collectives, per_device(): lax.all_to_all(jnp.broadcast_to(mine[None], parts.shape), 'feat', 0, 0)  11.8 us
    pallas_call x1, Pallas kernels, lay(): pl.pallas_call(functools.partial(lay_kernel, z_count=blk // share, n_w=le...  10.6 us
  transfers between devices with their start and end apart: 27, of which 10 were waited for; matrix products, arithmetic and copies ran while one was open for 5% of the time, Pallas kernels for 18%

profile of v5, /device:TPU:1, one launch (start us, length us, event | category | flops | bytes accessed | tf_op | source)
XLA Modules:
  0.0 151.2 jit_solution(10323201374593839056)
XLA Ops:
  0.7 2.2 %shard_map.104 = (bf16[2,5,24,384]{3,2,1,0:T(8,128)(2,1)}, bf16[2,5,24,384]{3,2,1,0:T(8,128)(2,1)}, bf16[2,5,24,384]{3,2,1,0:T(8,128)(2,1)}, bf16[2,5,24,384]{3,2,1,0:T(8,128)(2,1)}) custom-call(s32[1]{0:T(128)} %bitcast.own_ref, bf16[2,5,24,768]{3,2,1,0:T(8,128)(2,1)} %gate_ref.1, bf16[2,5,24,768]{3,2,1,0:T(8,128)(2,1)} %up_ref.1), custom_call_target="tpu_custom_call" | custom-call | tf_op jit(solution)/shard_map/pallas_call | solution.py:233
  2.9 3.2 %collective-permute-start = (bf16[2,5,24,384]{3,2,1,0:T(8,128)(2,1)}, bf16[2,5,24,384]{3,2,1,0:T(8,128)(2,1)S(1)}, u32[]{:S(2)}, u32[]{:S(2)}) collective-permute-start(bf16[2,5,24,384]{3,2,1,0:T(8,128)(2,1)} %get-tuple-element.52), channel_id=1, source_target_pairs={{0,1},{1,0},{2,3},{3,2},{4,5},{5,4},{6,7},{7,6},{8,9},{9,8},{10,11... | collective-permute-start | bytes 552968 | tf_op jit(solution)/shard_map/ppermute | solution.py:19
  9.7 2.2 %collective-permute-start.7 = (bf16[256,768]{1,0:T(8,128)(2,1)S(1)}, bf16[256,768]{1,0:T(8,128)(2,1)}, u32[]{:S(2)}, u32[]{:S(2)}) collective-permute-start(bf16[256,768]{1,0:T(8,128)(2,1)S(1)} %get-tuple-element.64), channel_id=1, source_target_pairs={{0,128},{32,160},{64,192},{96,224},{128,0},{160,32},{192,64},{224,... | collective-permute-start | bytes 1179656 | tf_op jit(solution)/shard_map/ppermute | solution.py:19
  12.6 4.4 %collective-permute-done.2.refs_3_ = bf16[2,5,24,384]{3,2,1,0:T(8,128)(2,1)} collective-permute-done((bf16[2,5,24,384]{3,2,1,0:T(8,128)(2,1)}, bf16[2,5,24,384]{3,2,1,0:T(8,128)(2,1)}, u32[]{:S(2)}, u32[]{:S(2)}) %collective-permute-start.2) | collective-permute-done | bytes 184352 | tf_op jit(solution)/shard_map/ppermute | solution.py:19
  17.0 2.1 %shard_map.105 = bf16[2,5,4,24,384]{4,3,2,1,0:T(8,128)(2,1)} custom-call(s32[1]{0:T(128)} %bitcast.own_ref, bf16[2,5,24,384]{3,2,1,0:T(8,128)(2,1)} %get-tuple-element.51.refs_0_, bf16[2,5,24,384]{3,2,1,0:T(8,128)(2,1)} %copy-done.12, bf16[2,5,24,384]{3,2,1,0:T(8,128)(2,1)} %copy-done.13, bf16[2,5,24,384]{3,2,1,0:T(8,128)(2,1)} %collective-permute-done.2.refs_3_), custom_call_target="tpu_custom_call" | custom-call | tf_op jit(solution)/shard_map/pallas_call | solution.py:243
  20.3 3.9 %collective-permute-start.4 = (bf16[2,5,96,384]{3,2,1,0:T(8,128)(2,1)}, bf16[2,5,96,384]{3,2,1,0:T(8,128)(2,1)S(1)}, u32[]{:S(2)}, u32[]{:S(2)}) collective-permute-start(bf16[2,5,96,384]{3,2,1,0:T(8,128)(2,1)} %bitcast.14), channel_id=1, source_target_pairs={{0,28},{1,29},{2,30},{3,31},{4,0},{5,1},{6,2},{7,3},{8,4},{9,5},{1... | collective-permute-start | bytes 2211848 | tf_op jit(solution)/shard_map/ppermute | solution.py:24
  24.2 5.1 %collective-permute-done.7 = bf16[256,768]{1,0:T(8,128)(2,1)} collective-permute-done((bf16[256,768]{1,0:T(8,128)(2,1)S(1)}, bf16[256,768]{1,0:T(8,128)(2,1)}, u32[]{:S(2)}, u32[]{:S(2)}) %collective-permute-start.7) | collective-permute-done | bytes 393248 | tf_op jit(solution)/shard_map/ppermute | solution.py:19
  31.0 10.1 %collective-permute-done.3.refs_1_ = bf16[2,5,96,384]{3,2,1,0:T(8,128)(2,1)S(1)} collective-permute-done((bf16[2,5,96,384]{3,2,1,0:T(8,128)(2,1)}, bf16[2,5,96,384]{3,2,1,0:T(8,128)(2,1)S(1)}, u32[]{:S(2)}, u32[]{:S(2)}) %collective-permute-start.3) | collective-permute-done | bytes 737312 | tf_op jit(solution)/shard_map/ppermute | solution.py:24
  42.2 2.5 %collective-permute-start.12 = (bf16[512,768]{1,0:T(8,128)(2,1)S(1)}, bf16[512,768]{1,0:T(8,128)(2,1)}, u32[]{:S(2)}, u32[]{:S(2)}) collective-permute-start(bf16[512,768]{1,0:T(8,128)(2,1)S(1)} %pad_maximum_fusion), channel_id=1, source_target_pairs={{0,32},{32,0},{64,96},{96,64},{128,160},{160,128},{192,224},{224,1... | collective-permute-start | bytes 2359304 | tf_op jit(solution)/shard_map/ppermute | solution.py:19
  46.4 3.9 %collective-permute-start.11 = (bf16[2,5,96,384]{3,2,1,0:T(8,128)(2,1)S(1)}, bf16[2,5,96,384]{3,2,1,0:T(8,128)(2,1)}, u32[]{:S(2)}, u32[]{:S(2)}) collective-permute-start(bf16[2,5,96,384]{3,2,1,0:T(8,128)(2,1)S(1)} %collective-permute-done.4.refs_2_), channel_id=1, source_target_pairs={{0,28},{1,29},{2,30},{3,31},{4,0},{5,1},{6,2},{7,3},{8,4},{9,5},{1... | collective-permute-start | bytes 2211848 | tf_op jit(solution)/shard_map/ppermute | solution.py:24
  55.0 7.0 %collective-permute-done.13 = bf16[256,768]{1,0:T(8,128)(2,1)S(1)} collective-permute-done((bf16[256,768]{1,0:T(8,128)(2,1)S(1)}, bf16[256,768]{1,0:T(8,128)(2,1)S(1)}, u32[]{:S(2)}, u32[]{:S(2)}) %collective-permute-start.13) | collective-permute-done | bytes 393248 | tf_op jit(solution)/shard_map/ppermute | solution.py:19
  62.0 5.0 %collective-permute-done.10.refs_3_ = bf16[2,5,96,384]{3,2,1,0:T(8,128)(2,1)} collective-permute-done((bf16[2,5,96,384]{3,2,1,0:T(8,128)(2,1)S(1)}, bf16[2,5,96,384]{3,2,1,0:T(8,128)(2,1)}, u32[]{:S(2)}, u32[]{:S(2)}) %collective-permute-start.10) | collective-permute-done | bytes 737312 | tf_op jit(solution)/shard_map/ppermute | solution.py:24
  71.1 2.7 %collective-permute-start.17 = (bf16[2,5,96,384]{3,2,1,0:T(8,128)(2,1)}, bf16[2,5,96,384]{3,2,1,0:T(8,128)(2,1)}, u32[]{:S(2)}, u32[]{:S(2)}) collective-permute-start(bf16[2,5,96,384]{3,2,1,0:T(8,128)(2,1)} %collective-permute-done.11.refs_4_), channel_id=1, source_target_pairs={{0,28},{1,29},{2,30},{3,31},{4,0},{5,1},{6,2},{7,3},{8,4},{9,5},{1... | collective-permute-start | bytes 2211848 | tf_op jit(solution)/shard_map/ppermute | solution.py:24
  77.0 10.6 %shard_map.106 = (bf16[5,1024,768]{2,1,0:T(8,128)(2,1)}, bf16[5,1024,256]{2,1,0:T(8,128)(2,1)}, bf16[5,768,768]{2,1,0:T(8,128)(2,1)}) custom-call(s32[7]{0:T(128)} %pad_add_fusion.place_ref, bf16[2,5,96,384]{3,2,1,0:T(8,128)(2,1)} %bitcast.15, bf16[2,5,96,384]{3,2,1,0:T(8,128)(2,1)} %copy-done.7, bf16[2,5,96,384]{3,2,1,0:T(8,128)(2,1)} %copy-done.8, ...), custom_call_target="tpu_custom_call" | custom-call | flops 1048576 | bytes 1048576 | tf_op jit(solution)/shard_map/pallas_call | solution.py:92
  87.7 2.7 %collective-permute-done.16.f_ref.below_ref = bf16[2,5,96,384]{3,2,1,0:T(8,128)(2,1)S(1)} collective-permute-done((bf16[2,5,96,384]{3,2,1,0:T(8,128)(2,1)}, bf16[2,5,96,384]{3,2,1,0:T(8,128)(2,1)S(1)}, u32[]{:S(2)}, u32[]{:S(2)}) %collective-permute-start.16) | collective-permute-done | bytes 737312 | tf_op jit(solution)/shard_map/ppermute | solution.py:24
  92.3 2.3 %collective-permute-start.22 = (bf16[1,5,96,384]{3,2,1,0:T(8,128)(2,1)}, bf16[1,5,96,384]{3,2,1,0:T(8,128)(2,1)S(1)}, u32[]{:S(2)}, u32[]{:S(2)}) collective-permute-start(bf16[1,5,96,384]{3,2,1,0:T(8,128)(2,1)} %get-tuple-element.89), channel_id=1, source_target_pairs={{0,4},{1,5},{2,6},{3,7},{4,8},{5,9},{6,10},{7,11},{8,12},{9,13},{1... | collective-permute-start | bytes 1105928 | tf_op jit(solution)/shard_map/ppermute | solution.py:24
  95.0 12.0 %shard_map.108.acc_ref = f32[1024,768]{1,0:T(8,128)S(1)} custom-call(s32[7]{0:T(128)S(1)} %copy-done.3, f32[5]{0:T(128)S(1)} %get-tuple-element.102.gs_ref, f32[5]{0:T(128)S(1)} %get-tuple-element.103.us_ref, bf16[5,1024,768]{2,1,0:T(8,128)(2,1)} %get-tuple-element.91.x_ref, bf16[5,768,768]{2,1,0:T(8,128)(2,1)} %get-tuple-element.92.w_ref, ...), custom_call_target="tpu_custom_call" | custom-call | flops 1048576 | bytes 1048576 | tf_op jit(solution)/shard_map/pallas_call | solution.py:133
  107.0 2.5 %shard_map.110 = (bf16[256,384]{1,0:T(8,128)(2,1)S(1)}, bf16[256,384]{1,0:T(8,128)(2,1)S(1)}) custom-call(s32[7]{0:T(128)S(1)} %copy-done.3, f32[5]{0:T(128)S(1)} %get-tuple-element.102.gs_ref, f32[5]{0:T(128)S(1)} %get-tuple-element.103.us_ref, bf16[1,5,96,384]{3,2,1,0:T(8,128)(2,1)S(1)} %collective-permute-done.22.g_ref, ...), custom_call_target="tpu_custom_call" | custom-call | flops 1006632960 | bytes 4194304 | tf_op jit(solution)/shard_map/pallas_call | solution.py:175
  109.7 3.2 %collective-permute-start.26 = (bf16[256,384]{1,0:T(8,128)(2,1)S(1)}, bf16[256,384]{1,0:T(8,128)(2,1)S(1)}, u32[]{:S(2)}, u32[]{:S(2)}) collective-permute-start(bf16[256,384]{1,0:T(8,128)(2,1)S(1)} %get-tuple-element.97), channel_id=1, source_target_pairs={{0,3},{1,2},{2,1},{3,0},{4,7},{5,6},{6,5},{7,4},{8,11},{9,10},{10,... | collective-permute-start | bytes 589832 | tf_op jit(solution)/shard_map/ppermute | solution.py:19
  112.9 2.5 %shard_map.109 = (bf16[256,384]{1,0:T(8,128)(2,1)S(1)}, bf16[256,384]{1,0:T(8,128)(2,1)S(1)}) custom-call(s32[7]{0:T(128)S(1)} %copy-done.3, f32[5]{0:T(128)S(1)} %get-tuple-element.102.gs_ref, f32[5]{0:T(128)S(1)} %get-tuple-element.103.us_ref, bf16[1,5,96,384]{3,2,1,0:T(8,128)(2,1)S(1)} %collective-permute-done.22.g_ref, ...), custom_call_target="tpu_custom_call" | custom-call | flops 1006632960 | bytes 4194304 | tf_op jit(solution)/shard_map/pallas_call | solution.py:175
  115.6 4.9 %collective-permute-done.26.refs_3_ = bf16[256,384]{1,0:T(8,128)(2,1)S(1)} collective-permute-done((bf16[256,384]{1,0:T(8,128)(2,1)S(1)}, bf16[256,384]{1,0:T(8,128)(2,1)S(1)}, u32[]{:S(2)}, u32[]{:S(2)}) %collective-permute-start.26) | collective-permute-done | bytes 196640 | tf_op jit(solution)/shard_map/ppermute | solution.py:19
  120.5 2.5 %shard_map.111 = (bf16[256,1536]{1,0:T(8,128)(2,1)}, bf16[256,768]{1,0:T(8,128)(2,1)S(1)}) custom-call(s32[1]{0:T(128)} %bitcast.own_ref, bf16[1536,768]{1,0:T(8,128)(2,1)S(1)} %copy-done.2, bf16[256,384]{1,0:T(8,128)(2,1)S(1)} %get-tuple-element.94.refs_0_, bf16[256,384]{1,0:T(8,128)(2,1)S(1)} %collective-permute-done.24.refs_1_, ...), custom_call_target="tpu_custom_call" | custom-call | flops 603979776 | bytes 4194304 | tf_op jit(solution)/shard_map/pallas_call | solution.py:308
  123.0 14.6 %all_to_all.10 = bf16[8,32,768]{2,1,0:T(8,128)(2,1)S(1)} all-to-all(bf16[8,32,768]{2,1,0:T(8,128)(2,1)S(1)} %bitcast.12), channel_id=1, replica_groups=mesh['feat'=8,'tok'=32] {'feat'}, dimensions={0} | all-to-all | bytes 786432 | tf_op jit(solution)/shard_map/all_to_all | solution.py:330
  137.7 11.8 %all_to_all.11 = bf16[8,32,768]{2,1,0:T(8,128)(2,1)S(1)} all-to-all(bf16[8,32,768]{2,1,0:T(8,128)(2,1)S(1)} %broadcast_in_dim.27), channel_id=1, replica_groups=mesh['feat'=8,'tok'=32] {'feat'}, dimensions={0} | all-to-all | bytes 786432 | tf_op jit(solution)/shard_map/all_to_all | solution.py:332
  (89 shorter events, 26.0 us)
Async XLA Ops:
  2.9 9.0 %collective-permute-start = (bf16[2,5,24,384]{3,2,1,0:T(8,128)(2,1)}, bf16[2,5,24,384]{3,2,1,0:T(8,128)(2,1)S(1)}, u32[]{:S(2)}, u32[]{:S(2)}) collective-permute-start(bf16[2,5,24,384]{3,2,1,0:T(8,128)(2,1)} %get-tuple-element.52), channel_id=1, source_target_pairs={{0,1},{1,0},{2,3},{3,2},{4,5},{5,4},{6,7},{7,6},{8,9},{9,8},{10,11... | collective-permute-start | bytes 552968 | tf_op jit(solution)/shard_map/ppermute | solution.py:19
  6.1 6.5 %collective-permute-start.1 = (bf16[2,5,24,384]{3,2,1,0:T(8,128)(2,1)}, bf16[2,5,24,384]{3,2,1,0:T(8,128)(2,1)S(1)}, u32[]{:S(2)}, u32[]{:S(2)}) collective-permute-start(bf16[2,5,24,384]{3,2,1,0:T(8,128)(2,1)} %get-tuple-element.53), channel_id=1, source_target_pairs={{0,2},{1,3},{2,0},{3,1},{4,6},{5,7},{6,4},{7,5},{8,10},{9,11},{10,... | collective-permute-start | bytes 552968 | tf_op jit(solution)/shard_map/ppermute | solution.py:19
  6.1 10.9 %collective-permute-start.2 = (bf16[2,5,24,384]{3,2,1,0:T(8,128)(2,1)}, bf16[2,5,24,384]{3,2,1,0:T(8,128)(2,1)}, u32[]{:S(2)}, u32[]{:S(2)}) collective-permute-start(bf16[2,5,24,384]{3,2,1,0:T(8,128)(2,1)} %get-tuple-element.54), channel_id=1, source_target_pairs={{0,3},{1,2},{2,1},{3,0},{4,7},{5,6},{6,5},{7,4},{8,11},{9,10},{10,... | collective-permute-start | bytes 552968 | tf_op jit(solution)/shard_map/ppermute | solution.py:19
  9.7 14.6 %collective-permute-start.6 = (bf16[256,768]{1,0:T(8,128)(2,1)S(1)}, bf16[256,768]{1,0:T(8,128)(2,1)}, u32[]{:S(2)}, u32[]{:S(2)}) collective-permute-start(bf16[256,768]{1,0:T(8,128)(2,1)S(1)} %get-tuple-element.64), channel_id=1, source_target_pairs={{0,64},{32,96},{64,0},{96,32},{128,192},{160,224},{192,128},{224,1... | collective-permute-start | bytes 1179656 | tf_op jit(solution)/shard_map/ppermute | solution.py:19
  9.7 19.7 %collective-permute-start.7 = (bf16[256,768]{1,0:T(8,128)(2,1)S(1)}, bf16[256,768]{1,0:T(8,128)(2,1)}, u32[]{:S(2)}, u32[]{:S(2)}) collective-permute-start(bf16[256,768]{1,0:T(8,128)(2,1)S(1)} %get-tuple-element.64), channel_id=1, source_target_pairs={{0,128},{32,160},{64,192},{96,224},{128,0},{160,32},{192,64},{224,... | collective-permute-start | bytes 1179656 | tf_op jit(solution)/shard_map/ppermute | solution.py:19
  19.2 10.9 %collective-permute-start.5 = (bf16[256,768]{1,0:T(8,128)(2,1)}, bf16[256,768]{1,0:T(8,128)(2,1)S(1)}, u32[]{:S(2)}, u32[]{:S(2)}) collective-permute-start(bf16[256,768]{1,0:T(8,128)(2,1)} %get-tuple-element.56), channel_id=1, source_target_pairs={{0,2},{1,3},{2,0},{3,1},{4,6},{5,7},{6,4},{7,5},{8,10},{9,11},{10,... | collective-permute-start | bytes 1179656 | tf_op jit(solution)/shard_map/ppermute | solution.py:19
  19.2 21.9 %collective-permute-start.3 = (bf16[2,5,96,384]{3,2,1,0:T(8,128)(2,1)}, bf16[2,5,96,384]{3,2,1,0:T(8,128)(2,1)S(1)}, u32[]{:S(2)}, u32[]{:S(2)}) collective-permute-start(bf16[2,5,96,384]{3,2,1,0:T(8,128)(2,1)} %bitcast.13), channel_id=1, source_target_pairs={{0,4},{1,5},{2,6},{3,7},{4,8},{5,9},{6,10},{7,11},{8,12},{9,13},{1... | collective-permute-start | bytes 2211848 | tf_op jit(solution)/shard_map/ppermute | solution.py:24
  20.3 20.8 %collective-permute-start.4 = (bf16[2,5,96,384]{3,2,1,0:T(8,128)(2,1)}, bf16[2,5,96,384]{3,2,1,0:T(8,128)(2,1)S(1)}, u32[]{:S(2)}, u32[]{:S(2)}) collective-permute-start(bf16[2,5,96,384]{3,2,1,0:T(8,128)(2,1)} %bitcast.14), channel_id=1, source_target_pairs={{0,28},{1,29},{2,30},{3,31},{4,0},{5,1},{6,2},{7,3},{8,4},{9,5},{1... | collective-permute-start | bytes 2211848 | tf_op jit(solution)/shard_map/ppermute | solution.py:24
  30.1 11.0 %collective-permute-start.8 = (bf16[256,768]{1,0:T(8,128)(2,1)S(1)}, bf16[256,768]{1,0:T(8,128)(2,1)S(1)}, u32[]{:S(2)}, u32[]{:S(2)}) collective-permute-start(bf16[256,768]{1,0:T(8,128)(2,1)S(1)} %get-tuple-element.64), channel_id=1, source_target_pairs={{0,2},{1,3},{2,0},{3,1},{4,6},{5,7},{6,4},{7,5},{8,10},{9,11},{10,... | collective-permute-start | bytes 1179656 | tf_op jit(solution)/shard_map/ppermute | solution.py:19
  30.6 10.5 %collective-permute-start.9 = (bf16[256,768]{1,0:T(8,128)(2,1)S(1)}, bf16[256,768]{1,0:T(8,128)(2,1)S(1)}, u32[]{:S(2)}, u32[]{:S(2)}) collective-permute-start(bf16[256,768]{1,0:T(8,128)(2,1)S(1)} %collective-permute-done.5.refs_7_), channel_id=1, source_target_pairs={{0,64},{32,96},{64,0},{96,32},{128,192},{160,224},{192,128},{224,1... | collective-permute-start | bytes 1179656 | tf_op jit(solution)/shard_map/ppermute | solution.py:19
  41.1 11.1 %collective-permute-start.14 = (bf16[256,1536]{1,0:T(8,128)(2,1)S(1)}, bf16[256,1536]{1,0:T(8,128)(2,1)S(1)}, u32[]{:S(2)}, u32[]{:S(2)}) collective-permute-start(bf16[256,1536]{1,0:T(8,128)(2,1)S(1)} %copy-done.4), channel_id=1, source_target_pairs={{0,1},{1,0},{2,3},{3,2},{4,5},{5,4},{6,7},{7,6},{8,9},{9,8},{10,11... | collective-permute-start | bytes 2359304 | tf_op jit(solution)/shard_map/ppermute | solution.py:19
  42.2 24.9 %collective-permute-start.12 = (bf16[512,768]{1,0:T(8,128)(2,1)S(1)}, bf16[512,768]{1,0:T(8,128)(2,1)}, u32[]{:S(2)}, u32[]{:S(2)}) collective-permute-start(bf16[512,768]{1,0:T(8,128)(2,1)S(1)} %pad_maximum_fusion), channel_id=1, source_target_pairs={{0,32},{32,0},{64,96},{96,64},{128,160},{160,128},{192,224},{224,1... | collective-permute-start | bytes 2359304 | tf_op jit(solution)/shard_map/ppermute | solution.py:19
  44.7 22.3 %collective-permute-start.10 = (bf16[2,5,96,384]{3,2,1,0:T(8,128)(2,1)S(1)}, bf16[2,5,96,384]{3,2,1,0:T(8,128)(2,1)}, u32[]{:S(2)}, u32[]{:S(2)}) collective-permute-start(bf16[2,5,96,384]{3,2,1,0:T(8,128)(2,1)S(1)} %collective-permute-done.3.refs_1_), channel_id=1, source_target_pairs={{0,4},{1,5},{2,6},{3,7},{4,8},{5,9},{6,10},{7,11},{8,12},{9,13},{1... | collective-permute-start | bytes 2211848 | tf_op jit(solution)/shard_map/ppermute | solution.py:24
  46.4 20.7 %collective-permute-start.11 = (bf16[2,5,96,384]{3,2,1,0:T(8,128)(2,1)S(1)}, bf16[2,5,96,384]{3,2,1,0:T(8,128)(2,1)}, u32[]{:S(2)}, u32[]{:S(2)}) collective-permute-start(bf16[2,5,96,384]{3,2,1,0:T(8,128)(2,1)S(1)} %collective-permute-done.4.refs_2_), channel_id=1, source_target_pairs={{0,28},{1,29},{2,30},{3,31},{4,0},{5,1},{6,2},{7,3},{8,4},{9,5},{1... | collective-permute-start | bytes 2211848 | tf_op jit(solution)/shard_map/ppermute | solution.py:24
  50.3 11.7 %collective-permute-start.13 = (bf16[256,768]{1,0:T(8,128)(2,1)S(1)}, bf16[256,768]{1,0:T(8,128)(2,1)S(1)}, u32[]{:S(2)}, u32[]{:S(2)}) collective-permute-start(bf16[256,768]{1,0:T(8,128)(2,1)S(1)} %collective-permute-done.5.refs_7_), channel_id=1, source_target_pairs={{0,128},{32,160},{64,192},{96,224},{128,0},{160,32},{192,64},{224,... | collective-permute-start | bytes 1179656 | tf_op jit(solution)/shard_map/ppermute | solution.py:19
  52.2 14.8 %collective-permute-start.15 = (bf16[256,768]{1,0:T(8,128)(2,1)S(1)}, bf16[256,768]{1,0:T(8,128)(2,1)S(1)}, u32[]{:S(2)}, u32[]{:S(2)}) collective-permute-start(bf16[256,768]{1,0:T(8,128)(2,1)S(1)} %collective-permute-done.8.refs_8_), channel_id=1, source_target_pairs={{0,1},{1,0},{2,3},{3,2},{4,5},{5,4},{6,7},{7,6},{8,9},{9,8},{10,11... | collective-permute-start | bytes 1179656 | tf_op jit(solution)/shard_map/ppermute | solution.py:19
  67.1 6.9 %collective-permute-start.18 = (bf16[512,768]{1,0:T(8,128)(2,1)}, bf16[512,768]{1,0:T(8,128)(2,1)}, u32[]{:S(2)}, u32[]{:S(2)}) collective-permute-start(bf16[512,768]{1,0:T(8,128)(2,1)} %pad_maximum_fusion.1.refs_12_), channel_id=1, source_target_pairs={{0,1},{1,0},{2,3},{3,2},{4,5},{5,4},{6,7},{7,6},{8,9},{9,8},{10,11... | collective-permute-start | bytes 2359304 | tf_op jit(solution)/shard_map/ppermute | solution.py:19
  70.5 5.2 %collective-permute-start.21 = (bf16[512,768]{1,0:T(8,128)(2,1)}, bf16[512,768]{1,0:T(8,128)(2,1)}, u32[]{:S(2)}, u32[]{:S(2)}) collective-permute-start(bf16[512,768]{1,0:T(8,128)(2,1)} %constant_dynamic-update-slice_fusion.refs_13_), channel_id=1, source_target_pairs={{0,1},{1,0},{2,3},{3,2},{4,5},{5,4},{6,7},{7,6},{8,9},{9,8},{10,11... | collective-permute-start | bytes 2359304 | tf_op jit(solution)/shard_map/ppermute | solution.py:19
  71.1 19.2 %collective-permute-start.16 = (bf16[2,5,96,384]{3,2,1,0:T(8,128)(2,1)}, bf16[2,5,96,384]{3,2,1,0:T(8,128)(2,1)S(1)}, u32[]{:S(2)}, u32[]{:S(2)}) collective-permute-start(bf16[2,5,96,384]{3,2,1,0:T(8,128)(2,1)} %collective-permute-done.10.refs_3_), channel_id=1, source_target_pairs={{0,4},{1,5},{2,6},{3,7},{4,8},{5,9},{6,10},{7,11},{8,12},{9,13},{1... | collective-permute-start | bytes 2211848 | tf_op jit(solution)/shard_map/ppermute | solution.py:24
  71.1 19.2 %collective-permute-start.17 = (bf16[2,5,96,384]{3,2,1,0:T(8,128)(2,1)}, bf16[2,5,96,384]{3,2,1,0:T(8,128)(2,1)}, u32[]{:S(2)}, u32[]{:S(2)}) collective-permute-start(bf16[2,5,96,384]{3,2,1,0:T(8,128)(2,1)} %collective-permute-done.11.refs_4_), channel_id=1, source_target_pairs={{0,28},{1,29},{2,30},{3,31},{4,0},{5,1},{6,2},{7,3},{8,4},{9,5},{1... | collective-permute-start | bytes 2211848 | tf_op jit(solution)/shard_map/ppermute | solution.py:24
  92.3 14.7 %collective-permute-start.22 = (bf16[1,5,96,384]{3,2,1,0:T(8,128)(2,1)}, bf16[1,5,96,384]{3,2,1,0:T(8,128)(2,1)S(1)}, u32[]{:S(2)}, u32[]{:S(2)}) collective-permute-start(bf16[1,5,96,384]{3,2,1,0:T(8,128)(2,1)} %get-tuple-element.89), channel_id=1, source_target_pairs={{0,4},{1,5},{2,6},{3,7},{4,8},{5,9},{6,10},{7,11},{8,12},{9,13},{1... | collective-permute-start | bytes 1105928 | tf_op jit(solution)/shard_map/ppermute | solution.py:24
  94.6 12.5 %collective-permute-start.23 = (bf16[1,5,96,384]{3,2,1,0:T(8,128)(2,1)}, bf16[1,5,96,384]{3,2,1,0:T(8,128)(2,1)}, u32[]{:S(2)}, u32[]{:S(2)}) collective-permute-start(bf16[1,5,96,384]{3,2,1,0:T(8,128)(2,1)} %get-tuple-element.90), channel_id=1, source_target_pairs={{0,28},{1,29},{2,30},{3,31},{4,0},{5,1},{6,2},{7,3},{8,4},{9,5},{1... | collective-permute-start | bytes 1105928 | tf_op jit(solution)/shard_map/ppermute | solution.py:24
  109.6 6.0 %collective-permute-start.25 = (bf16[256,384]{1,0:T(8,128)(2,1)S(1)}, bf16[256,384]{1,0:T(8,128)(2,1)S(1)}, u32[]{:S(2)}, u32[]{:S(2)}) collective-permute-start(bf16[256,384]{1,0:T(8,128)(2,1)S(1)} %get-tuple-element.96), channel_id=1, source_target_pairs={{0,2},{1,3},{2,0},{3,1},{4,6},{5,7},{6,4},{7,5},{8,10},{9,11},{10,... | collective-permute-start | bytes 589832 | tf_op jit(solution)/shard_map/ppermute | solution.py:19
  109.7 10.8 %collective-permute-start.26 = (bf16[256,384]{1,0:T(8,128)(2,1)S(1)}, bf16[256,384]{1,0:T(8,128)(2,1)S(1)}, u32[]{:S(2)}, u32[]{:S(2)}) collective-permute-start(bf16[256,384]{1,0:T(8,128)(2,1)S(1)} %get-tuple-element.97), channel_id=1, source_target_pairs={{0,3},{1,2},{2,1},{3,0},{4,7},{5,6},{6,5},{7,4},{8,11},{9,10},{10,... | collective-permute-start | bytes 589832 | tf_op jit(solution)/shard_map/ppermute | solution.py:19
  (21 other events, 557.8 us)

commit v6 on v5

--- a/solution.py
+++ b/solution.py
@@ -51,7 +51,9 @@
     column = pl.ds(pl.multiple_of(start, 128), width)
     if j < 2:
         return own_refs[2 * m - 2 + j][:, column]
-    return partner_refs[m % 2 * 3 + j - 2][pl.ds(m // 2 * rows, rows), column]
+    if j < 4:
+        return partner_refs[m % 2 * 4 + j - 2][pl.ds(m // 2 * rows, rows), column]
+    return partner_refs[m % 2 * 4 + 2 + m // 2][:, column]
 
 
 def last_window(z, z_count, share, blk, window):
@@ -65,8 +67,8 @@
 
 
 def lay_kernel(place_ref, *refs, z_count, n_w):
-    w_refs, own_refs, partner_refs = refs[:n_w], refs[n_w : n_w + 6], refs[n_w + 6 : n_w + 12]
-    x_ref, windows, w_out = refs[n_w + 12 :]
+    w_refs, own_refs, partner_refs = refs[:n_w], refs[n_w : n_w + 6], refs[n_w + 6 : n_w + 14]
+    x_ref, windows, w_out = refs[n_w + 14 :]
     x_lo, z = place_ref[5], place_ref[6]
     share, width = w_refs[0].shape[2:]
     rows, (blk, window) = own_refs[0].shape[0], (x_ref.shape[2], windows.shape[2])
@@ -92,7 +94,7 @@
     return pl.pallas_call(
         functools.partial(lay_kernel, z_count=blk // share, n_w=len(weights)),
         out_shape=[jax.ShapeDtypeStruct(shape, jnp.bfloat16) for shape in shapes],
-        in_specs=[SMEM] + [VMEM] * (len(weights) + 12),
+        in_specs=[SMEM] + [VMEM] * (len(weights) + 14),
         out_specs=[VMEM] * 3,
         compiler_params=pltpu.CompilerParams(vmem_limit_bytes=LAY_BYTES),
         cost_estimate=pl.CostEstimate(flops=2**20, bytes_accessed=2**20, transcendentals=0),
@@ -279,11 +281,14 @@
     p_y1 = jnp.concatenate([p0_y1, p2_y1])
     w2, p_x, p2_y2, p0_y2, p_y1, s2_own, s1, s3_other = barrier((w2, p_x, p2_y2, p0_y2, p_y1, s2_own, s1, s3_other))
     w3 = step(*w2)
-    p_y2 = jnp.concatenate([p0_y2, p2_y2])
+    q_x = swapped(p_x, "tok", 1)
     q_y1 = swapped(p_y1, "tok", 1)
-    q_y1, s2_own = barrier((q_y1, s2_own))
+    q_y1, p0_y2 = barrier((q_y1, p0_y2))
+    q0_y2 = swapped(p0_y2, "tok", 1)
+    q2_y2 = swapped(p2_y2, "tok", 1)
+    q2_y2, s2_own = barrier((q2_y2, s2_own))
     s3_own = swapped(s2_own, "tok", 1)
-    partner_rows = [p_x, p_y1, p_y2, swapped(p_x, "tok", 1), q_y1, swapped(p_y2, "tok", 1)]
+    partner_rows = [p_x, p_y1, p0_y2, p2_y2, q_x, q_y1, q0_y2, q2_y2]
     own_rows = [later, s1, s2_own, s2_other, s3_own, s3_other]
     x, windows, w_laid = lay(here, (w0, *w1, *w2), own_rows, partner_rows)
     w3, x, windows, w_laid = barrier((w3, x, windows, w_laid))

time: 152 us -> 149 us (0.980)
  local copies, waits for them, and re-layouts: 5.54 us -> 2.21 us
    unnamed x37 -> x36, local copies, waits for them, and re-layouts: 2.63 us -> 0.08 us
    ppermute x19 -> x20, waiting for transfers between devices: 23.6 us -> 24.3 us  [swapped(): lax.ppermute(value, axis, [(i, i ^ mask) for i in range(lax.axis_size(axi...]
    ppermute x19 -> x20, starting transfers between devices: 20 us -> 20.1 us  [swapped(): lax.ppermute(value, axis, [(i, i ^ mask) for i in range(lax.axis_size(axi...]
  transfers between devices with their start and end apart: 27 -> 28, of which waited for: 10 -> 11; matrix products, arithmetic and copies ran while one was open for 5% -> 3% of each run, Pallas kernels for 18% -> 18%
where the time goes in v6:
time: 149 us
  waiting for transfers between devices  42 us (28%)
  Pallas kernels  36.4 us (24%)
  starting transfers between devices  36.1 us (24%)
  blocking collectives  26.4 us (18%)
  other arithmetic  2.88 us (2%)
  local copies, waits for them, and re-layouts  2.21 us (1%)
  matrix products  1.66 us (1%)
    ppermute x20, waiting for transfers between devices, swapped(): lax.ppermute(value, axis, [(i, i ^ mask) for i in range(lax.axis_size(axi...  24.3 us
    ppermute x20, starting transfers between devices, swapped(): lax.ppermute(value, axis, [(i, i ^ mask) for i in range(lax.axis_size(axi...  20.1 us
    ppermute x8, waiting for transfers between devices, shifted(): lax.ppermute(value, 'tok', [(i, (i + step * GROUP) % count) for i in rang...  17.6 us
    ppermute x8, starting transfers between devices, shifted(): lax.ppermute(value, 'tok', [(i, (i + step * GROUP) % count) for i in rang...  16 us
    all_to_all x1, blocking collectives, per_device(): terms = lax.all_to_all(parts, 'feat', 0, 0)  14.6 us
    pallas_call x1, Pallas kernels, early(): pl.pallas_call(functools.partial(early_kernel, z_count=blk // share), out...  12 us
    all_to_all x1, blocking collectives, per_device(): lax.all_to_all(jnp.broadcast_to(mine[None], parts.shape), 'feat', 0, 0)  11.8 us
    pallas_call x1, Pallas kernels, lay(): pl.pallas_call(functools.partial(lay_kernel, z_count=blk // share, n_w=le...  10.6 us
  transfers between devices with their start and end apart: 28, of which 11 were waited for; matrix products, arithmetic and copies ran while one was open for 3% of the time, Pallas kernels for 18%

profile of v6, /device:TPU:1, one launch (start us, length us, event | category | flops | bytes accessed | tf_op | source)
XLA Modules:
  0.0 148.5 jit_solution(726338183278719264)
XLA Ops:
  0.7 2.2 %shard_map.104 = (bf16[2,5,24,384]{3,2,1,0:T(8,128)(2,1)}, bf16[2,5,24,384]{3,2,1,0:T(8,128)(2,1)}, bf16[2,5,24,384]{3,2,1,0:T(8,128)(2,1)}, bf16[2,5,24,384]{3,2,1,0:T(8,128)(2,1)}) custom-call(s32[1]{0:T(128)} %bitcast.own_ref, bf16[2,5,24,768]{3,2,1,0:T(8,128)(2,1)} %gate_ref.1, bf16[2,5,24,768]{3,2,1,0:T(8,128)(2,1)} %up_ref.1), custom_call_target="tpu_custom_call" | custom-call | tf_op jit(solution)/shard_map/pallas_call | solution.py:235
  2.9 3.2 %collective-permute-start = (bf16[2,5,24,384]{3,2,1,0:T(8,128)(2,1)}, bf16[2,5,24,384]{3,2,1,0:T(8,128)(2,1)S(1)}, u32[]{:S(2)}, u32[]{:S(2)}) collective-permute-start(bf16[2,5,24,384]{3,2,1,0:T(8,128)(2,1)} %get-tuple-element.54), channel_id=1, source_target_pairs={{0,1},{1,0},{2,3},{3,2},{4,5},{5,4},{6,7},{7,6},{8,9},{9,8},{10,11... | collective-permute-start | bytes 552968 | tf_op jit(solution)/shard_map/ppermute | solution.py:19
  9.7 2.2 %collective-permute-start.7 = (bf16[256,768]{1,0:T(8,128)(2,1)S(1)}, bf16[256,768]{1,0:T(8,128)(2,1)}, u32[]{:S(2)}, u32[]{:S(2)}) collective-permute-start(bf16[256,768]{1,0:T(8,128)(2,1)S(1)} %get-tuple-element.66), channel_id=1, source_target_pairs={{0,128},{32,160},{64,192},{96,224},{128,0},{160,32},{192,64},{224,... | collective-permute-start | bytes 1179656 | tf_op jit(solution)/shard_map/ppermute | solution.py:19
  12.6 4.4 %collective-permute-done.2.refs_3_ = bf16[2,5,24,384]{3,2,1,0:T(8,128)(2,1)} collective-permute-done((bf16[2,5,24,384]{3,2,1,0:T(8,128)(2,1)}, bf16[2,5,24,384]{3,2,1,0:T(8,128)(2,1)}, u32[]{:S(2)}, u32[]{:S(2)}) %collective-permute-start.2) | collective-permute-done | bytes 184352 | tf_op jit(solution)/shard_map/ppermute | solution.py:19
  17.0 2.2 %shard_map.105 = bf16[2,5,4,24,384]{4,3,2,1,0:T(8,128)(2,1)} custom-call(s32[1]{0:T(128)} %bitcast.own_ref, bf16[2,5,24,384]{3,2,1,0:T(8,128)(2,1)} %get-tuple-element.53.refs_0_, bf16[2,5,24,384]{3,2,1,0:T(8,128)(2,1)} %copy-done.12, bf16[2,5,24,384]{3,2,1,0:T(8,128)(2,1)} %copy-done.13, bf16[2,5,24,384]{3,2,1,0:T(8,128)(2,1)} %collective-permute-done.2.refs_3_), custom_call_target="tpu_custom_call" | custom-call | tf_op jit(solution)/shard_map/pallas_call | solution.py:245
  20.3 3.9 %collective-permute-start.4 = (bf16[2,5,96,384]{3,2,1,0:T(8,128)(2,1)}, bf16[2,5,96,384]{3,2,1,0:T(8,128)(2,1)S(1)}, u32[]{:S(2)}, u32[]{:S(2)}) collective-permute-start(bf16[2,5,96,384]{3,2,1,0:T(8,128)(2,1)} %bitcast.14), channel_id=1, source_target_pairs={{0,28},{1,29},{2,30},{3,31},{4,0},{5,1},{6,2},{7,3},{8,4},{9,5},{1... | collective-permute-start | bytes 2211848 | tf_op jit(solution)/shard_map/ppermute | solution.py:24
  24.3 5.1 %collective-permute-done.7.refs_13_ = bf16[256,768]{1,0:T(8,128)(2,1)} collective-permute-done((bf16[256,768]{1,0:T(8,128)(2,1)S(1)}, bf16[256,768]{1,0:T(8,128)(2,1)}, u32[]{:S(2)}, u32[]{:S(2)}) %collective-permute-start.7) | collective-permute-done | bytes 393248 | tf_op jit(solution)/shard_map/ppermute | solution.py:19
  31.0 10.1 %collective-permute-done.3.refs_1_ = bf16[2,5,96,384]{3,2,1,0:T(8,128)(2,1)S(1)} collective-permute-done((bf16[2,5,96,384]{3,2,1,0:T(8,128)(2,1)}, bf16[2,5,96,384]{3,2,1,0:T(8,128)(2,1)S(1)}, u32[]{:S(2)}, u32[]{:S(2)}) %collective-permute-start.3) | collective-permute-done | bytes 737312 | tf_op jit(solution)/shard_map/ppermute | solution.py:24
  42.2 2.5 %collective-permute-start.12 = (bf16[512,768]{1,0:T(8,128)(2,1)S(1)}, bf16[512,768]{1,0:T(8,128)(2,1)}, u32[]{:S(2)}, u32[]{:S(2)}) collective-permute-start(bf16[512,768]{1,0:T(8,128)(2,1)S(1)} %pad_maximum_fusion), channel_id=1, source_target_pairs={{0,32},{32,0},{64,96},{96,64},{128,160},{160,128},{192,224},{224,1... | collective-permute-start | bytes 2359304 | tf_op jit(solution)/shard_map/ppermute | solution.py:19
  46.4 3.9 %collective-permute-start.11 = (bf16[2,5,96,384]{3,2,1,0:T(8,128)(2,1)S(1)}, bf16[2,5,96,384]{3,2,1,0:T(8,128)(2,1)}, u32[]{:S(2)}, u32[]{:S(2)}) collective-permute-start(bf16[2,5,96,384]{3,2,1,0:T(8,128)(2,1)S(1)} %collective-permute-done.4.refs_2_), channel_id=1, source_target_pairs={{0,28},{1,29},{2,30},{3,31},{4,0},{5,1},{6,2},{7,3},{8,4},{9,5},{1... | collective-permute-start | bytes 2211848 | tf_op jit(solution)/shard_map/ppermute | solution.py:24
  55.0 7.0 %collective-permute-done.13.refs_14_ = bf16[256,768]{1,0:T(8,128)(2,1)} collective-permute-done((bf16[256,768]{1,0:T(8,128)(2,1)S(1)}, bf16[256,768]{1,0:T(8,128)(2,1)}, u32[]{:S(2)}, u32[]{:S(2)}) %collective-permute-start.13) | collective-permute-done | bytes 393248 | tf_op jit(solution)/shard_map/ppermute | solution.py:19
  62.0 5.0 %collective-permute-done.10.refs_3_ = bf16[2,5,96,384]{3,2,1,0:T(8,128)(2,1)} collective-permute-done((bf16[2,5,96,384]{3,2,1,0:T(8,128)(2,1)S(1)}, bf16[2,5,96,384]{3,2,1,0:T(8,128)(2,1)}, u32[]{:S(2)}, u32[]{:S(2)}) %collective-permute-start.10) | collective-permute-done | bytes 737312 | tf_op jit(solution)/shard_map/ppermute | solution.py:24
  68.5 2.7 %collective-permute-start.17 = (bf16[2,5,96,384]{3,2,1,0:T(8,128)(2,1)}, bf16[2,5,96,384]{3,2,1,0:T(8,128)(2,1)}, u32[]{:S(2)}, u32[]{:S(2)}) collective-permute-start(bf16[2,5,96,384]{3,2,1,0:T(8,128)(2,1)} %collective-permute-done.11.refs_4_), channel_id=1, source_target_pairs={{0,28},{1,29},{2,30},{3,31},{4,0},{5,1},{6,2},{7,3},{8,4},{9,5},{1... | collective-permute-start | bytes 2211848 | tf_op jit(solution)/shard_map/ppermute | solution.py:24
  74.6 10.6 %shard_map.106 = (bf16[5,1024,768]{2,1,0:T(8,128)(2,1)}, bf16[5,1024,256]{2,1,0:T(8,128)(2,1)}, bf16[5,768,768]{2,1,0:T(8,128)(2,1)}) custom-call(s32[7]{0:T(128)} %pad_add_fusion.place_ref, bf16[2,5,96,384]{3,2,1,0:T(8,128)(2,1)} %bitcast.15, bf16[2,5,96,384]{3,2,1,0:T(8,128)(2,1)} %copy-done.7, bf16[2,5,96,384]{3,2,1,0:T(8,128)(2,1)} %copy-done.8, ...), custom_call_target="tpu_custom_call" | custom-call | flops 1048576 | bytes 1048576 | tf_op jit(solution)/shard_map/pallas_call | solution.py:94
  85.2 2.5 %collective-permute-done.16.f_ref.below_ref = bf16[2,5,96,384]{3,2,1,0:T(8,128)(2,1)S(1)} collective-permute-done((bf16[2,5,96,384]{3,2,1,0:T(8,128)(2,1)}, bf16[2,5,96,384]{3,2,1,0:T(8,128)(2,1)S(1)}, u32[]{:S(2)}, u32[]{:S(2)}) %collective-permute-start.16) | collective-permute-done | bytes 737312 | tf_op jit(solution)/shard_map/ppermute | solution.py:24
  89.6 2.4 %collective-permute-start.23 = (bf16[1,5,96,384]{3,2,1,0:T(8,128)(2,1)}, bf16[1,5,96,384]{3,2,1,0:T(8,128)(2,1)S(1)}, u32[]{:S(2)}, u32[]{:S(2)}) collective-permute-start(bf16[1,5,96,384]{3,2,1,0:T(8,128)(2,1)} %get-tuple-element.93), channel_id=1, source_target_pairs={{0,4},{1,5},{2,6},{3,7},{4,8},{5,9},{6,10},{7,11},{8,12},{9,13},{1... | collective-permute-start | bytes 1105928 | tf_op jit(solution)/shard_map/ppermute | solution.py:24
  92.3 12.0 %shard_map.108.acc_ref = f32[1024,768]{1,0:T(8,128)S(1)} custom-call(s32[7]{0:T(128)S(1)} %copy-done.3, f32[5]{0:T(128)S(1)} %get-tuple-element.106.gs_ref, f32[5]{0:T(128)S(1)} %get-tuple-element.107.us_ref, bf16[5,1024,768]{2,1,0:T(8,128)(2,1)} %get-tuple-element.95.x_ref, bf16[5,768,768]{2,1,0:T(8,128)(2,1)} %get-tuple-element.96.w_ref, ...), custom_call_target="tpu_custom_call" | custom-call | flops 1048576 | bytes 1048576 | tf_op jit(solution)/shard_map/pallas_call | solution.py:135
  104.4 2.5 %shard_map.110 = (bf16[256,384]{1,0:T(8,128)(2,1)S(1)}, bf16[256,384]{1,0:T(8,128)(2,1)S(1)}) custom-call(s32[7]{0:T(128)S(1)} %copy-done.3, f32[5]{0:T(128)S(1)} %get-tuple-element.106.gs_ref, f32[5]{0:T(128)S(1)} %get-tuple-element.107.us_ref, bf16[1,5,96,384]{3,2,1,0:T(8,128)(2,1)S(1)} %collective-permute-done.23.g_ref, ...), custom_call_target="tpu_custom_call" | custom-call | flops 1006632960 | bytes 4194304 | tf_op jit(solution)/shard_map/pallas_call | solution.py:177
  107.0 3.2 %collective-permute-start.27 = (bf16[256,384]{1,0:T(8,128)(2,1)S(1)}, bf16[256,384]{1,0:T(8,128)(2,1)S(1)}, u32[]{:S(2)}, u32[]{:S(2)}) collective-permute-start(bf16[256,384]{1,0:T(8,128)(2,1)S(1)} %get-tuple-element.101), channel_id=1, source_target_pairs={{0,3},{1,2},{2,1},{3,0},{4,7},{5,6},{6,5},{7,4},{8,11},{9,10},{10,... | collective-permute-start | bytes 589832 | tf_op jit(solution)/shard_map/ppermute | solution.py:19
  110.3 2.5 %shard_map.109 = (bf16[256,384]{1,0:T(8,128)(2,1)S(1)}, bf16[256,384]{1,0:T(8,128)(2,1)S(1)}) custom-call(s32[7]{0:T(128)S(1)} %copy-done.3, f32[5]{0:T(128)S(1)} %get-tuple-element.106.gs_ref, f32[5]{0:T(128)S(1)} %get-tuple-element.107.us_ref, bf16[1,5,96,384]{3,2,1,0:T(8,128)(2,1)S(1)} %collective-permute-done.23.g_ref, ...), custom_call_target="tpu_custom_call" | custom-call | flops 1006632960 | bytes 4194304 | tf_op jit(solution)/shard_map/pallas_call | solution.py:177
  112.9 4.9 %collective-permute-done.27.refs_3_ = bf16[256,384]{1,0:T(8,128)(2,1)S(1)} collective-permute-done((bf16[256,384]{1,0:T(8,128)(2,1)S(1)}, bf16[256,384]{1,0:T(8,128)(2,1)S(1)}, u32[]{:S(2)}, u32[]{:S(2)}) %collective-permute-start.27) | collective-permute-done | bytes 196640 | tf_op jit(solution)/shard_map/ppermute | solution.py:19
  117.9 2.5 %shard_map.111 = (bf16[256,1536]{1,0:T(8,128)(2,1)}, bf16[256,768]{1,0:T(8,128)(2,1)S(1)}) custom-call(s32[1]{0:T(128)} %bitcast.own_ref, bf16[1536,768]{1,0:T(8,128)(2,1)S(1)} %copy-done.2, bf16[256,384]{1,0:T(8,128)(2,1)S(1)} %get-tuple-element.98.refs_0_, bf16[256,384]{1,0:T(8,128)(2,1)S(1)} %collective-permute-done.25.refs_1_, ...), custom_call_target="tpu_custom_call" | custom-call | flops 603979776 | bytes 4194304 | tf_op jit(solution)/shard_map/pallas_call | solution.py:313
  120.4 14.6 %all_to_all.10 = bf16[8,32,768]{2,1,0:T(8,128)(2,1)S(1)} all-to-all(bf16[8,32,768]{2,1,0:T(8,128)(2,1)S(1)} %bitcast.12), channel_id=1, replica_groups=mesh['feat'=8,'tok'=32] {'feat'}, dimensions={0} | all-to-all | bytes 786432 | tf_op jit(solution)/shard_map/all_to_all | solution.py:335
  135.0 11.8 %all_to_all.11 = bf16[8,32,768]{2,1,0:T(8,128)(2,1)S(1)} all-to-all(bf16[8,32,768]{2,1,0:T(8,128)(2,1)S(1)} %broadcast_in_dim.27), channel_id=1, replica_groups=mesh['feat'=8,'tok'=32] {'feat'}, dimensions={0} | all-to-all | bytes 786432 | tf_op jit(solution)/shard_map/all_to_all | solution.py:337
  (89 shorter events, 23.4 us)
Async XLA Ops:
  2.9 9.0 %collective-permute-start = (bf16[2,5,24,384]{3,2,1,0:T(8,128)(2,1)}, bf16[2,5,24,384]{3,2,1,0:T(8,128)(2,1)S(1)}, u32[]{:S(2)}, u32[]{:S(2)}) collective-permute-start(bf16[2,5,24,384]{3,2,1,0:T(8,128)(2,1)} %get-tuple-element.54), channel_id=1, source_target_pairs={{0,1},{1,0},{2,3},{3,2},{4,5},{5,4},{6,7},{7,6},{8,9},{9,8},{10,11... | collective-permute-start | bytes 552968 | tf_op jit(solution)/shard_map/ppermute | solution.py:19
  6.1 6.5 %collective-permute-start.1 = (bf16[2,5,24,384]{3,2,1,0:T(8,128)(2,1)}, bf16[2,5,24,384]{3,2,1,0:T(8,128)(2,1)S(1)}, u32[]{:S(2)}, u32[]{:S(2)}) collective-permute-start(bf16[2,5,24,384]{3,2,1,0:T(8,128)(2,1)} %get-tuple-element.55), channel_id=1, source_target_pairs={{0,2},{1,3},{2,0},{3,1},{4,6},{5,7},{6,4},{7,5},{8,10},{9,11},{10,... | collective-permute-start | bytes 552968 | tf_op jit(solution)/shard_map/ppermute | solution.py:19
  6.1 10.9 %collective-permute-start.2 = (bf16[2,5,24,384]{3,2,1,0:T(8,128)(2,1)}, bf16[2,5,24,384]{3,2,1,0:T(8,128)(2,1)}, u32[]{:S(2)}, u32[]{:S(2)}) collective-permute-start(bf16[2,5,24,384]{3,2,1,0:T(8,128)(2,1)} %get-tuple-element.56), channel_id=1, source_target_pairs={{0,3},{1,2},{2,1},{3,0},{4,7},{5,6},{6,5},{7,4},{8,11},{9,10},{10,... | collective-permute-start | bytes 552968 | tf_op jit(solution)/shard_map/ppermute | solution.py:19
  9.7 14.6 %collective-permute-start.6 = (bf16[256,768]{1,0:T(8,128)(2,1)S(1)}, bf16[256,768]{1,0:T(8,128)(2,1)}, u32[]{:S(2)}, u32[]{:S(2)}) collective-permute-start(bf16[256,768]{1,0:T(8,128)(2,1)S(1)} %get-tuple-element.66), channel_id=1, source_target_pairs={{0,64},{32,96},{64,0},{96,32},{128,192},{160,224},{192,128},{224,1... | collective-permute-start | bytes 1179656 | tf_op jit(solution)/shard_map/ppermute | solution.py:19
  9.7 19.7 %collective-permute-start.7 = (bf16[256,768]{1,0:T(8,128)(2,1)S(1)}, bf16[256,768]{1,0:T(8,128)(2,1)}, u32[]{:S(2)}, u32[]{:S(2)}) collective-permute-start(bf16[256,768]{1,0:T(8,128)(2,1)S(1)} %get-tuple-element.66), channel_id=1, source_target_pairs={{0,128},{32,160},{64,192},{96,224},{128,0},{160,32},{192,64},{224,... | collective-permute-start | bytes 1179656 | tf_op jit(solution)/shard_map/ppermute | solution.py:19
  19.2 10.9 %collective-permute-start.5 = (bf16[256,768]{1,0:T(8,128)(2,1)}, bf16[256,768]{1,0:T(8,128)(2,1)S(1)}, u32[]{:S(2)}, u32[]{:S(2)}) collective-permute-start(bf16[256,768]{1,0:T(8,128)(2,1)} %get-tuple-element.58), channel_id=1, source_target_pairs={{0,2},{1,3},{2,0},{3,1},{4,6},{5,7},{6,4},{7,5},{8,10},{9,11},{10,... | collective-permute-start | bytes 1179656 | tf_op jit(solution)/shard_map/ppermute | solution.py:19
  19.2 21.9 %collective-permute-start.3 = (bf16[2,5,96,384]{3,2,1,0:T(8,128)(2,1)}, bf16[2,5,96,384]{3,2,1,0:T(8,128)(2,1)S(1)}, u32[]{:S(2)}, u32[]{:S(2)}) collective-permute-start(bf16[2,5,96,384]{3,2,1,0:T(8,128)(2,1)} %bitcast.13), channel_id=1, source_target_pairs={{0,4},{1,5},{2,6},{3,7},{4,8},{5,9},{6,10},{7,11},{8,12},{9,13},{1... | collective-permute-start | bytes 2211848 | tf_op jit(solution)/shard_map/ppermute | solution.py:24
  20.3 20.8 %collective-permute-start.4 = (bf16[2,5,96,384]{3,2,1,0:T(8,128)(2,1)}, bf16[2,5,96,384]{3,2,1,0:T(8,128)(2,1)S(1)}, u32[]{:S(2)}, u32[]{:S(2)}) collective-permute-start(bf16[2,5,96,384]{3,2,1,0:T(8,128)(2,1)} %bitcast.14), channel_id=1, source_target_pairs={{0,28},{1,29},{2,30},{3,31},{4,0},{5,1},{6,2},{7,3},{8,4},{9,5},{1... | collective-permute-start | bytes 2211848 | tf_op jit(solution)/shard_map/ppermute | solution.py:24
  30.2 11.0 %collective-permute-start.8 = (bf16[256,768]{1,0:T(8,128)(2,1)S(1)}, bf16[256,768]{1,0:T(8,128)(2,1)S(1)}, u32[]{:S(2)}, u32[]{:S(2)}) collective-permute-start(bf16[256,768]{1,0:T(8,128)(2,1)S(1)} %get-tuple-element.66), channel_id=1, source_target_pairs={{0,2},{1,3},{2,0},{3,1},{4,6},{5,7},{6,4},{7,5},{8,10},{9,11},{10,... | collective-permute-start | bytes 1179656 | tf_op jit(solution)/shard_map/ppermute | solution.py:19
  30.6 10.5 %collective-permute-start.9 = (bf16[256,768]{1,0:T(8,128)(2,1)S(1)}, bf16[256,768]{1,0:T(8,128)(2,1)S(1)}, u32[]{:S(2)}, u32[]{:S(2)}) collective-permute-start(bf16[256,768]{1,0:T(8,128)(2,1)S(1)} %collective-permute-done.5.refs_7_), channel_id=1, source_target_pairs={{0,64},{32,96},{64,0},{96,32},{128,192},{160,224},{192,128},{224,1... | collective-permute-start | bytes 1179656 | tf_op jit(solution)/shard_map/ppermute | solution.py:19
  41.2 11.1 %collective-permute-start.14 = (bf16[256,1536]{1,0:T(8,128)(2,1)S(1)}, bf16[256,1536]{1,0:T(8,128)(2,1)S(1)}, u32[]{:S(2)}, u32[]{:S(2)}) collective-permute-start(bf16[256,1536]{1,0:T(8,128)(2,1)S(1)} %copy-done.4), channel_id=1, source_target_pairs={{0,1},{1,0},{2,3},{3,2},{4,5},{5,4},{6,7},{7,6},{8,9},{9,8},{10,11... | collective-permute-start | bytes 2359304 | tf_op jit(solution)/shard_map/ppermute | solution.py:19
  42.2 24.9 %collective-permute-start.12 = (bf16[512,768]{1,0:T(8,128)(2,1)S(1)}, bf16[512,768]{1,0:T(8,128)(2,1)}, u32[]{:S(2)}, u32[]{:S(2)}) collective-permute-start(bf16[512,768]{1,0:T(8,128)(2,1)S(1)} %pad_maximum_fusion), channel_id=1, source_target_pairs={{0,32},{32,0},{64,96},{96,64},{128,160},{160,128},{192,224},{224,1... | collective-permute-start | bytes 2359304 | tf_op jit(solution)/shard_map/ppermute | solution.py:19
  44.7 22.3 %collective-permute-start.10 = (bf16[2,5,96,384]{3,2,1,0:T(8,128)(2,1)S(1)}, bf16[2,5,96,384]{3,2,1,0:T(8,128)(2,1)}, u32[]{:S(2)}, u32[]{:S(2)}) collective-permute-start(bf16[2,5,96,384]{3,2,1,0:T(8,128)(2,1)S(1)} %collective-permute-done.3.refs_1_), channel_id=1, source_target_pairs={{0,4},{1,5},{2,6},{3,7},{4,8},{5,9},{6,10},{7,11},{8,12},{9,13},{1... | collective-permute-start | bytes 2211848 | tf_op jit(solution)/shard_map/ppermute | solution.py:24
  46.4 20.7 %collective-permute-start.11 = (bf16[2,5,96,384]{3,2,1,0:T(8,128)(2,1)S(1)}, bf16[2,5,96,384]{3,2,1,0:T(8,128)(2,1)}, u32[]{:S(2)}, u32[]{:S(2)}) collective-permute-start(bf16[2,5,96,384]{3,2,1,0:T(8,128)(2,1)S(1)} %collective-permute-done.4.refs_2_), channel_id=1, source_target_pairs={{0,28},{1,29},{2,30},{3,31},{4,0},{5,1},{6,2},{7,3},{8,4},{9,5},{1... | collective-permute-start | bytes 2211848 | tf_op jit(solution)/shard_map/ppermute | solution.py:24
  50.3 11.7 %collective-permute-start.13 = (bf16[256,768]{1,0:T(8,128)(2,1)S(1)}, bf16[256,768]{1,0:T(8,128)(2,1)}, u32[]{:S(2)}, u32[]{:S(2)}) collective-permute-start(bf16[256,768]{1,0:T(8,128)(2,1)S(1)} %collective-permute-done.5.refs_7_), channel_id=1, source_target_pairs={{0,128},{32,160},{64,192},{96,224},{128,0},{160,32},{192,64},{224,... | collective-permute-start | bytes 1179656 | tf_op jit(solution)/shard_map/ppermute | solution.py:19
  52.3 14.8 %collective-permute-start.15 = (bf16[256,768]{1,0:T(8,128)(2,1)S(1)}, bf16[256,768]{1,0:T(8,128)(2,1)S(1)}, u32[]{:S(2)}, u32[]{:S(2)}) collective-permute-start(bf16[256,768]{1,0:T(8,128)(2,1)S(1)} %collective-permute-done.8.refs_8_), channel_id=1, source_target_pairs={{0,1},{1,0},{2,3},{3,2},{4,5},{5,4},{6,7},{7,6},{8,9},{9,8},{10,11... | collective-permute-start | bytes 1179656 | tf_op jit(solution)/shard_map/ppermute | solution.py:19
  67.1 5.3 %collective-permute-start.20 = (bf16[512,768]{1,0:T(8,128)(2,1)}, bf16[512,768]{1,0:T(8,128)(2,1)}, u32[]{:S(2)}, u32[]{:S(2)}) collective-permute-start(bf16[512,768]{1,0:T(8,128)(2,1)} %pad_maximum_fusion.1.refs_12_), channel_id=1, source_target_pairs={{0,1},{1,0},{2,3},{3,2},{4,5},{5,4},{6,7},{7,6},{8,9},{9,8},{10,11... | collective-permute-start | bytes 2359304 | tf_op jit(solution)/shard_map/ppermute | solution.py:19
  68.1 5.6 %collective-permute-start.21 = (bf16[512,768]{1,0:T(8,128)(2,1)}, bf16[512,768]{1,0:T(8,128)(2,1)}, u32[]{:S(2)}, u32[]{:S(2)}) collective-permute-start(bf16[512,768]{1,0:T(8,128)(2,1)} %collective-permute-done.12.refs_11_), channel_id=1, source_target_pairs={{0,1},{1,0},{2,3},{3,2},{4,5},{5,4},{6,7},{7,6},{8,9},{9,8},{10,11... | collective-permute-start | bytes 2359304 | tf_op jit(solution)/shard_map/ppermute | solution.py:19
  68.5 19.2 %collective-permute-start.16 = (bf16[2,5,96,384]{3,2,1,0:T(8,128)(2,1)}, bf16[2,5,96,384]{3,2,1,0:T(8,128)(2,1)S(1)}, u32[]{:S(2)}, u32[]{:S(2)}) collective-permute-start(bf16[2,5,96,384]{3,2,1,0:T(8,128)(2,1)} %collective-permute-done.10.refs_3_), channel_id=1, source_target_pairs={{0,4},{1,5},{2,6},{3,7},{4,8},{5,9},{6,10},{7,11},{8,12},{9,13},{1... | collective-permute-start | bytes 2211848 | tf_op jit(solution)/shard_map/ppermute | solution.py:24
  68.5 19.2 %collective-permute-start.17 = (bf16[2,5,96,384]{3,2,1,0:T(8,128)(2,1)}, bf16[2,5,96,384]{3,2,1,0:T(8,128)(2,1)}, u32[]{:S(2)}, u32[]{:S(2)}) collective-permute-start(bf16[2,5,96,384]{3,2,1,0:T(8,128)(2,1)} %collective-permute-done.11.refs_4_), channel_id=1, source_target_pairs={{0,28},{1,29},{2,30},{3,31},{4,0},{5,1},{6,2},{7,3},{8,4},{9,5},{1... | collective-permute-start | bytes 2211848 | tf_op jit(solution)/shard_map/ppermute | solution.py:24
  89.6 14.7 %collective-permute-start.23 = (bf16[1,5,96,384]{3,2,1,0:T(8,128)(2,1)}, bf16[1,5,96,384]{3,2,1,0:T(8,128)(2,1)S(1)}, u32[]{:S(2)}, u32[]{:S(2)}) collective-permute-start(bf16[1,5,96,384]{3,2,1,0:T(8,128)(2,1)} %get-tuple-element.93), channel_id=1, source_target_pairs={{0,4},{1,5},{2,6},{3,7},{4,8},{5,9},{6,10},{7,11},{8,12},{9,13},{1... | collective-permute-start | bytes 1105928 | tf_op jit(solution)/shard_map/ppermute | solution.py:24
  92.0 12.4 %collective-permute-start.24 = (bf16[1,5,96,384]{3,2,1,0:T(8,128)(2,1)}, bf16[1,5,96,384]{3,2,1,0:T(8,128)(2,1)}, u32[]{:S(2)}, u32[]{:S(2)}) collective-permute-start(bf16[1,5,96,384]{3,2,1,0:T(8,128)(2,1)} %get-tuple-element.94), channel_id=1, source_target_pairs={{0,28},{1,29},{2,30},{3,31},{4,0},{5,1},{6,2},{7,3},{8,4},{9,5},{1... | collective-permute-start | bytes 1105928 | tf_op jit(solution)/shard_map/ppermute | solution.py:24
  106.9 6.0 %collective-permute-start.26 = (bf16[256,384]{1,0:T(8,128)(2,1)S(1)}, bf16[256,384]{1,0:T(8,128)(2,1)S(1)}, u32[]{:S(2)}, u32[]{:S(2)}) collective-permute-start(bf16[256,384]{1,0:T(8,128)(2,1)S(1)} %get-tuple-element.100), channel_id=1, source_target_pairs={{0,2},{1,3},{2,0},{3,1},{4,6},{5,7},{6,4},{7,5},{8,10},{9,11},{10,... | collective-permute-start | bytes 589832 | tf_op jit(solution)/shard_map/ppermute | solution.py:19
  107.0 10.8 %collective-permute-start.27 = (bf16[256,384]{1,0:T(8,128)(2,1)S(1)}, bf16[256,384]{1,0:T(8,128)(2,1)S(1)}, u32[]{:S(2)}, u32[]{:S(2)}) collective-permute-start(bf16[256,384]{1,0:T(8,128)(2,1)S(1)} %get-tuple-element.101), channel_id=1, source_target_pairs={{0,3},{1,2},{2,1},{3,0},{4,7},{5,6},{6,5},{7,4},{8,11},{9,10},{10,... | collective-permute-start | bytes 589832 | tf_op jit(solution)/shard_map/ppermute | solution.py:19
  (22 other events, 558.3 us)

commit v7 on v6

--- a/solution.py
+++ b/solution.py
@@ -197,21 +197,27 @@
 
 
 def latent_kernel(own_ref, lin_ref, *refs):
-    pieces, hidden_ref, part_ref, total = refs[:4], refs[4], refs[5], refs[6]
-    step = pl.program_id(0)
+    pieces, hidden_ref, out_refs, part = refs[:4], refs[4], refs[5:-1], refs[-1]
+    width = pieces[0].shape[1]
+    total = None
     for m in range(4):
-
-        @pl.when(step == m)
-        def _(m=m):
-            piece = pieces[m][...]
-            hidden_ref[...] = piece
-            term = jnp.dot(piece, lin_ref[...], preferred_element_type=jnp.float32)
-            if m > 0:
-                term += total[...]
-            if m < 3:
-                total[...] = term
-            else:
-                part_ref[...] = term.astype(jnp.bfloat16)
+        at = pl.ds(pl.multiple_of((own_ref[0] ^ m) * width, width), width)
+        piece = pieces[m][...]
+        hidden_ref[:, at] = piece
+        term = jnp.dot(piece, lin_ref[at], preferred_element_type=jnp.float32)
+        total = term if total is None else total + term
+    part[...] = total
+    share = part.shape[0] // len(out_refs)
+    for m, ref in enumerate(out_refs):
+        ref[...] = part[pl.ds(pl.multiple_of((own_ref[1] ^ m) * share, share), share)].astype(ref.dtype)
+
+
+def rank_kernel(own_ref, lout_ref, *refs):
+    pieces, out_ref, latent = refs[:-2], refs[-2], refs[-1]
+    share = pieces[0].shape[0]
+    for m, ref in enumerate(pieces):
+        latent[pl.ds(pl.multiple_of((own_ref[1] ^ m) * share, share), share)] = ref[...]
+    out_ref[...] = jnp.dot(latent[...], lout_ref[...], preferred_element_type=jnp.float32).astype(out_ref.dtype)
 
 
 def per_device(tokens, gate_weight, up_weight, gate_scale, up_scale, partners, latent_in, latent_out):
@@ -310,32 +316,34 @@
     made = late(here, gs, us, w4, acc, windows, z_count, 0)
     hidden_pieces = [made[0], swapped(made[1], "tok", 1), *far_hidden]
     rank = latent_in.shape[1]
-    hidden, part = pl.pallas_call(
+    y_count = feat_count // 2
+    own = jnp.stack([member, feat // 2]).astype(jnp.int32)
+    hidden, *terms = pl.pallas_call(
         latent_kernel,
-        out_shape=(
-            jax.ShapeDtypeStruct((rows, features), jnp.bfloat16),
-            jax.ShapeDtypeStruct((rows, rank), jnp.bfloat16),
-        ),
-        grid_spec=pltpu.PrefetchScalarGridSpec(
-            num_scalar_prefetch=1,
-            grid=(4,),
-            in_specs=[pl.BlockSpec((half, rank), lambda m, own: (own[0] ^ m, 0))]
-            + [pl.BlockSpec((rows, half), lambda m, own: (0, 0))] * 4,
-            out_specs=[
-                pl.BlockSpec((rows, half), lambda m, own: (0, own[0] ^ m)),
-                pl.BlockSpec((rows, rank), lambda m, own: (0, 0)),
-            ],
-            scratch_shapes=[pltpu.VMEM((rows, rank), jnp.float32)],
-        ),
-        compiler_params=pltpu.CompilerParams(vmem_limit_bytes=VMEM_BYTES),
+        out_shape=[jax.ShapeDtypeStruct((rows, features), jnp.bfloat16)]
+        + [jax.ShapeDtypeStruct((rows // y_count, rank), jnp.bfloat16)] * y_count,
+        in_specs=[SMEM] + [VMEM] * 5,
+        out_specs=[VMEM] * (1 + y_count),
+        scratch_shapes=[pltpu.VMEM((rows, rank), jnp.float32)],
+        compiler_params=pltpu.CompilerParams(vmem_limit_bytes=SMALL_BYTES),
         cost_estimate=pl.CostEstimate(flops=2 * rows * features * rank, bytes_accessed=4 * 2**20, transcendentals=0),
     )(own, latent_in, *hidden_pieces)
 
-    parts = part.reshape(feat_count, rows // feat_count, -1)
-    terms = lax.all_to_all(parts, "feat", 0, 0)
-    mine = jnp.sum(terms.astype(jnp.float32), axis=0).astype(jnp.bfloat16)
-    latent = lax.all_to_all(jnp.broadcast_to(mine[None], parts.shape), "feat", 0, 0).reshape(rows, -1)
-    rank_term = jnp.dot(latent, latent_out, preferred_element_type=jnp.float32).astype(jnp.bfloat16)
+    def summed(values):
+        return sum(v.astype(jnp.float32) for v in values).astype(jnp.bfloat16)
+
+    mine = summed([terms[0]] + [swapped(terms[m], "feat", 2 * m) for m in range(1, y_count)])
+    mine = summed([mine, swapped(mine, "feat", 1)])
+    latents = [mine] + [swapped(mine, "feat", 2 * m) for m in range(1, y_count)]
+    rank_term = pl.pallas_call(
+        rank_kernel,
+        out_shape=jax.ShapeDtypeStruct((rows, features), jnp.bfloat16),
+        in_specs=[SMEM] + [VMEM] * (1 + y_count),
+        out_specs=VMEM,
+        scratch_shapes=[pltpu.VMEM((rows, rank), jnp.bfloat16)],
+        compiler_params=pltpu.CompilerParams(vmem_limit_bytes=SMALL_BYTES),
+        cost_estimate=pl.CostEstimate(flops=2 * rows * features * rank, bytes_accessed=4 * 2**20, transcendentals=0),
+    )(own, latent_out, *latents)
     return hidden, rank_term
 
 

time: 149 us -> 145 us (0.973)
  blocking collectives: 26.4 us -> 0 us
  waiting for transfers between devices: 42 us -> 56.3 us
  starting transfers between devices: 36.1 us -> 45.8 us
  matrix products: 1.66 us -> 0 us
  local copies, waits for them, and re-layouts: 2.21 us -> 3.71 us
    all_to_all x2 -> x0, blocking collectives: 26.4 us -> none  [the longest x1 14.6 us: per_device(): terms = lax.all_to_all(parts, 'feat', 0, 0)]
    ppermute x20 -> x27, waiting for transfers between devices: 24.3 us -> 38.4 us  [swapped(): lax.ppermute(value, axis, [(i, i ^ mask) for i in range(lax.axis_size(axi...]
    ppermute x20 -> x27, starting transfers between devices: 20.1 us -> 30.6 us  [swapped(): lax.ppermute(value, axis, [(i, i ^ mask) for i in range(lax.axis_size(axi...]
    unnamed x36 -> x44, local copies, waits for them, and re-layouts: 0.08 us -> 2.36 us
    pallas_call x1 -> x2, Pallas kernels: 2.5 us -> 4.38 us  [the longest x1 2.2 us: per_device(): pl.pallas_call(rank_kernel, out_shape=jax.ShapeDtypeStruct((rows, feature...]
    pallas_call x1, Pallas kernels: 1.88 us -> 0.06 us  [per_device(): pl.pallas_call(halves_kernel, grid=(1,), out_shape=[jax.ShapeDtypeStruct(...]
    dot_general x1 -> x0, matrix products: 1.66 us -> none  [per_device(): jnp.dot(latent, latent_out, preferred_element_type=jnp.float32)]
  transfers between devices with their start and end apart: 28 -> 35, of which waited for: 11 -> 16; matrix products, arithmetic and copies ran while one was open for 3% -> 2% of each run, Pallas kernels for 18% -> 19%
where the time goes in v7:
time: 145 us
  waiting for transfers between devices  56.3 us (39%)
  starting transfers between devices  45.8 us (32%)
  Pallas kernels  36.2 us (25%)
  local copies, waits for them, and re-layouts  3.71 us (3%)
  other arithmetic  2.06 us (1%)
    ppermute x27, waiting for transfers between devices, swapped(): lax.ppermute(value, axis, [(i, i ^ mask) for i in range(lax.axis_size(axi...  38.4 us
    ppermute x27, starting transfers between devices, swapped(): lax.ppermute(value, axis, [(i, i ^ mask) for i in range(lax.axis_size(axi...  30.6 us
    ppermute x8, waiting for transfers between devices, shifted(): lax.ppermute(value, 'tok', [(i, (i + step * GROUP) % count) for i in rang...  17.9 us
    ppermute x8, starting transfers between devices, shifted(): lax.ppermute(value, 'tok', [(i, (i + step * GROUP) % count) for i in rang...  15.2 us
    pallas_call x1, Pallas kernels, early(): pl.pallas_call(functools.partial(early_kernel, z_count=blk // share), out...  11.4 us
    pallas_call x1, Pallas kernels, lay(): pl.pallas_call(functools.partial(lay_kernel, z_count=blk // share, n_w=le...  10.7 us
    pallas_call x2, Pallas kernels, late(): pl.pallas_call(functools.partial(late_kernel, z_count=z_count), out_shape...  5.49 us
  transfers between devices with their start and end apart: 35, of which 16 were waited for; matrix products, arithmetic and copies ran while one was open for 2% of the time, Pallas kernels for 19%

profile of v7, /device:TPU:1, one launch (start us, length us, event | category | flops | bytes accessed | tf_op | source)
XLA Modules:
  0.0 144.9 jit_solution(5521992321163424640)
XLA Ops:
  2.8 3.2 %collective-permute-start = (bf16[2,5,24,384]{3,2,1,0:T(8,128)(2,1)}, bf16[2,5,24,384]{3,2,1,0:T(8,128)(2,1)S(1)}, u32[]{:S(2)}, u32[]{:S(2)}) collective-permute-start(bf16[2,5,24,384]{3,2,1,0:T(8,128)(2,1)} %get-tuple-element.57), channel_id=1, source_target_pairs={{0,1},{1,0},{2,3},{3,2},{4,5},{5,4},{6,7},{7,6},{8,9},{9,8},{10,11... | collective-permute-start | bytes 552968 | tf_op jit(solution)/shard_map/ppermute | solution.py:19
  12.6 4.3 %collective-permute-done.2.refs_3_ = bf16[2,5,24,384]{3,2,1,0:T(8,128)(2,1)S(1)} collective-permute-done((bf16[2,5,24,384]{3,2,1,0:T(8,128)(2,1)}, bf16[2,5,24,384]{3,2,1,0:T(8,128)(2,1)S(1)}, u32[]{:S(2)}, u32[]{:S(2)}) %collective-permute-start.2) | collective-permute-done | bytes 184352 | tf_op jit(solution)/shard_map/ppermute | solution.py:19
  20.8 3.9 %collective-permute-start.4 = (bf16[2,5,96,384]{3,2,1,0:T(8,128)(2,1)}, bf16[2,5,96,384]{3,2,1,0:T(8,128)(2,1)S(1)}, u32[]{:S(2)}, u32[]{:S(2)}) collective-permute-start(bf16[2,5,96,384]{3,2,1,0:T(8,128)(2,1)} %bitcast.10), channel_id=1, source_target_pairs={{0,28},{1,29},{2,30},{3,31},{4,0},{5,1},{6,2},{7,3},{8,4},{9,5},{1... | collective-permute-start | bytes 2211848 | tf_op jit(solution)/shard_map/ppermute | solution.py:24
  24.8 3.9 %collective-permute-done.7.refs_13_ = bf16[256,768]{1,0:T(8,128)(2,1)} collective-permute-done((bf16[256,768]{1,0:T(8,128)(2,1)S(1)}, bf16[256,768]{1,0:T(8,128)(2,1)}, u32[]{:S(2)}, u32[]{:S(2)}) %collective-permute-start.7) | collective-permute-done | bytes 393248 | tf_op jit(solution)/shard_map/ppermute | solution.py:19
  31.4 10.4 %collective-permute-done.3.refs_1_ = bf16[2,5,96,384]{3,2,1,0:T(8,128)(2,1)S(1)} collective-permute-done((bf16[2,5,96,384]{3,2,1,0:T(8,128)(2,1)}, bf16[2,5,96,384]{3,2,1,0:T(8,128)(2,1)S(1)}, u32[]{:S(2)}, u32[]{:S(2)}) %collective-permute-start.3) | collective-permute-done | bytes 737312 | tf_op jit(solution)/shard_map/ppermute | solution.py:24
  42.6 2.5 %collective-permute-start.12 = (bf16[512,768]{1,0:T(8,128)(2,1)S(1)}, bf16[512,768]{1,0:T(8,128)(2,1)}, u32[]{:S(2)}, u32[]{:S(2)}) collective-permute-start(bf16[512,768]{1,0:T(8,128)(2,1)S(1)} %pad_maximum_fusion), channel_id=1, source_target_pairs={{0,32},{32,0},{64,96},{96,64},{128,160},{160,128},{192,224},{224,1... | collective-permute-start | bytes 2359304 | tf_op jit(solution)/shard_map/ppermute | solution.py:19
  45.9 3.9 %collective-permute-start.11 = (bf16[2,5,96,384]{3,2,1,0:T(8,128)(2,1)S(1)}, bf16[2,5,96,384]{3,2,1,0:T(8,128)(2,1)}, u32[]{:S(2)}, u32[]{:S(2)}) collective-permute-start(bf16[2,5,96,384]{3,2,1,0:T(8,128)(2,1)S(1)} %collective-permute-done.4.refs_2_), channel_id=1, source_target_pairs={{0,28},{1,29},{2,30},{3,31},{4,0},{5,1},{6,2},{7,3},{8,4},{9,5},{1... | collective-permute-start | bytes 2211848 | tf_op jit(solution)/shard_map/ppermute | solution.py:24
  49.9 2.8 %collective-permute-start.13 = (bf16[256,768]{1,0:T(8,128)(2,1)S(1)}, bf16[256,768]{1,0:T(8,128)(2,1)}, u32[]{:S(2)}, u32[]{:S(2)}) collective-permute-start(bf16[256,768]{1,0:T(8,128)(2,1)S(1)} %collective-permute-done.5.refs_7_), channel_id=1, source_target_pairs={{0,128},{32,160},{64,192},{96,224},{128,0},{160,32},{192,64},{224,... | collective-permute-start | bytes 1179656 | tf_op jit(solution)/shard_map/ppermute | solution.py:19
  54.6 7.0 %collective-permute-done.13.refs_14_ = bf16[256,768]{1,0:T(8,128)(2,1)} collective-permute-done((bf16[256,768]{1,0:T(8,128)(2,1)S(1)}, bf16[256,768]{1,0:T(8,128)(2,1)}, u32[]{:S(2)}, u32[]{:S(2)}) %collective-permute-start.13) | collective-permute-done | bytes 393248 | tf_op jit(solution)/shard_map/ppermute | solution.py:19
  61.6 5.0 %collective-permute-done.10.refs_3_ = bf16[2,5,96,384]{3,2,1,0:T(8,128)(2,1)} collective-permute-done((bf16[2,5,96,384]{3,2,1,0:T(8,128)(2,1)S(1)}, bf16[2,5,96,384]{3,2,1,0:T(8,128)(2,1)}, u32[]{:S(2)}, u32[]{:S(2)}) %collective-permute-start.10) | collective-permute-done | bytes 737312 | tf_op jit(solution)/shard_map/ppermute | solution.py:24
  68.1 2.7 %collective-permute-start.17 = (bf16[2,5,96,384]{3,2,1,0:T(8,128)(2,1)}, bf16[2,5,96,384]{3,2,1,0:T(8,128)(2,1)S(1)}, u32[]{:S(2)}, u32[]{:S(2)}) collective-permute-start(bf16[2,5,96,384]{3,2,1,0:T(8,128)(2,1)} %collective-permute-done.11.refs_4_), channel_id=1, source_target_pairs={{0,28},{1,29},{2,30},{3,31},{4,0},{5,1},{6,2},{7,3},{8,4},{9,5},{1... | collective-permute-start | bytes 2211848 | tf_op jit(solution)/shard_map/ppermute | solution.py:24
  74.1 10.7 %shard_map.106 = (bf16[5,1024,768]{2,1,0:T(8,128)(2,1)}, bf16[5,1024,256]{2,1,0:T(8,128)(2,1)}, bf16[5,768,768]{2,1,0:T(8,128)(2,1)}) custom-call(s32[7]{0:T(128)} %pad_add_fusion.1.place_ref, bf16[2,5,96,384]{3,2,1,0:T(8,128)(2,1)} %bitcast.11, bf16[2,5,96,384]{3,2,1,0:T(8,128)(2,1)} %copy-done.12, bf16[2,5,96,384]{3,2,1,0:T(8,128)(2,1)} %copy-done.13, ...), custom_call_target="tpu_custom_call" | custom-call | flops 1048576 | bytes 1048576 | tf_op jit(solution)/shard_map/pallas_call | solution.py:94
  84.8 2.5 %collective-permute-done.16.f_ref.below_ref = bf16[2,5,96,384]{3,2,1,0:T(8,128)(2,1)S(1)} collective-permute-done((bf16[2,5,96,384]{3,2,1,0:T(8,128)(2,1)}, bf16[2,5,96,384]{3,2,1,0:T(8,128)(2,1)S(1)}, u32[]{:S(2)}, u32[]{:S(2)}) %collective-permute-start.16) | collective-permute-done | bytes 737312 | tf_op jit(solution)/shard_map/ppermute | solution.py:24
  90.1 11.4 %shard_map.108.acc_ref = f32[1024,768]{1,0:T(8,128)S(1)} custom-call(s32[7]{0:T(128)S(1)} %copy-done.6, f32[5]{0:T(128)S(1)} %get-tuple-element.112.gs_ref, f32[5]{0:T(128)S(1)} %get-tuple-element.113.us_ref, bf16[5,1024,768]{2,1,0:T(8,128)(2,1)} %get-tuple-element.98.x_ref, bf16[5,768,768]{2,1,0:T(8,128)(2,1)} %get-tuple-element.99.w_ref, ...), custom_call_target="tpu_custom_call" | custom-call | flops 1048576 | bytes 1048576 | tf_op jit(solution)/shard_map/pallas_call | solution.py:135
  101.6 2.7 %shard_map.110 = (bf16[256,384]{1,0:T(8,128)(2,1)}, bf16[256,384]{1,0:T(8,128)(2,1)}) custom-call(s32[7]{0:T(128)S(1)} %copy-done.6, f32[5]{0:T(128)S(1)} %get-tuple-element.112.gs_ref, f32[5]{0:T(128)S(1)} %get-tuple-element.113.us_ref, bf16[1,5,96,384]{3,2,1,0:T(8,128)(2,1)S(1)} %collective-permute-done.23.g_ref, ...), custom_call_target="tpu_custom_call" | custom-call | flops 1006632960 | bytes 4194304 | tf_op jit(solution)/shard_map/pallas_call | solution.py:177
  104.3 3.3 %collective-permute-start.27 = (bf16[256,384]{1,0:T(8,128)(2,1)}, bf16[256,384]{1,0:T(8,128)(2,1)S(1)}, u32[]{:S(2)}, u32[]{:S(2)}) collective-permute-start(bf16[256,384]{1,0:T(8,128)(2,1)} %get-tuple-element.104), channel_id=1, source_target_pairs={{0,3},{1,2},{2,1},{3,0},{4,7},{5,6},{6,5},{7,4},{8,11},{9,10},{10,... | collective-permute-start | bytes 589832 | tf_op jit(solution)/shard_map/ppermute | solution.py:19
  107.6 2.7 %shard_map.109 = (bf16[256,384]{1,0:T(8,128)(2,1)S(1)}, bf16[256,384]{1,0:T(8,128)(2,1)}) custom-call(s32[7]{0:T(128)S(1)} %copy-done.6, f32[5]{0:T(128)S(1)} %get-tuple-element.112.gs_ref, f32[5]{0:T(128)S(1)} %get-tuple-element.113.us_ref, bf16[1,5,96,384]{3,2,1,0:T(8,128)(2,1)S(1)} %collective-permute-done.23.g_ref, ...), custom_call_target="tpu_custom_call" | custom-call | flops 1006632960 | bytes 4194304 | tf_op jit(solution)/shard_map/pallas_call | solution.py:177
  111.1 4.3 %collective-permute-done.27.refs_3_ = bf16[256,384]{1,0:T(8,128)(2,1)S(1)} collective-permute-done((bf16[256,384]{1,0:T(8,128)(2,1)}, bf16[256,384]{1,0:T(8,128)(2,1)S(1)}, u32[]{:S(2)}, u32[]{:S(2)}) %collective-permute-start.27) | collective-permute-done | bytes 196640 | tf_op jit(solution)/shard_map/ppermute | solution.py:19
  119.7 2.6 %collective-permute-start.29 = (bf16[64,768]{1,0:T(8,128)(2,1)S(1)}, bf16[64,768]{1,0:T(8,128)(2,1)S(1)}, u32[]{:S(2)}, u32[]{:S(2)}) collective-permute-start(bf16[64,768]{1,0:T(8,128)(2,1)S(1)} %get-tuple-element.108), channel_id=1, source_target_pairs={{0,128},{32,160},{64,192},{96,224},{128,0},{160,32},{192,64},{224,... | collective-permute-start | bytes 294920 | tf_op jit(solution)/shard_map/ppermute | solution.py:19
  122.3 4.3 %collective-permute-done.29 = bf16[64,768]{1,0:T(8,128)(2,1)S(1)} collective-permute-done((bf16[64,768]{1,0:T(8,128)(2,1)S(1)}, bf16[64,768]{1,0:T(8,128)(2,1)S(1)}, u32[]{:S(2)}, u32[]{:S(2)}) %collective-permute-start.29) | collective-permute-done | bytes 98336 | tf_op jit(solution)/shard_map/ppermute | solution.py:19
  126.6 2.3 %collective-permute-done.30 = bf16[64,768]{1,0:T(8,128)(2,1)S(1)} collective-permute-done((bf16[64,768]{1,0:T(8,128)(2,1)S(1)}, bf16[64,768]{1,0:T(8,128)(2,1)S(1)}, u32[]{:S(2)}, u32[]{:S(2)}) %collective-permute-start.30) | collective-permute-done | bytes 98336 | tf_op jit(solution)/shard_map/ppermute | solution.py:19
  128.9 2.2 %collective-permute-start.31 = (bf16[64,768]{1,0:T(8,128)(2,1)S(1)}, bf16[64,768]{1,0:T(8,128)(2,1)S(1)}, u32[]{:S(2)}, u32[]{:S(2)}) collective-permute-start(bf16[64,768]{1,0:T(8,128)(2,1)S(1)} %add_convert_fusion.1), channel_id=1, source_target_pairs={{0,32},{32,0},{64,96},{96,64},{128,160},{160,128},{192,224},{224,1... | collective-permute-start | bytes 294920 | tf_op jit(solution)/shard_map/ppermute | solution.py:19
  131.2 3.4 %collective-permute-done.31 = bf16[64,768]{1,0:T(8,128)(2,1)S(1)} collective-permute-done((bf16[64,768]{1,0:T(8,128)(2,1)S(1)}, bf16[64,768]{1,0:T(8,128)(2,1)S(1)}, u32[]{:S(2)}, u32[]{:S(2)}) %collective-permute-start.31) | collective-permute-done | bytes 98336 | tf_op jit(solution)/shard_map/ppermute | solution.py:19
  136.2 2.3 %collective-permute-start.34 = (bf16[64,768]{1,0:T(8,128)(2,1)S(1)}, bf16[64,768]{1,0:T(8,128)(2,1)S(1)}, u32[]{:S(2)}, u32[]{:S(2)}) collective-permute-start(bf16[64,768]{1,0:T(8,128)(2,1)S(1)} %add_convert_fusion.refs_0_), channel_id=1, source_target_pairs={{0,192},{32,224},{64,128},{96,160},{128,64},{160,96},{192,0},{224,... | collective-permute-start | bytes 294920 | tf_op jit(solution)/shard_map/ppermute | solution.py:19
  (110 shorter events, 39.8 us)
Async XLA Ops:
  2.8 8.3 %collective-permute-start = (bf16[2,5,24,384]{3,2,1,0:T(8,128)(2,1)}, bf16[2,5,24,384]{3,2,1,0:T(8,128)(2,1)S(1)}, u32[]{:S(2)}, u32[]{:S(2)}) collective-permute-start(bf16[2,5,24,384]{3,2,1,0:T(8,128)(2,1)} %get-tuple-element.57), channel_id=1, source_target_pairs={{0,1},{1,0},{2,3},{3,2},{4,5},{5,4},{6,7},{7,6},{8,9},{9,8},{10,11... | collective-permute-start | bytes 552968 | tf_op jit(solution)/shard_map/ppermute | solution.py:19
  6.0 6.6 %collective-permute-start.1 = (bf16[2,5,24,384]{3,2,1,0:T(8,128)(2,1)}, bf16[2,5,24,384]{3,2,1,0:T(8,128)(2,1)S(1)}, u32[]{:S(2)}, u32[]{:S(2)}) collective-permute-start(bf16[2,5,24,384]{3,2,1,0:T(8,128)(2,1)} %get-tuple-element.58), channel_id=1, source_target_pairs={{0,2},{1,3},{2,0},{3,1},{4,6},{5,7},{6,4},{7,5},{8,10},{9,11},{10,... | collective-permute-start | bytes 552968 | tf_op jit(solution)/shard_map/ppermute | solution.py:19
  6.0 10.9 %collective-permute-start.2 = (bf16[2,5,24,384]{3,2,1,0:T(8,128)(2,1)}, bf16[2,5,24,384]{3,2,1,0:T(8,128)(2,1)S(1)}, u32[]{:S(2)}, u32[]{:S(2)}) collective-permute-start(bf16[2,5,24,384]{3,2,1,0:T(8,128)(2,1)} %get-tuple-element.59), channel_id=1, source_target_pairs={{0,3},{1,2},{2,1},{3,0},{4,7},{5,6},{6,5},{7,4},{8,11},{9,10},{10,... | collective-permute-start | bytes 552968 | tf_op jit(solution)/shard_map/ppermute | solution.py:19
  8.8 16.0 %collective-permute-start.6 = (bf16[256,768]{1,0:T(8,128)(2,1)S(1)}, bf16[256,768]{1,0:T(8,128)(2,1)}, u32[]{:S(2)}, u32[]{:S(2)}) collective-permute-start(bf16[256,768]{1,0:T(8,128)(2,1)S(1)} %get-tuple-element.69), channel_id=1, source_target_pairs={{0,64},{32,96},{64,0},{96,32},{128,192},{160,224},{192,128},{224,1... | collective-permute-start | bytes 1179656 | tf_op jit(solution)/shard_map/ppermute | solution.py:19
  8.9 19.7 %collective-permute-start.7 = (bf16[256,768]{1,0:T(8,128)(2,1)S(1)}, bf16[256,768]{1,0:T(8,128)(2,1)}, u32[]{:S(2)}, u32[]{:S(2)}) collective-permute-start(bf16[256,768]{1,0:T(8,128)(2,1)S(1)} %get-tuple-element.69), channel_id=1, source_target_pairs={{0,128},{32,160},{64,192},{96,224},{128,0},{160,32},{192,64},{224,... | collective-permute-start | bytes 1179656 | tf_op jit(solution)/shard_map/ppermute | solution.py:19
  19.7 10.8 %collective-permute-start.5 = (bf16[256,768]{1,0:T(8,128)(2,1)S(1)}, bf16[256,768]{1,0:T(8,128)(2,1)S(1)}, u32[]{:S(2)}, u32[]{:S(2)}) collective-permute-start(bf16[256,768]{1,0:T(8,128)(2,1)S(1)} %get-tuple-element.61), channel_id=1, source_target_pairs={{0,2},{1,3},{2,0},{3,1},{4,6},{5,7},{6,4},{7,5},{8,10},{9,11},{10,... | collective-permute-start | bytes 1179656 | tf_op jit(solution)/shard_map/ppermute | solution.py:19
  19.8 22.0 %collective-permute-start.3 = (bf16[2,5,96,384]{3,2,1,0:T(8,128)(2,1)}, bf16[2,5,96,384]{3,2,1,0:T(8,128)(2,1)S(1)}, u32[]{:S(2)}, u32[]{:S(2)}) collective-permute-start(bf16[2,5,96,384]{3,2,1,0:T(8,128)(2,1)} %bitcast.9), channel_id=1, source_target_pairs={{0,4},{1,5},{2,6},{3,7},{4,8},{5,9},{6,10},{7,11},{8,12},{9,13},{1... | collective-permute-start | bytes 2211848 | tf_op jit(solution)/shard_map/ppermute | solution.py:24
  20.8 20.9 %collective-permute-start.4 = (bf16[2,5,96,384]{3,2,1,0:T(8,128)(2,1)}, bf16[2,5,96,384]{3,2,1,0:T(8,128)(2,1)S(1)}, u32[]{:S(2)}, u32[]{:S(2)}) collective-permute-start(bf16[2,5,96,384]{3,2,1,0:T(8,128)(2,1)} %bitcast.10), channel_id=1, source_target_pairs={{0,28},{1,29},{2,30},{3,31},{4,0},{5,1},{6,2},{7,3},{8,4},{9,5},{1... | collective-permute-start | bytes 2211848 | tf_op jit(solution)/shard_map/ppermute | solution.py:24
  30.6 11.2 %collective-permute-start.8 = (bf16[256,768]{1,0:T(8,128)(2,1)S(1)}, bf16[256,768]{1,0:T(8,128)(2,1)S(1)}, u32[]{:S(2)}, u32[]{:S(2)}) collective-permute-start(bf16[256,768]{1,0:T(8,128)(2,1)S(1)} %get-tuple-element.69), channel_id=1, source_target_pairs={{0,2},{1,3},{2,0},{3,1},{4,6},{5,7},{6,4},{7,5},{8,10},{9,11},{10,... | collective-permute-start | bytes 1179656 | tf_op jit(solution)/shard_map/ppermute | solution.py:19
  30.6 11.2 %collective-permute-start.9 = (bf16[256,768]{1,0:T(8,128)(2,1)S(1)}, bf16[256,768]{1,0:T(8,128)(2,1)S(1)}, u32[]{:S(2)}, u32[]{:S(2)}) collective-permute-start(bf16[256,768]{1,0:T(8,128)(2,1)S(1)} %collective-permute-done.5.refs_7_), channel_id=1, source_target_pairs={{0,64},{32,96},{64,0},{96,32},{128,192},{160,224},{192,128},{224,1... | collective-permute-start | bytes 1179656 | tf_op jit(solution)/shard_map/ppermute | solution.py:19
  41.8 10.9 %collective-permute-start.14 = (bf16[256,1536]{1,0:T(8,128)(2,1)S(1)}, bf16[256,1536]{1,0:T(8,128)(2,1)S(1)}, u32[]{:S(2)}, u32[]{:S(2)}) collective-permute-start(bf16[256,1536]{1,0:T(8,128)(2,1)S(1)} %copy-done.8), channel_id=1, source_target_pairs={{0,1},{1,0},{2,3},{3,2},{4,5},{5,4},{6,7},{7,6},{8,9},{9,8},{10,11... | collective-permute-start | bytes 2359304 | tf_op jit(solution)/shard_map/ppermute | solution.py:19
  42.6 24.0 %collective-permute-start.12 = (bf16[512,768]{1,0:T(8,128)(2,1)S(1)}, bf16[512,768]{1,0:T(8,128)(2,1)}, u32[]{:S(2)}, u32[]{:S(2)}) collective-permute-start(bf16[512,768]{1,0:T(8,128)(2,1)S(1)} %pad_maximum_fusion), channel_id=1, source_target_pairs={{0,32},{32,0},{64,96},{96,64},{128,160},{160,128},{192,224},{224,1... | collective-permute-start | bytes 2359304 | tf_op jit(solution)/shard_map/ppermute | solution.py:19
  45.2 21.5 %collective-permute-start.10 = (bf16[2,5,96,384]{3,2,1,0:T(8,128)(2,1)S(1)}, bf16[2,5,96,384]{3,2,1,0:T(8,128)(2,1)}, u32[]{:S(2)}, u32[]{:S(2)}) collective-permute-start(bf16[2,5,96,384]{3,2,1,0:T(8,128)(2,1)S(1)} %collective-permute-done.3.refs_1_), channel_id=1, source_target_pairs={{0,4},{1,5},{2,6},{3,7},{4,8},{5,9},{6,10},{7,11},{8,12},{9,13},{1... | collective-permute-start | bytes 2211848 | tf_op jit(solution)/shard_map/ppermute | solution.py:24
  45.9 20.7 %collective-permute-start.11 = (bf16[2,5,96,384]{3,2,1,0:T(8,128)(2,1)S(1)}, bf16[2,5,96,384]{3,2,1,0:T(8,128)(2,1)}, u32[]{:S(2)}, u32[]{:S(2)}) collective-permute-start(bf16[2,5,96,384]{3,2,1,0:T(8,128)(2,1)S(1)} %collective-permute-done.4.refs_2_), channel_id=1, source_target_pairs={{0,28},{1,29},{2,30},{3,31},{4,0},{5,1},{6,2},{7,3},{8,4},{9,5},{1... | collective-permute-start | bytes 2211848 | tf_op jit(solution)/shard_map/ppermute | solution.py:24
  49.9 11.7 %collective-permute-start.13 = (bf16[256,768]{1,0:T(8,128)(2,1)S(1)}, bf16[256,768]{1,0:T(8,128)(2,1)}, u32[]{:S(2)}, u32[]{:S(2)}) collective-permute-start(bf16[256,768]{1,0:T(8,128)(2,1)S(1)} %collective-permute-done.5.refs_7_), channel_id=1, source_target_pairs={{0,128},{32,160},{64,192},{96,224},{128,0},{160,32},{192,64},{224,... | collective-permute-start | bytes 1179656 | tf_op jit(solution)/shard_map/ppermute | solution.py:19
  52.7 14.0 %collective-permute-start.15 = (bf16[256,768]{1,0:T(8,128)(2,1)S(1)}, bf16[256,768]{1,0:T(8,128)(2,1)}, u32[]{:S(2)}, u32[]{:S(2)}) collective-permute-start(bf16[256,768]{1,0:T(8,128)(2,1)S(1)} %collective-permute-done.8.refs_8_), channel_id=1, source_target_pairs={{0,1},{1,0},{2,3},{3,2},{4,5},{5,4},{6,7},{7,6},{8,9},{9,8},{10,11... | collective-permute-start | bytes 1179656 | tf_op jit(solution)/shard_map/ppermute | solution.py:19
  68.0 19.2 %collective-permute-start.16 = (bf16[2,5,96,384]{3,2,1,0:T(8,128)(2,1)}, bf16[2,5,96,384]{3,2,1,0:T(8,128)(2,1)S(1)}, u32[]{:S(2)}, u32[]{:S(2)}) collective-permute-start(bf16[2,5,96,384]{3,2,1,0:T(8,128)(2,1)} %collective-permute-done.10.refs_3_), channel_id=1, source_target_pairs={{0,4},{1,5},{2,6},{3,7},{4,8},{5,9},{6,10},{7,11},{8,12},{9,13},{1... | collective-permute-start | bytes 2211848 | tf_op jit(solution)/shard_map/ppermute | solution.py:24
  68.1 19.2 %collective-permute-start.17 = (bf16[2,5,96,384]{3,2,1,0:T(8,128)(2,1)}, bf16[2,5,96,384]{3,2,1,0:T(8,128)(2,1)S(1)}, u32[]{:S(2)}, u32[]{:S(2)}) collective-permute-start(bf16[2,5,96,384]{3,2,1,0:T(8,128)(2,1)} %collective-permute-done.11.refs_4_), channel_id=1, source_target_pairs={{0,28},{1,29},{2,30},{3,31},{4,0},{5,1},{6,2},{7,3},{8,4},{9,5},{1... | collective-permute-start | bytes 2211848 | tf_op jit(solution)/shard_map/ppermute | solution.py:24
  87.3 14.2 %collective-permute-start.23 = (bf16[1,5,96,384]{3,2,1,0:T(8,128)(2,1)S(1)}, bf16[1,5,96,384]{3,2,1,0:T(8,128)(2,1)S(1)}, u32[]{:S(2)}, u32[]{:S(2)}) collective-permute-start(bf16[1,5,96,384]{3,2,1,0:T(8,128)(2,1)S(1)} %get-tuple-element.96), channel_id=1, source_target_pairs={{0,4},{1,5},{2,6},{3,7},{4,8},{5,9},{6,10},{7,11},{8,12},{9,13},{1... | collective-permute-start | bytes 1105928 | tf_op jit(solution)/shard_map/ppermute | solution.py:24
  89.5 12.0 %collective-permute-start.24 = (bf16[1,5,96,384]{3,2,1,0:T(8,128)(2,1)S(1)}, bf16[1,5,96,384]{3,2,1,0:T(8,128)(2,1)S(1)}, u32[]{:S(2)}, u32[]{:S(2)}) collective-permute-start(bf16[1,5,96,384]{3,2,1,0:T(8,128)(2,1)S(1)} %get-tuple-element.97), channel_id=1, source_target_pairs={{0,28},{1,29},{2,30},{3,31},{4,0},{5,1},{6,2},{7,3},{8,4},{9,5},{1... | collective-permute-start | bytes 1105928 | tf_op jit(solution)/shard_map/ppermute | solution.py:24
  104.3 6.8 %collective-permute-start.26 = (bf16[256,384]{1,0:T(8,128)(2,1)}, bf16[256,384]{1,0:T(8,128)(2,1)S(1)}, u32[]{:S(2)}, u32[]{:S(2)}) collective-permute-start(bf16[256,384]{1,0:T(8,128)(2,1)} %get-tuple-element.103), channel_id=1, source_target_pairs={{0,2},{1,3},{2,0},{3,1},{4,6},{5,7},{6,4},{7,5},{8,10},{9,11},{10,... | collective-permute-start | bytes 589832 | tf_op jit(solution)/shard_map/ppermute | solution.py:19
  104.3 11.0 %collective-permute-start.27 = (bf16[256,384]{1,0:T(8,128)(2,1)}, bf16[256,384]{1,0:T(8,128)(2,1)S(1)}, u32[]{:S(2)}, u32[]{:S(2)}) collective-permute-start(bf16[256,384]{1,0:T(8,128)(2,1)} %get-tuple-element.104), channel_id=1, source_target_pairs={{0,3},{1,2},{2,1},{3,0},{4,7},{5,6},{6,5},{7,4},{8,11},{9,10},{10,... | collective-permute-start | bytes 589832 | tf_op jit(solution)/shard_map/ppermute | solution.py:19
  119.7 6.9 %collective-permute-start.29 = (bf16[64,768]{1,0:T(8,128)(2,1)S(1)}, bf16[64,768]{1,0:T(8,128)(2,1)S(1)}, u32[]{:S(2)}, u32[]{:S(2)}) collective-permute-start(bf16[64,768]{1,0:T(8,128)(2,1)S(1)} %get-tuple-element.108), channel_id=1, source_target_pairs={{0,128},{32,160},{64,192},{96,224},{128,0},{160,32},{192,64},{224,... | collective-permute-start | bytes 294920 | tf_op jit(solution)/shard_map/ppermute | solution.py:19
  122.3 6.6 %collective-permute-start.30 = (bf16[64,768]{1,0:T(8,128)(2,1)S(1)}, bf16[64,768]{1,0:T(8,128)(2,1)S(1)}, u32[]{:S(2)}, u32[]{:S(2)}) collective-permute-start(bf16[64,768]{1,0:T(8,128)(2,1)S(1)} %get-tuple-element.109), channel_id=1, source_target_pairs={{0,192},{32,224},{64,128},{96,160},{128,64},{160,96},{192,0},{224,... | collective-permute-start | bytes 294920 | tf_op jit(solution)/shard_map/ppermute | solution.py:19
  (33 other events, 501.8 us)

commit v8 on v7

--- a/solution.py
+++ b/solution.py
@@ -281,9 +281,9 @@
     w2 = step(*w1)
     p_x = swapped(jnp.concatenate([first, s2_own]), "feat", 1)
     p2_y2 = swapped(s2_own, "feat", 4)
+    s3_other = swapped(s2_other, "tok", 1)
+    s3_other, later = barrier((s3_other, later))
     s1 = swapped(later, "tok", 1)
-    s1, s2_other = barrier((s1, s2_other))
-    s3_other = swapped(s2_other, "tok", 1)
     p_y1 = jnp.concatenate([p0_y1, p2_y1])
     w2, p_x, p2_y2, p0_y2, p_y1, s2_own, s1, s3_other = barrier((w2, p_x, p2_y2, p0_y2, p_y1, s2_own, s1, s3_other))
     w3 = step(*w2)

time: 145 us -> 146 us (level)
  no operation moved by 1% of the time
where the time goes in v8:
time: 146 us
  waiting for transfers between devices  57.5 us (39%)
  starting transfers between devices  45.3 us (31%)
  Pallas kernels  36.2 us (25%)
  local copies, waits for them, and re-layouts  3.7 us (3%)
  other arithmetic  2.02 us (1%)
    ppermute x27, waiting for transfers between devices, swapped(): lax.ppermute(value, axis, [(i, i ^ mask) for i in range(lax.axis_size(axi...  39.6 us
    ppermute x27, starting transfers between devices, swapped(): lax.ppermute(value, axis, [(i, i ^ mask) for i in range(lax.axis_size(axi...  30.1 us
    ppermute x8, waiting for transfers between devices, shifted(): lax.ppermute(value, 'tok', [(i, (i + step * GROUP) % count) for i in rang...  18 us
    ppermute x8, starting transfers between devices, shifted(): lax.ppermute(value, 'tok', [(i, (i + step * GROUP) % count) for i in rang...  15.2 us
    pallas_call x1, Pallas kernels, early(): pl.pallas_call(functools.partial(early_kernel, z_count=blk // share), out...  11.4 us
    pallas_call x1, Pallas kernels, lay(): pl.pallas_call(functools.partial(lay_kernel, z_count=blk // share, n_w=le...  10.7 us
    pallas_call x2, Pallas kernels, late(): pl.pallas_call(functools.partial(late_kernel, z_count=z_count), out_shape...  5.49 us
  transfers between devices with their start and end apart: 35, of which 16 were waited for; matrix products, arithmetic and copies ran while one was open for 2% of the time, Pallas kernels for 19%

profile of v8, /device:TPU:1, one launch (start us, length us, event | category | flops | bytes accessed | tf_op | source)
XLA Modules:
  0.0 145.6 jit_solution(1219986987601976845)
XLA Ops:
  2.7 3.2 %collective-permute-start = (bf16[2,5,24,384]{3,2,1,0:T(8,128)(2,1)}, bf16[2,5,24,384]{3,2,1,0:T(8,128)(2,1)S(1)}, u32[]{:S(2)}, u32[]{:S(2)}) collective-permute-start(bf16[2,5,24,384]{3,2,1,0:T(8,128)(2,1)} %get-tuple-element.57), channel_id=1, source_target_pairs={{0,1},{1,0},{2,3},{3,2},{4,5},{5,4},{6,7},{7,6},{8,9},{9,8},{10,11... | collective-permute-start | bytes 552968 | tf_op jit(solution)/shard_map/ppermute | solution.py:19
  12.4 4.4 %collective-permute-done.2.refs_3_ = bf16[2,5,24,384]{3,2,1,0:T(8,128)(2,1)S(1)} collective-permute-done((bf16[2,5,24,384]{3,2,1,0:T(8,128)(2,1)}, bf16[2,5,24,384]{3,2,1,0:T(8,128)(2,1)S(1)}, u32[]{:S(2)}, u32[]{:S(2)}) %collective-permute-start.2) | collective-permute-done | bytes 184352 | tf_op jit(solution)/shard_map/ppermute | solution.py:19
  20.8 3.9 %collective-permute-start.4 = (bf16[2,5,96,384]{3,2,1,0:T(8,128)(2,1)}, bf16[2,5,96,384]{3,2,1,0:T(8,128)(2,1)S(1)}, u32[]{:S(2)}, u32[]{:S(2)}) collective-permute-start(bf16[2,5,96,384]{3,2,1,0:T(8,128)(2,1)} %bitcast.10), channel_id=1, source_target_pairs={{0,28},{1,29},{2,30},{3,31},{4,0},{5,1},{6,2},{7,3},{8,4},{9,5},{1... | collective-permute-start | bytes 2211848 | tf_op jit(solution)/shard_map/ppermute | solution.py:24
  24.7 3.9 %collective-permute-done.7.refs_13_ = bf16[256,768]{1,0:T(8,128)(2,1)S(1)} collective-permute-done((bf16[256,768]{1,0:T(8,128)(2,1)S(1)}, bf16[256,768]{1,0:T(8,128)(2,1)S(1)}, u32[]{:S(2)}, u32[]{:S(2)}) %collective-permute-start.7) | collective-permute-done | bytes 393248 | tf_op jit(solution)/shard_map/ppermute | solution.py:19
  31.3 10.4 %collective-permute-done.3.refs_1_ = bf16[2,5,96,384]{3,2,1,0:T(8,128)(2,1)S(1)} collective-permute-done((bf16[2,5,96,384]{3,2,1,0:T(8,128)(2,1)}, bf16[2,5,96,384]{3,2,1,0:T(8,128)(2,1)S(1)}, u32[]{:S(2)}, u32[]{:S(2)}) %collective-permute-start.3) | collective-permute-done | bytes 737312 | tf_op jit(solution)/shard_map/ppermute | solution.py:24
  42.5 2.5 %collective-permute-start.12 = (bf16[512,768]{1,0:T(8,128)(2,1)S(1)}, bf16[512,768]{1,0:T(8,128)(2,1)}, u32[]{:S(2)}, u32[]{:S(2)}) collective-permute-start(bf16[512,768]{1,0:T(8,128)(2,1)S(1)} %pad_maximum_fusion), channel_id=1, source_target_pairs={{0,32},{32,0},{64,96},{96,64},{128,160},{160,128},{192,224},{224,1... | collective-permute-start | bytes 2359304 | tf_op jit(solution)/shard_map/ppermute | solution.py:19
  46.2 3.9 %collective-permute-start.11 = (bf16[2,5,96,384]{3,2,1,0:T(8,128)(2,1)S(1)}, bf16[2,5,96,384]{3,2,1,0:T(8,128)(2,1)}, u32[]{:S(2)}, u32[]{:S(2)}) collective-permute-start(bf16[2,5,96,384]{3,2,1,0:T(8,128)(2,1)S(1)} %collective-permute-done.4.refs_2_), channel_id=1, source_target_pairs={{0,28},{1,29},{2,30},{3,31},{4,0},{5,1},{6,2},{7,3},{8,4},{9,5},{1... | collective-permute-start | bytes 2211848 | tf_op jit(solution)/shard_map/ppermute | solution.py:24
  50.1 2.9 %collective-permute-start.13 = (bf16[256,768]{1,0:T(8,128)(2,1)S(1)}, bf16[256,768]{1,0:T(8,128)(2,1)}, u32[]{:S(2)}, u32[]{:S(2)}) collective-permute-start(bf16[256,768]{1,0:T(8,128)(2,1)S(1)} %collective-permute-done.5.refs_7_), channel_id=1, source_target_pairs={{0,128},{32,160},{64,192},{96,224},{128,0},{160,32},{192,64},{224,... | collective-permute-start | bytes 1179656 | tf_op jit(solution)/shard_map/ppermute | solution.py:19
  54.1 7.8 %collective-permute-done.13.refs_14_ = bf16[256,768]{1,0:T(8,128)(2,1)} collective-permute-done((bf16[256,768]{1,0:T(8,128)(2,1)S(1)}, bf16[256,768]{1,0:T(8,128)(2,1)}, u32[]{:S(2)}, u32[]{:S(2)}) %collective-permute-start.13) | collective-permute-done | bytes 393248 | tf_op jit(solution)/shard_map/ppermute | solution.py:19
  61.9 5.0 %collective-permute-done.10.refs_3_ = bf16[2,5,96,384]{3,2,1,0:T(8,128)(2,1)} collective-permute-done((bf16[2,5,96,384]{3,2,1,0:T(8,128)(2,1)S(1)}, bf16[2,5,96,384]{3,2,1,0:T(8,128)(2,1)}, u32[]{:S(2)}, u32[]{:S(2)}) %collective-permute-start.10) | collective-permute-done | bytes 737312 | tf_op jit(solution)/shard_map/ppermute | solution.py:24
  68.8 2.5 %collective-permute-start.17 = (bf16[2,5,96,384]{3,2,1,0:T(8,128)(2,1)}, bf16[2,5,96,384]{3,2,1,0:T(8,128)(2,1)S(1)}, u32[]{:S(2)}, u32[]{:S(2)}) collective-permute-start(bf16[2,5,96,384]{3,2,1,0:T(8,128)(2,1)} %collective-permute-done.11.refs_4_), channel_id=1, source_target_pairs={{0,28},{1,29},{2,30},{3,31},{4,0},{5,1},{6,2},{7,3},{8,4},{9,5},{1... | collective-permute-start | bytes 2211848 | tf_op jit(solution)/shard_map/ppermute | solution.py:24
  74.6 10.7 %shard_map.106 = (bf16[5,1024,768]{2,1,0:T(8,128)(2,1)}, bf16[5,1024,256]{2,1,0:T(8,128)(2,1)}, bf16[5,768,768]{2,1,0:T(8,128)(2,1)}) custom-call(s32[7]{0:T(128)} %pad_add_fusion.1.place_ref, bf16[2,5,96,384]{3,2,1,0:T(8,128)(2,1)} %bitcast.11, bf16[2,5,96,384]{3,2,1,0:T(8,128)(2,1)} %copy-done.12, bf16[2,5,96,384]{3,2,1,0:T(8,128)(2,1)} %copy-done.13, ...), custom_call_target="tpu_custom_call" | custom-call | flops 1048576 | bytes 1048576 | tf_op jit(solution)/shard_map/pallas_call | solution.py:94
  85.3 2.5 %collective-permute-done.16.f_ref.below_ref = bf16[2,5,96,384]{3,2,1,0:T(8,128)(2,1)S(1)} collective-permute-done((bf16[2,5,96,384]{3,2,1,0:T(8,128)(2,1)}, bf16[2,5,96,384]{3,2,1,0:T(8,128)(2,1)S(1)}, u32[]{:S(2)}, u32[]{:S(2)}) %collective-permute-start.16) | collective-permute-done | bytes 737312 | tf_op jit(solution)/shard_map/ppermute | solution.py:24
  87.9 2.3 %collective-permute-start.23 = (bf16[1,5,96,384]{3,2,1,0:T(8,128)(2,1)S(1)}, bf16[1,5,96,384]{3,2,1,0:T(8,128)(2,1)S(1)}, u32[]{:S(2)}, u32[]{:S(2)}) collective-permute-start(bf16[1,5,96,384]{3,2,1,0:T(8,128)(2,1)S(1)} %get-tuple-element.96), channel_id=1, source_target_pairs={{0,4},{1,5},{2,6},{3,7},{4,8},{5,9},{6,10},{7,11},{8,12},{9,13},{1... | collective-permute-start | bytes 1105928 | tf_op jit(solution)/shard_map/ppermute | solution.py:24
  90.6 11.4 %shard_map.108.acc_ref = f32[1024,768]{1,0:T(8,128)S(1)} custom-call(s32[7]{0:T(128)S(1)} %copy-done.6, f32[5]{0:T(128)S(1)} %get-tuple-element.112.gs_ref, f32[5]{0:T(128)S(1)} %get-tuple-element.113.us_ref, bf16[5,1024,768]{2,1,0:T(8,128)(2,1)} %get-tuple-element.98.x_ref, bf16[5,768,768]{2,1,0:T(8,128)(2,1)} %get-tuple-element.99.w_ref, ...), custom_call_target="tpu_custom_call" | custom-call | flops 1048576 | bytes 1048576 | tf_op jit(solution)/shard_map/pallas_call | solution.py:135
  102.1 2.7 %shard_map.110 = (bf16[256,384]{1,0:T(8,128)(2,1)}, bf16[256,384]{1,0:T(8,128)(2,1)}) custom-call(s32[7]{0:T(128)S(1)} %copy-done.6, f32[5]{0:T(128)S(1)} %get-tuple-element.112.gs_ref, f32[5]{0:T(128)S(1)} %get-tuple-element.113.us_ref, bf16[1,5,96,384]{3,2,1,0:T(8,128)(2,1)S(1)} %collective-permute-done.23.g_ref, ...), custom_call_target="tpu_custom_call" | custom-call | flops 1006632960 | bytes 4194304 | tf_op jit(solution)/shard_map/pallas_call | solution.py:177
  104.8 3.3 %collective-permute-start.27 = (bf16[256,384]{1,0:T(8,128)(2,1)}, bf16[256,384]{1,0:T(8,128)(2,1)S(1)}, u32[]{:S(2)}, u32[]{:S(2)}) collective-permute-start(bf16[256,384]{1,0:T(8,128)(2,1)} %get-tuple-element.104), channel_id=1, source_target_pairs={{0,3},{1,2},{2,1},{3,0},{4,7},{5,6},{6,5},{7,4},{8,11},{9,10},{10,... | collective-permute-start | bytes 589832 | tf_op jit(solution)/shard_map/ppermute | solution.py:19
  108.1 2.7 %shard_map.109 = (bf16[256,384]{1,0:T(8,128)(2,1)S(1)}, bf16[256,384]{1,0:T(8,128)(2,1)}) custom-call(s32[7]{0:T(128)S(1)} %copy-done.6, f32[5]{0:T(128)S(1)} %get-tuple-element.112.gs_ref, f32[5]{0:T(128)S(1)} %get-tuple-element.113.us_ref, bf16[1,5,96,384]{3,2,1,0:T(8,128)(2,1)S(1)} %collective-permute-done.23.g_ref, ...), custom_call_target="tpu_custom_call" | custom-call | flops 1006632960 | bytes 4194304 | tf_op jit(solution)/shard_map/pallas_call | solution.py:177
  111.6 4.3 %collective-permute-done.27.refs_3_ = bf16[256,384]{1,0:T(8,128)(2,1)S(1)} collective-permute-done((bf16[256,384]{1,0:T(8,128)(2,1)}, bf16[256,384]{1,0:T(8,128)(2,1)S(1)}, u32[]{:S(2)}, u32[]{:S(2)}) %collective-permute-start.27) | collective-permute-done | bytes 196640 | tf_op jit(solution)/shard_map/ppermute | solution.py:19
  120.3 2.6 %collective-permute-start.29 = (bf16[64,768]{1,0:T(8,128)(2,1)S(1)}, bf16[64,768]{1,0:T(8,128)(2,1)S(1)}, u32[]{:S(2)}, u32[]{:S(2)}) collective-permute-start(bf16[64,768]{1,0:T(8,128)(2,1)S(1)} %get-tuple-element.108), channel_id=1, source_target_pairs={{0,128},{32,160},{64,192},{96,224},{128,0},{160,32},{192,64},{224,... | collective-permute-start | bytes 294920 | tf_op jit(solution)/shard_map/ppermute | solution.py:19
  122.9 4.3 %collective-permute-done.29 = bf16[64,768]{1,0:T(8,128)(2,1)S(1)} collective-permute-done((bf16[64,768]{1,0:T(8,128)(2,1)S(1)}, bf16[64,768]{1,0:T(8,128)(2,1)S(1)}, u32[]{:S(2)}, u32[]{:S(2)}) %collective-permute-start.29) | collective-permute-done | bytes 98336 | tf_op jit(solution)/shard_map/ppermute | solution.py:19
  127.2 2.3 %collective-permute-done.30 = bf16[64,768]{1,0:T(8,128)(2,1)S(1)} collective-permute-done((bf16[64,768]{1,0:T(8,128)(2,1)S(1)}, bf16[64,768]{1,0:T(8,128)(2,1)S(1)}, u32[]{:S(2)}, u32[]{:S(2)}) %collective-permute-start.30) | collective-permute-done | bytes 98336 | tf_op jit(solution)/shard_map/ppermute | solution.py:19
  131.4 3.7 %collective-permute-done.31 = bf16[64,768]{1,0:T(8,128)(2,1)S(1)} collective-permute-done((bf16[64,768]{1,0:T(8,128)(2,1)S(1)}, bf16[64,768]{1,0:T(8,128)(2,1)S(1)}, u32[]{:S(2)}, u32[]{:S(2)}) %collective-permute-start.31) | collective-permute-done | bytes 98336 | tf_op jit(solution)/shard_map/ppermute | solution.py:19
  136.8 2.3 %collective-permute-start.34 = (bf16[64,768]{1,0:T(8,128)(2,1)S(1)}, bf16[64,768]{1,0:T(8,128)(2,1)S(1)}, u32[]{:S(2)}, u32[]{:S(2)}) collective-permute-start(bf16[64,768]{1,0:T(8,128)(2,1)S(1)} %add_convert_fusion.refs_0_), channel_id=1, source_target_pairs={{0,192},{32,224},{64,128},{96,160},{128,64},{160,96},{192,0},{224,... | collective-permute-start | bytes 294920 | tf_op jit(solution)/shard_map/ppermute | solution.py:19
  (114 shorter events, 39.0 us)
Async XLA Ops:
  2.7 8.4 %collective-permute-start = (bf16[2,5,24,384]{3,2,1,0:T(8,128)(2,1)}, bf16[2,5,24,384]{3,2,1,0:T(8,128)(2,1)S(1)}, u32[]{:S(2)}, u32[]{:S(2)}) collective-permute-start(bf16[2,5,24,384]{3,2,1,0:T(8,128)(2,1)} %get-tuple-element.57), channel_id=1, source_target_pairs={{0,1},{1,0},{2,3},{3,2},{4,5},{5,4},{6,7},{7,6},{8,9},{9,8},{10,11... | collective-permute-start | bytes 552968 | tf_op jit(solution)/shard_map/ppermute | solution.py:19
  5.9 6.5 %collective-permute-start.1 = (bf16[2,5,24,384]{3,2,1,0:T(8,128)(2,1)}, bf16[2,5,24,384]{3,2,1,0:T(8,128)(2,1)S(1)}, u32[]{:S(2)}, u32[]{:S(2)}) collective-permute-start(bf16[2,5,24,384]{3,2,1,0:T(8,128)(2,1)} %get-tuple-element.58), channel_id=1, source_target_pairs={{0,2},{1,3},{2,0},{3,1},{4,6},{5,7},{6,4},{7,5},{8,10},{9,11},{10,... | collective-permute-start | bytes 552968 | tf_op jit(solution)/shard_map/ppermute | solution.py:19
  5.9 10.9 %collective-permute-start.2 = (bf16[2,5,24,384]{3,2,1,0:T(8,128)(2,1)}, bf16[2,5,24,384]{3,2,1,0:T(8,128)(2,1)S(1)}, u32[]{:S(2)}, u32[]{:S(2)}) collective-permute-start(bf16[2,5,24,384]{3,2,1,0:T(8,128)(2,1)} %get-tuple-element.59), channel_id=1, source_target_pairs={{0,3},{1,2},{2,1},{3,0},{4,7},{5,6},{6,5},{7,4},{8,11},{9,10},{10,... | collective-permute-start | bytes 552968 | tf_op jit(solution)/shard_map/ppermute | solution.py:19
  8.8 15.9 %collective-permute-start.6 = (bf16[256,768]{1,0:T(8,128)(2,1)S(1)}, bf16[256,768]{1,0:T(8,128)(2,1)}, u32[]{:S(2)}, u32[]{:S(2)}) collective-permute-start(bf16[256,768]{1,0:T(8,128)(2,1)S(1)} %get-tuple-element.69), channel_id=1, source_target_pairs={{0,64},{32,96},{64,0},{96,32},{128,192},{160,224},{192,128},{224,1... | collective-permute-start | bytes 1179656 | tf_op jit(solution)/shard_map/ppermute | solution.py:19
  8.9 19.7 %collective-permute-start.7 = (bf16[256,768]{1,0:T(8,128)(2,1)S(1)}, bf16[256,768]{1,0:T(8,128)(2,1)S(1)}, u32[]{:S(2)}, u32[]{:S(2)}) collective-permute-start(bf16[256,768]{1,0:T(8,128)(2,1)S(1)} %get-tuple-element.69), channel_id=1, source_target_pairs={{0,128},{32,160},{64,192},{96,224},{128,0},{160,32},{192,64},{224,... | collective-permute-start | bytes 1179656 | tf_op jit(solution)/shard_map/ppermute | solution.py:19
  19.7 10.8 %collective-permute-start.5 = (bf16[256,768]{1,0:T(8,128)(2,1)S(1)}, bf16[256,768]{1,0:T(8,128)(2,1)S(1)}, u32[]{:S(2)}, u32[]{:S(2)}) collective-permute-start(bf16[256,768]{1,0:T(8,128)(2,1)S(1)} %get-tuple-element.61), channel_id=1, source_target_pairs={{0,2},{1,3},{2,0},{3,1},{4,6},{5,7},{6,4},{7,5},{8,10},{9,11},{10,... | collective-permute-start | bytes 1179656 | tf_op jit(solution)/shard_map/ppermute | solution.py:19
  19.7 22.0 %collective-permute-start.3 = (bf16[2,5,96,384]{3,2,1,0:T(8,128)(2,1)}, bf16[2,5,96,384]{3,2,1,0:T(8,128)(2,1)S(1)}, u32[]{:S(2)}, u32[]{:S(2)}) collective-permute-start(bf16[2,5,96,384]{3,2,1,0:T(8,128)(2,1)} %bitcast.9), channel_id=1, source_target_pairs={{0,4},{1,5},{2,6},{3,7},{4,8},{5,9},{6,10},{7,11},{8,12},{9,13},{1... | collective-permute-start | bytes 2211848 | tf_op jit(solution)/shard_map/ppermute | solution.py:24
  20.8 20.9 %collective-permute-start.4 = (bf16[2,5,96,384]{3,2,1,0:T(8,128)(2,1)}, bf16[2,5,96,384]{3,2,1,0:T(8,128)(2,1)S(1)}, u32[]{:S(2)}, u32[]{:S(2)}) collective-permute-start(bf16[2,5,96,384]{3,2,1,0:T(8,128)(2,1)} %bitcast.10), channel_id=1, source_target_pairs={{0,28},{1,29},{2,30},{3,31},{4,0},{5,1},{6,2},{7,3},{8,4},{9,5},{1... | collective-permute-start | bytes 2211848 | tf_op jit(solution)/shard_map/ppermute | solution.py:24
  30.5 11.2 %collective-permute-start.8 = (bf16[256,768]{1,0:T(8,128)(2,1)S(1)}, bf16[256,768]{1,0:T(8,128)(2,1)S(1)}, u32[]{:S(2)}, u32[]{:S(2)}) collective-permute-start(bf16[256,768]{1,0:T(8,128)(2,1)S(1)} %get-tuple-element.69), channel_id=1, source_target_pairs={{0,2},{1,3},{2,0},{3,1},{4,6},{5,7},{6,4},{7,5},{8,10},{9,11},{10,... | collective-permute-start | bytes 1179656 | tf_op jit(solution)/shard_map/ppermute | solution.py:19
  30.5 11.2 %collective-permute-start.9 = (bf16[256,768]{1,0:T(8,128)(2,1)S(1)}, bf16[256,768]{1,0:T(8,128)(2,1)S(1)}, u32[]{:S(2)}, u32[]{:S(2)}) collective-permute-start(bf16[256,768]{1,0:T(8,128)(2,1)S(1)} %collective-permute-done.5.refs_7_), channel_id=1, source_target_pairs={{0,64},{32,96},{64,0},{96,32},{128,192},{160,224},{192,128},{224,1... | collective-permute-start | bytes 1179656 | tf_op jit(solution)/shard_map/ppermute | solution.py:19
  42.5 24.4 %collective-permute-start.12 = (bf16[512,768]{1,0:T(8,128)(2,1)S(1)}, bf16[512,768]{1,0:T(8,128)(2,1)}, u32[]{:S(2)}, u32[]{:S(2)}) collective-permute-start(bf16[512,768]{1,0:T(8,128)(2,1)S(1)} %pad_maximum_fusion), channel_id=1, source_target_pairs={{0,32},{32,0},{64,96},{96,64},{128,160},{160,128},{192,224},{224,1... | collective-permute-start | bytes 2359304 | tf_op jit(solution)/shard_map/ppermute | solution.py:19
  45.1 21.8 %collective-permute-start.15 = (bf16[256,1536]{1,0:T(8,128)(2,1)S(1)}, bf16[256,1536]{1,0:T(8,128)(2,1)S(1)}, u32[]{:S(2)}, u32[]{:S(2)}) collective-permute-start(bf16[256,1536]{1,0:T(8,128)(2,1)S(1)} %copy-done.8), channel_id=1, source_target_pairs={{0,1},{1,0},{2,3},{3,2},{4,5},{5,4},{6,7},{7,6},{8,9},{9,8},{10,11... | collective-permute-start | bytes 2359304 | tf_op jit(solution)/shard_map/ppermute | solution.py:19
  45.5 21.4 %collective-permute-start.10 = (bf16[2,5,96,384]{3,2,1,0:T(8,128)(2,1)S(1)}, bf16[2,5,96,384]{3,2,1,0:T(8,128)(2,1)}, u32[]{:S(2)}, u32[]{:S(2)}) collective-permute-start(bf16[2,5,96,384]{3,2,1,0:T(8,128)(2,1)S(1)} %collective-permute-done.3.refs_1_), channel_id=1, source_target_pairs={{0,4},{1,5},{2,6},{3,7},{4,8},{5,9},{6,10},{7,11},{8,12},{9,13},{1... | collective-permute-start | bytes 2211848 | tf_op jit(solution)/shard_map/ppermute | solution.py:24
  46.2 20.8 %collective-permute-start.11 = (bf16[2,5,96,384]{3,2,1,0:T(8,128)(2,1)S(1)}, bf16[2,5,96,384]{3,2,1,0:T(8,128)(2,1)}, u32[]{:S(2)}, u32[]{:S(2)}) collective-permute-start(bf16[2,5,96,384]{3,2,1,0:T(8,128)(2,1)S(1)} %collective-permute-done.4.refs_2_), channel_id=1, source_target_pairs={{0,28},{1,29},{2,30},{3,31},{4,0},{5,1},{6,2},{7,3},{8,4},{9,5},{1... | collective-permute-start | bytes 2211848 | tf_op jit(solution)/shard_map/ppermute | solution.py:24
  50.1 11.8 %collective-permute-start.13 = (bf16[256,768]{1,0:T(8,128)(2,1)S(1)}, bf16[256,768]{1,0:T(8,128)(2,1)}, u32[]{:S(2)}, u32[]{:S(2)}) collective-permute-start(bf16[256,768]{1,0:T(8,128)(2,1)S(1)} %collective-permute-done.5.refs_7_), channel_id=1, source_target_pairs={{0,128},{32,160},{64,192},{96,224},{128,0},{160,32},{192,64},{224,... | collective-permute-start | bytes 1179656 | tf_op jit(solution)/shard_map/ppermute | solution.py:19
  68.5 19.2 %collective-permute-start.16 = (bf16[2,5,96,384]{3,2,1,0:T(8,128)(2,1)}, bf16[2,5,96,384]{3,2,1,0:T(8,128)(2,1)S(1)}, u32[]{:S(2)}, u32[]{:S(2)}) collective-permute-start(bf16[2,5,96,384]{3,2,1,0:T(8,128)(2,1)} %collective-permute-done.10.refs_3_), channel_id=1, source_target_pairs={{0,4},{1,5},{2,6},{3,7},{4,8},{5,9},{6,10},{7,11},{8,12},{9,13},{1... | collective-permute-start | bytes 2211848 | tf_op jit(solution)/shard_map/ppermute | solution.py:24
  68.8 19.0 %collective-permute-start.17 = (bf16[2,5,96,384]{3,2,1,0:T(8,128)(2,1)}, bf16[2,5,96,384]{3,2,1,0:T(8,128)(2,1)S(1)}, u32[]{:S(2)}, u32[]{:S(2)}) collective-permute-start(bf16[2,5,96,384]{3,2,1,0:T(8,128)(2,1)} %collective-permute-done.11.refs_4_), channel_id=1, source_target_pairs={{0,28},{1,29},{2,30},{3,31},{4,0},{5,1},{6,2},{7,3},{8,4},{9,5},{1... | collective-permute-start | bytes 2211848 | tf_op jit(solution)/shard_map/ppermute | solution.py:24
  87.9 14.2 %collective-permute-start.23 = (bf16[1,5,96,384]{3,2,1,0:T(8,128)(2,1)S(1)}, bf16[1,5,96,384]{3,2,1,0:T(8,128)(2,1)S(1)}, u32[]{:S(2)}, u32[]{:S(2)}) collective-permute-start(bf16[1,5,96,384]{3,2,1,0:T(8,128)(2,1)S(1)} %get-tuple-element.96), channel_id=1, source_target_pairs={{0,4},{1,5},{2,6},{3,7},{4,8},{5,9},{6,10},{7,11},{8,12},{9,13},{1... | collective-permute-start | bytes 1105928 | tf_op jit(solution)/shard_map/ppermute | solution.py:24
  90.1 11.9 %collective-permute-start.24 = (bf16[1,5,96,384]{3,2,1,0:T(8,128)(2,1)S(1)}, bf16[1,5,96,384]{3,2,1,0:T(8,128)(2,1)S(1)}, u32[]{:S(2)}, u32[]{:S(2)}) collective-permute-start(bf16[1,5,96,384]{3,2,1,0:T(8,128)(2,1)S(1)} %get-tuple-element.97), channel_id=1, source_target_pairs={{0,28},{1,29},{2,30},{3,31},{4,0},{5,1},{6,2},{7,3},{8,4},{9,5},{1... | collective-permute-start | bytes 1105928 | tf_op jit(solution)/shard_map/ppermute | solution.py:24
  104.8 6.8 %collective-permute-start.26 = (bf16[256,384]{1,0:T(8,128)(2,1)}, bf16[256,384]{1,0:T(8,128)(2,1)S(1)}, u32[]{:S(2)}, u32[]{:S(2)}) collective-permute-start(bf16[256,384]{1,0:T(8,128)(2,1)} %get-tuple-element.103), channel_id=1, source_target_pairs={{0,2},{1,3},{2,0},{3,1},{4,6},{5,7},{6,4},{7,5},{8,10},{9,11},{10,... | collective-permute-start | bytes 589832 | tf_op jit(solution)/shard_map/ppermute | solution.py:19
  104.8 11.0 %collective-permute-start.27 = (bf16[256,384]{1,0:T(8,128)(2,1)}, bf16[256,384]{1,0:T(8,128)(2,1)S(1)}, u32[]{:S(2)}, u32[]{:S(2)}) collective-permute-start(bf16[256,384]{1,0:T(8,128)(2,1)} %get-tuple-element.104), channel_id=1, source_target_pairs={{0,3},{1,2},{2,1},{3,0},{4,7},{5,6},{6,5},{7,4},{8,11},{9,10},{10,... | collective-permute-start | bytes 589832 | tf_op jit(solution)/shard_map/ppermute | solution.py:19
  120.3 7.0 %collective-permute-start.29 = (bf16[64,768]{1,0:T(8,128)(2,1)S(1)}, bf16[64,768]{1,0:T(8,128)(2,1)S(1)}, u32[]{:S(2)}, u32[]{:S(2)}) collective-permute-start(bf16[64,768]{1,0:T(8,128)(2,1)S(1)} %get-tuple-element.108), channel_id=1, source_target_pairs={{0,128},{32,160},{64,192},{96,224},{128,0},{160,32},{192,64},{224,... | collective-permute-start | bytes 294920 | tf_op jit(solution)/shard_map/ppermute | solution.py:19
  122.9 6.6 %collective-permute-start.30 = (bf16[64,768]{1,0:T(8,128)(2,1)S(1)}, bf16[64,768]{1,0:T(8,128)(2,1)S(1)}, u32[]{:S(2)}, u32[]{:S(2)}) collective-permute-start(bf16[64,768]{1,0:T(8,128)(2,1)S(1)} %get-tuple-element.109), channel_id=1, source_target_pairs={{0,192},{32,224},{64,128},{96,160},{128,64},{160,96},{192,0},{224,... | collective-permute-start | bytes 294920 | tf_op jit(solution)/shard_map/ppermute | solution.py:19
  136.8 6.5 %collective-permute-start.34 = (bf16[64,768]{1,0:T(8,128)(2,1)S(1)}, bf16[64,768]{1,0:T(8,128)(2,1)S(1)}, u32[]{:S(2)}, u32[]{:S(2)}) collective-permute-start(bf16[64,768]{1,0:T(8,128)(2,1)S(1)} %add_convert_fusion.refs_0_), channel_id=1, source_target_pairs={{0,192},{32,224},{64,128},{96,160},{128,64},{160,96},{192,0},{224,... | collective-permute-start | bytes 294920 | tf_op jit(solution)/shard_map/ppermute | solution.py:19
  (35 other events, 508.1 us)
